TPU v7x, 32 devices: a whole 2x2x4 slice. The times are simulated.
32 devices in a mesh: energy: 2 (over y), slab: 4 (over z), col: 2 (over x), orb: 2 (over core).
Axes of the slice: x: 2, y: 2, z: 4, core: 2. Of those that a mesh axis runs over, the one named last changes fastest.
Arguments:
- rhs: bfloat16 [2, 8, 512, 1024], P(None, ('energy', 'slab'), None, ('col', 'orb')), parts along dimension 1, may hold values from -6 to 6
- dinv: bfloat16 [2, 8, 512, 512], P(None, ('energy', 'slab'), 'orb'), parts along dimension 1, may hold values from -0.078125 to 1.125
- spikes: bfloat16 [2, 8, 2, 512, 512], P(None, ('energy', 'slab'), None, 'orb'), parts along dimension 1, may hold values from -0.09375 to 0.09375
- merge_inv: bfloat16 [2, 8, 512, 512], P(None, ('energy', 'slab'), 'orb'), parts along dimension 1, may hold values from -0.078125 to 1.125
Outputs:
- solution: float32 [2, 8, 512, 1024], P(None, ('energy', 'slab'), None, ('col', 'orb')), parts along dimension 1
There are 2 independent parts, one for each index of `energy`. A program takes and returns all parts, laid end to end along the dimension named above; each array names one. Nothing has to cross between parts.
All inputs are finite; a program needn't handle non-finite values.
Results may differ from a plain program's by a relative error of at most 0.013.
Values may be sent and summed in bfloat16 or wider, within the bound.
No kernel may reach another device: no remote copies, remote signals or barrier semaphores. Data moves between devices by JAX's collectives and lax.ppermute only.
A program may use at most 64 MiB of HBM per device.

v0:
```python
import jax
import jax.numpy as jnp
from jax import lax
from jax.sharding import PartitionSpec as P


def partner_2(block, axis, apart):
    count = lax.axis_size(axis)
    route = []
    for low in range(count):
        high = low | 1 << apart
        if high != low and high < count:
            route += [(low, high), (high, low)]
    return lax.ppermute(block, axis, route)


def from_behind(array, axis, by):
    devices = lax.axis_size(axis)
    pairs = [(i, i + by) for i in range(devices) if 0 <= i + by < devices]
    return lax.ppermute(array, axis, pairs)


def complex_product(matrix, operand):
    real_part = jnp.dot(matrix[0], operand[0], preferred_element_type=jnp.float32) - jnp.dot(
        matrix[1], operand[1], preferred_element_type=jnp.float32
    )
    imag_part = jnp.dot(matrix[0], operand[1], preferred_element_type=jnp.float32) + jnp.dot(
        matrix[1], operand[0], preferred_element_type=jnp.float32
    )
    return jnp.stack([real_part, imag_part])


def spread_group(values, root_device, height, device):
    for which_bit in range(height + 1):
        partner = partner_2(values, "slab", which_bit)
        receive_mask = (device ^ root_device) >> which_bit == 1
        values = jnp.where(receive_mask, partner, values)
    return values


def per_device(rhs, dinv, spikes, merge_inv):
    inverse_full, spike_full, merge_full = (
        lax.all_gather(dinv, "orb", axis=2, tiled=True),
        lax.all_gather(spikes, "orb", axis=3, tiled=True),
        lax.all_gather(merge_inv, "orb", axis=2, tiled=True),
    )
    inverse_full = inverse_full[:, 0]
    merge_full = merge_full[:, 0]
    current = complex_product(inverse_full, rhs[:, 0])
    device = lax.axis_index("slab")
    levels_count = spikes.shape[2]
    for height in range(levels_count):
        half_span = 1 << height
        position = device % (2 * half_span)
        group_first = device - position
        spike_now = spike_full[:, 0, height]
        rounded = current.astype(jnp.bfloat16)
        upper_tip = from_behind(rounded, "slab", -1)
        is_left = position == half_span - 1
        in_right = position >= half_span

        def merge_tip():
            interior = current - complex_product(spike_now, upper_tip)
            return complex_product(merge_full, interior.astype(jnp.bfloat16)).astype(jnp.bfloat16)

        left_tip = lax.cond(is_left, merge_tip, lambda: rounded)
        left_tip = spread_group(left_tip, group_first + half_span - 1, height, device)
        current = lax.cond(
            in_right, lambda: current - complex_product(spike_now, left_tip), lambda: current
        )
        right_tip = current.astype(jnp.bfloat16)
        right_tip = spread_group(right_tip, group_first + half_span, height, device)
        current = lax.cond(
            in_right, lambda: current, lambda: current - complex_product(spike_now, right_tip)
        )
    return current[:, None]


def solution(mesh):
    placed = (
        P(None, ("energy", "slab"), None, ("col", "orb")),
        P(None, ("energy", "slab"), "orb", None),
        P(None, ("energy", "slab"), None, "orb", None),
        P(None, ("energy", "slab"), "orb", None),
    )
    return jax.shard_map(
        per_device,
        mesh=mesh,
        in_specs=placed,
        out_specs=P(None, ("energy", "slab"), None, ("col", "orb")),
        check_vma=False,
    )
```

profile of v0, /device:TPU:0, one launch (start us, length us, event | category | flops | bytes accessed | tf_op | source)
XLA Modules:
  0.0 199.4 jit_solution(16464014938704535066)
XLA Ops:
  7.3 2.3 %copy.7 = bf16[2,1,2,256,512]{4,3,0,2,1:T(8,128)(2,1)} copy(bf16[2,1,2,256,512]{4,3,2,1,0:T(8,128)(2,1)} %param.18) | data formatting | bytes 2097152 | tf_op args[2]
  10.3 10.3 %all-gather.6.cloned.1.call-done = bf16[2,1,512,512]{3,2,1,0:T(8,128)(2,1)} async-done(((bf16[2,1,256,512]{3,2,1,0:T(8,128)(2,1)}), bf16[2,1,512,512]{3,2,1,0:T(8,128)(2,1)}) %all-gather.6.cloned.1.call-update) | async-done | bytes 1048592 | tf_op jit(solution)/shard_map/all_gather | solution.py:43
  20.7 1.4 fusion.121
  22.1 1.3 fusion.119
  24.1 1.3 collective-permute-start
  25.5 1.1 pad_maximum_fusion.2
  26.5 7.5 %all-gather.4.cloned.1.call-done = bf16[2,1,2,512,512]{4,3,0,2,1:T(8,128)(2,1)} async-done(((bf16[2,1,2,256,512]{4,3,0,2,1:T(8,128)(2,1)}), bf16[2,1,2,512,512]{4,3,0,2,1:T(8,128)(2,1)}) %all-gather.4.cloned.1.call-update) | async-done | bytes 2097168 | tf_op jit(solution)/shard_map/all_gather | solution.py:44
  34.0 1.7 slice_bitcast_fusion.36
  35.7 10.1 %all-gather.8.cloned.1.call-done = bf16[2,1,512,512]{3,2,0,1:T(8,128)(2,1)} async-done(((bf16[2,1,256,512]{3,2,0,1:T(8,128)(2,1)}), bf16[2,1,512,512]{3,2,0,1:T(8,128)(2,1)}) %all-gather.8.cloned.1.call-update) | async-done | bytes 1048592 | tf_op jit(solution)/shard_map/all_gather | solution.py:45
  45.8 4.1 %conditional.6 = (bf16[2,512,256]{1,2,0:T(8,128)(2,1)S(1)}) conditional(s32[]{:T(128)} %convert_element_type.42, (bf16[2,512,256]{2,1,0:T(8,128)(2,1)S(1)}) %tuple.57, (bf16[2,512,512]{2,1,0:T(8,128)(2,1)S(1)}, bf16[2,512,256]{2,1,0:T(8,128)(2,1)S(1)}, f32[2,512,256]{2,1,0:T(8,128)}, bf16[2,512,512]{2,1,0:T(8,128)(2,1)}) %tuple.85), branch_computations={%region_0.1_spmd, %region_1.2_spmd} | conditional | flops 1075576832 | bytes 26214492 | solution.py:66
  46.9 1.3 fusion.1
  49.9 1.0 copy.10
  50.9 14.3 %collective-permute-done.1 = bf16[2,512,256]{2,1,0:T(8,128)(2,1)S(1)} collective-permute-done((bf16[2,512,256]{2,1,0:T(8,128)(2,1)}, bf16[2,512,256]{2,1,0:T(8,128)(2,1)S(1)}, u32[]{:S(2)}, u32[]{:S(2)}) %collective-permute-start.1) | collective-permute-done | bytes 524320 | tf_op jit(solution)/shard_map/ppermute | solution.py:14
  65.1 1.6 conditional.7
  65.1 1.6 copy.23
  66.7 1.0 copy.14
  67.7 6.9 %collective-permute-start.2 = (bf16[2,512,256]{2,1,0:T(8,128)(2,1)}, bf16[2,512,256]{2,1,0:T(8,128)(2,1)S(1)}, u32[]{:S(2)}, u32[]{:S(2)}) collective-permute-start(bf16[2,512,256]{2,1,0:T(8,128)(2,1)} %copy.14), channel_id=1, source_target_pairs={{0,4},{4,0},{8,12},{12,8},{1,5},{5,1},{9,13},{13,9},{2,6},{6,2},{1... | collective-permute-start | bytes 1572872 | tf_op jit(solution)/shard_map/ppermute | solution.py:14
  74.6 12.0 %collective-permute-done.2 = bf16[2,512,256]{2,1,0:T(8,128)(2,1)S(1)} collective-permute-done((bf16[2,512,256]{2,1,0:T(8,128)(2,1)}, bf16[2,512,256]{2,1,0:T(8,128)(2,1)S(1)}, u32[]{:S(2)}, u32[]{:S(2)}) %collective-permute-start.2) | collective-permute-done | bytes 524320 | tf_op jit(solution)/shard_map/ppermute | solution.py:14
  86.6 3.6 %conditional.8 = (f32[2,512,256]{1,2,0:T(8,128)S(1)}) conditional(s32[]{:T(128)} %convert_element_type.41, (bf16[2,512,512]{2,1,0:T(8,128)(2,1)S(1)}, s32[]{:T(128)}, f32[2,512,256]{1,2,0:T(8,128)S(1)}, bf16[2,512,256]{2,1,0:T(8,128)(2,1)S(1)}, bf16[2,512,256]{2,1,0:T(8,128)(2,1)}, /*index=5*/s32[]{:T(128)}, s32[]{:T(128)}, ...), branch_computations={%region_4.5_spmd.clone, %region_5.6_spmd} | conditional | flops 537919488 | bytes 13107282 | solution.py:73
  86.6 0.8 copy-done.10
  87.4 1.1 broadcast_select_fusion.2
  90.4 1.3 collective-permute-start.3
  91.7 13.5 %collective-permute-done.3 = bf16[2,512,256]{2,1,0:T(8,128)(2,1)S(1)} collective-permute-done((bf16[2,512,256]{2,1,0:T(8,128)(2,1)S(1)}, bf16[2,512,256]{2,1,0:T(8,128)(2,1)S(1)}, u32[]{:S(2)}, u32[]{:S(2)}) %collective-permute-start.3) | collective-permute-done | bytes 524320 | tf_op jit(solution)/shard_map/ppermute | solution.py:20
  105.3 9.3 %collective-permute-start.4 = (bf16[2,512,256]{2,1,0:T(8,128)(2,1)S(1)}, bf16[2,512,256]{2,1,0:T(8,128)(2,1)}, u32[]{:S(2)}, u32[]{:S(2)}) collective-permute-start(bf16[2,512,256]{2,1,0:T(8,128)(2,1)S(1)} %get-tuple-element.193), channel_id=1, source_target_pairs={{0,4},{4,0},{8,12},{12,8},{1,5},{5,1},{9,13},{13,9},{2,6},{6,2},{1... | collective-permute-start | bytes 1572872 | tf_op jit(solution)/shard_map/ppermute | solution.py:14
  114.6 10.8 %collective-permute-done.4 = bf16[2,512,256]{2,1,0:T(8,128)(2,1)} collective-permute-done((bf16[2,512,256]{2,1,0:T(8,128)(2,1)S(1)}, bf16[2,512,256]{2,1,0:T(8,128)(2,1)}, u32[]{:S(2)}, u32[]{:S(2)}) %collective-permute-start.4) | collective-permute-done | bytes 524320 | tf_op jit(solution)/shard_map/ppermute | solution.py:14
  125.4 1.1 broadcast_select_fusion.4
  126.6 23.8 %collective-permute-done.5 = bf16[2,512,256]{2,1,0:T(8,128)(2,1)S(1)} collective-permute-done((bf16[2,512,256]{2,1,0:T(8,128)(2,1)S(1)}, bf16[2,512,256]{2,1,0:T(8,128)(2,1)S(1)}, u32[]{:S(2)}, u32[]{:S(2)}) %collective-permute-start.5) | collective-permute-done | bytes 524320 | tf_op jit(solution)/shard_map/ppermute | solution.py:14
  150.6 13.9 %collective-permute-done.6 = bf16[2,512,256]{2,1,0:T(8,128)(2,1)} collective-permute-done((bf16[2,512,256]{2,1,0:T(8,128)(2,1)S(1)}, bf16[2,512,256]{2,1,0:T(8,128)(2,1)}, u32[]{:S(2)}, u32[]{:S(2)}) %collective-permute-start.6) | collective-permute-done | bytes 524320 | tf_op jit(solution)/shard_map/ppermute | solution.py:14
  164.6 1.4 collective-permute-start.7
  166.0 23.8 %collective-permute-done.7 = bf16[2,512,256]{2,1,0:T(8,128)(2,1)S(1)} collective-permute-done((bf16[2,512,256]{2,1,0:T(8,128)(2,1)S(1)}, bf16[2,512,256]{2,1,0:T(8,128)(2,1)S(1)}, u32[]{:S(2)}, u32[]{:S(2)}) %collective-permute-start.7) | collective-permute-done | bytes 524320 | tf_op jit(solution)/shard_map/ppermute | solution.py:14
  189.8 2.0 %conditional.11 = (f32[2,1,512,256]{3,2,1,0:T(8,128)S(1)}) conditional(s32[]{:T(128)} %convert_element_type.40, (s32[]{:T(128)}, bf16[2,512,256]{2,1,0:T(8,128)(2,1)S(1)}, bf16[2,512,256]{2,1,0:T(8,128)(2,1)S(1)}, bf16[2,512,512]{2,1,0:T(8,128)(2,1)S(1)}, f32[2,512,256]{1,2,0:T(8,128)S(1)}) %tuple.50, ...), branch_computations={%region_10.11_spmd, %region_11.12_spmd} | conditional | flops 537919488 | bytes 13107230 | solution.py:73
  191.9 1.0 copy-done.8
  (51 shorter events, 9.1 us)
Async XLA Ops:
  6.5 14.1 %copy-start.5 = (bf16[2,1,512,256]{3,2,1,0:T(8,128)(2,1)S(1)}, bf16[2,1,512,256]{3,2,1,0:T(8,128)(2,1)}, u32[]{:S(2)}) copy-start(bf16[2,1,512,256]{3,2,1,0:T(8,128)(2,1)} %param.16) | copy-start | bytes 1572868
  6.5 14.1 %all-gather.6.cloned.1.call-start = ((), (), s32[]{:S(2)}) async-start(), calls=%async_computation.1 | async-start | bytes 1572864 | tf_op jit(solution)/shard_map/all_gather | solution.py:43
  7.3 26.7 %all-gather.4.cloned.1.call-start = ((), (), s32[]{:S(2)}) async-start(), calls=%async_computation | async-start | bytes 3145728 | tf_op jit(solution)/shard_map/all_gather | solution.py:44
  9.6 36.2 %all-gather.8.cloned.1.call-start = ((), (), s32[]{:S(2)}) async-start(), calls=%async_computation.2 | async-start | bytes 1572864 | tf_op jit(solution)/shard_map/all_gather | solution.py:45
  20.7 2.8 %copy-start.4 = (bf16[2,1,512,512]{3,2,1,0:T(8,128)(2,1)S(1)}, bf16[2,1,512,512]{3,2,1,0:T(8,128)(2,1)}, u32[]{:S(2)}) copy-start(bf16[2,1,512,512]{3,2,1,0:T(8,128)(2,1)} %all-gather.6.cloned.1.call-done) | copy-start | bytes 3145732
  24.1 21.6 %collective-permute-start = (bf16[2,512,256]{2,1,0:T(8,128)(2,1)S(1)}, bf16[2,512,256]{2,1,0:T(8,128)(2,1)S(1)}, u32[]{:S(2)}, u32[]{:S(2)}) collective-permute-start(bf16[2,512,256]{2,1,0:T(8,128)(2,1)S(1)} %fusion.131), channel_id=1, source_target_pairs={{4,0},{8,4},{12,8},{5,1},{9,5},{13,9},{6,2},{10,6},{14,10},{7,3},{... | collective-permute-start | bytes 1572872 | tf_op jit(solution)/shard_map/ppermute | solution.py:20
  45.8 0.8 copy-start.6
  46.1 2.1 %copy-start.2 = (f32[2,512,256]{2,1,0:T(8,128)S(1)}, f32[2,512,256]{2,1,0:T(8,128)}, u32[]{:S(2)}) copy-start(f32[2,512,256]{2,1,0:T(8,128)} %get-tuple-element.94) | copy-start | bytes 3145732 | tf_op jit(solution)/shard_map/cond
  46.9 1.5 copy-start
  50.9 14.3 %collective-permute-start.1 = (bf16[2,512,256]{2,1,0:T(8,128)(2,1)}, bf16[2,512,256]{2,1,0:T(8,128)(2,1)S(1)}, u32[]{:S(2)}, u32[]{:S(2)}) collective-permute-start(bf16[2,512,256]{2,1,0:T(8,128)(2,1)} %copy.10), channel_id=1, source_target_pairs={{0,4},{4,0},{8,12},{12,8},{1,5},{5,1},{9,13},{13,9},{2,6},{6,2},{1... | collective-permute-start | bytes 1572872 | tf_op jit(solution)/shard_map/ppermute | solution.py:14
  67.7 18.9 %collective-permute-start.2 = (bf16[2,512,256]{2,1,0:T(8,128)(2,1)}, bf16[2,512,256]{2,1,0:T(8,128)(2,1)S(1)}, u32[]{:S(2)}, u32[]{:S(2)}) collective-permute-start(bf16[2,512,256]{2,1,0:T(8,128)(2,1)} %copy.14), channel_id=1, source_target_pairs={{0,4},{4,0},{8,12},{12,8},{1,5},{5,1},{9,13},{13,9},{2,6},{6,2},{1... | collective-permute-start | bytes 1572872 | tf_op jit(solution)/shard_map/ppermute | solution.py:14
  86.6 0.8 copy-start.10
  90.4 14.9 %collective-permute-start.3 = (bf16[2,512,256]{2,1,0:T(8,128)(2,1)S(1)}, bf16[2,512,256]{2,1,0:T(8,128)(2,1)S(1)}, u32[]{:S(2)}, u32[]{:S(2)}) collective-permute-start(bf16[2,512,256]{2,1,0:T(8,128)(2,1)S(1)} %copy.15), channel_id=1, source_target_pairs={{4,0},{8,4},{12,8},{5,1},{9,5},{13,9},{6,2},{10,6},{14,10},{7,3},{... | collective-permute-start | bytes 1572872 | tf_op jit(solution)/shard_map/ppermute | solution.py:20
  105.3 20.1 %collective-permute-start.4 = (bf16[2,512,256]{2,1,0:T(8,128)(2,1)S(1)}, bf16[2,512,256]{2,1,0:T(8,128)(2,1)}, u32[]{:S(2)}, u32[]{:S(2)}) collective-permute-start(bf16[2,512,256]{2,1,0:T(8,128)(2,1)S(1)} %get-tuple-element.193), channel_id=1, source_target_pairs={{0,4},{4,0},{8,12},{12,8},{1,5},{5,1},{9,13},{13,9},{2,6},{6,2},{1... | collective-permute-start | bytes 1572872 | tf_op jit(solution)/shard_map/ppermute | solution.py:14
  126.5 23.9 %collective-permute-start.5 = (bf16[2,512,256]{2,1,0:T(8,128)(2,1)S(1)}, bf16[2,512,256]{2,1,0:T(8,128)(2,1)S(1)}, u32[]{:S(2)}, u32[]{:S(2)}) collective-permute-start(bf16[2,512,256]{2,1,0:T(8,128)(2,1)S(1)} %broadcast_select_fusion.4), channel_id=1, source_target_pairs={{0,8},{8,0},{4,12},{12,4},{1,9},{9,1},{5,13},{13,5},{2,10},{10,2},... | collective-permute-start | bytes 1572872 | tf_op jit(solution)/shard_map/ppermute | solution.py:14
  150.5 14.0 %collective-permute-start.6 = (bf16[2,512,256]{2,1,0:T(8,128)(2,1)S(1)}, bf16[2,512,256]{2,1,0:T(8,128)(2,1)}, u32[]{:S(2)}, u32[]{:S(2)}) collective-permute-start(bf16[2,512,256]{2,1,0:T(8,128)(2,1)S(1)} %copy.20), channel_id=1, source_target_pairs={{0,4},{4,0},{8,12},{12,8},{1,5},{5,1},{9,13},{13,9},{2,6},{6,2},{1... | collective-permute-start | bytes 1572872 | tf_op jit(solution)/shard_map/ppermute | solution.py:14
  164.6 25.2 %collective-permute-start.7 = (bf16[2,512,256]{2,1,0:T(8,128)(2,1)S(1)}, bf16[2,512,256]{2,1,0:T(8,128)(2,1)S(1)}, u32[]{:S(2)}, u32[]{:S(2)}) collective-permute-start(bf16[2,512,256]{2,1,0:T(8,128)(2,1)S(1)} %broadcast_select_fusion.5), channel_id=1, source_target_pairs={{0,8},{8,0},{4,12},{12,4},{1,9},{9,1},{5,13},{13,5},{2,10},{10,2},... | collective-permute-start | bytes 1572872 | tf_op jit(solution)/shard_map/ppermute | solution.py:14
  191.9 1.0 copy-start.8
Sparse Core Ops, SparseCore 0:
  8.9 11.7 all-gather.5
  22.2 11.7 all-gather.3
  35.5 10.1 all-gather.7
where the time goes:
time: 200 us; the launch traced here: 199 us
  waiting for transfers between devices  141 us (70%)
  starting transfers between devices  20.4 us (10%)
  between operations  13.3 us (7%)
  local copies, waits for them, and re-layouts  10.2 us (5%)
  matrix products  9.68 us (5%)
  other arithmetic  4.16 us (2%)
    ppermute x6, waiting for transfers between devices, partner_2(): return lax.ppermute(block, axis, route)  98.6 us
    ppermute x6, starting transfers between devices, partner_2(): return lax.ppermute(block, axis, route)  17.7 us
    ppermute x2, waiting for transfers between devices, from_behind(): return lax.ppermute(array, axis, pairs)  13.6 us
    all_gather x1, waiting for transfers between devices, per_device(): lax.all_gather(dinv, 'orb', axis=2, tiled=True)  10.3 us
    all_gather x1, waiting for transfers between devices, per_device(): lax.all_gather(merge_inv, 'orb', axis=2, tiled=True)  10.1 us
    all_gather x1, waiting for transfers between devices, per_device(): lax.all_gather(spikes, 'orb', axis=3, tiled=True)  7.48 us
  transfers between devices with their start and end apart: 11, of which 10 were waited for; matrix products, arithmetic and copies ran while one was open for 4% of the time, Pallas kernels for 0%

commit v1 on v0

v1 whole, which is shorter than its diff:
```python
import functools

import jax
import jax.numpy as jnp
from jax import lax
from jax.experimental import pallas as pl
from jax.experimental.pallas import tpu as pltpu
from jax.sharding import PartitionSpec as P

VMEM = pl.BlockSpec(memory_space=pltpu.VMEM)


def ring_gather(block, axis):
    count = lax.axis_size(axis)
    blocks = [block]
    for step in range(1, count):
        blocks.append(lax.ppermute(block, axis, [((i + step) % count, i) for i in range(count)]))
    return blocks


def row_starts(height, orb_count, col_parts):
    orb = lax.axis_index("orb")
    per_orb = height // orb_count
    starts = []
    for j in range(orb_count):
        base = lax.rem(orb + j, orb_count) * per_orb
        if col_parts == 1:
            starts.append(base)
            continue
        col = lax.axis_index("col")
        for k in range(col_parts):
            starts.append(base + lax.rem(col + k, col_parts) * (per_orb // col_parts))
    return starts


def rows_of(start, size):
    return pl.ds(pl.multiple_of(start, size), size)


def turned(field):
    half = field.shape[1] // 2
    return jnp.concatenate([-field[:, half:], field[:, :half]], axis=1)


def each_product(pieces, starts, field):
    field_i = turned(field)
    for piece, start in zip(pieces, starts):
        real, imag = piece[0], piece[1]
        yield (
            rows_of(start, real.shape[0]),
            jnp.dot(real, field, preferred_element_type=jnp.float32)
            + jnp.dot(imag, field_i, preferred_element_type=jnp.float32),
        )


def call(body, outs, scratch, *args, flops=0, aliases=None):
    nbytes = sum(a.size * a.dtype.itemsize for a in args) + sum(o.size * o.dtype.itemsize for o in outs)
    return pl.pallas_call(
        body,
        out_shape=outs,
        in_specs=[VMEM] * len(args),
        out_specs=[VMEM] * len(outs),
        scratch_shapes=scratch,
        compiler_params=pltpu.CompilerParams(vmem_limit_bytes=24 * 2**20),
        cost_estimate=pl.CostEstimate(flops=flops, bytes_accessed=nbytes, transcendentals=0),
    )(*args)


def product_flops(height, width):
    return 2 * 2 * height * height * width


def start_state(pieces, rhs, chunks):
    height, columns = rhs.shape[1:]
    part = columns // chunks
    orb_count = len(pieces)

    def body(*refs):
        mats, rhs_ref, outs = refs[:orb_count], refs[orb_count], refs[orb_count + 1 :]
        starts = row_starts(height, orb_count, 1)
        for c in range(chunks):
            window = pl.ds(c * part, part)
            field = jnp.concatenate([rhs_ref[0, :, window], rhs_ref[1, :, window]], axis=1)
            for rows, value in each_product(mats, starts, field):
                outs[2 * c][rows, :] = value
                outs[2 * c + 1][rows, :] = value.astype(jnp.bfloat16)

    shape = (height, 2 * part)
    outs = [jax.ShapeDtypeStruct(shape, t) for _ in range(chunks) for t in (jnp.float32, jnp.bfloat16)]
    flat = call(body, outs, [], *pieces, rhs, flops=chunks * product_flops(height, 2 * part))
    return flat[0::2], flat[1::2]


def left_tip(is_left, state, hb_next, spike, merge):
    height, width = state.shape
    n = len(spike)

    def body(*refs):
        state_ref, hb_ref = refs[:2]
        spike_refs, merge_refs = refs[2 : 2 + n], refs[2 + n : 2 + 2 * n]
        out, inner = refs[2 + 2 * n :]
        starts = row_starts(height, n, 1)

        @pl.when(is_left())
        def _():
            for rows, value in each_product(spike_refs, starts, hb_ref[...]):
                inner[rows, :] = (state_ref[rows, :] - value).astype(jnp.bfloat16)
            for rows, value in each_product(merge_refs, starts, inner[...]):
                out[rows, :] = value.astype(jnp.bfloat16)

    (zl,) = call(
        body,
        [jax.ShapeDtypeStruct((height, width), jnp.bfloat16)],
        [pltpu.VMEM((height, width), jnp.bfloat16)],
        state, hb_next, *spike, *merge,
        flops=2 * product_flops(height, width),
    )
    return zl


def left_update(is_left, state, hb_next, zl, spike, spike_next):
    height, width = state.shape
    n, m = len(spike), len(spike_next)

    def body(*refs):
        state_ref, hb_ref, zl_ref = refs[:3]
        spike_refs, next_refs = refs[3 : 3 + n], refs[3 + n : 3 + n + m]
        out, out_b, inner = refs[3 + n + m :]

        @pl.when(is_left())
        def _():
            for rows, value in each_product(next_refs, row_starts(height, n, m // n), zl_ref[...]):
                inner[rows, :] = (hb_ref[rows, :].astype(jnp.float32) - value).astype(jnp.bfloat16)
            for rows, value in each_product(spike_refs, row_starts(height, n, 1), inner[...]):
                new = state_ref[rows, :] - value
                out[rows, :] = new
                out_b[rows, :] = new.astype(jnp.bfloat16)

        @pl.when(jnp.logical_not(is_left()))
        def _():
            out[...] = state_ref[...]
            out_b[...] = state_ref[...].astype(jnp.bfloat16)

    return call(
        body,
        [jax.ShapeDtypeStruct((height, width), t) for t in (jnp.float32, jnp.bfloat16)],
        [pltpu.VMEM((height, width), jnp.bfloat16)],
        state, hb_next, zl, *spike, *spike_next,
        flops=2 * product_flops(height, width),
    )


def right_update(is_right, state, zl, spike):
    height, width = state.shape
    n = len(spike)

    def body(*refs):
        state_ref, zl_ref = refs[:2]
        spike_refs, (out,) = refs[2 : 2 + n], refs[2 + n :]

        @pl.when(is_right())
        def _():
            for rows, value in each_product(spike_refs, row_starts(height, n, 1), zl_ref[...]):
                out[rows, :] = state_ref[rows, :] - value

        @pl.when(jnp.logical_not(is_right()))
        def _():
            out[...] = state_ref[...]

    (new,) = call(
        body,
        [jax.ShapeDtypeStruct((height, width), jnp.float32)],
        [],
        state, zl, *spike,
        flops=product_flops(height, width),
    )
    return new


def tip_of(is_left, hb_next, zl, arrived, spike_next, orb_count):
    height, width = zl.shape
    m = len(spike_next)

    def body(*refs):
        hb_ref, zl_ref, arrived_ref = refs[:3]
        next_refs, (out,) = refs[3 : 3 + m], refs[3 + m :]

        @pl.when(is_left())
        def _():
            starts = row_starts(height, orb_count, m // orb_count)
            for rows, value in each_product(next_refs, starts, zl_ref[...]):
                out[rows, :] = (hb_ref[rows, :].astype(jnp.float32) - value).astype(jnp.bfloat16)

        @pl.when(jnp.logical_not(is_left()))
        def _():
            out[...] = arrived_ref[...]

    (tip,) = call(
        body,
        [jax.ShapeDtypeStruct((height, width), jnp.bfloat16)],
        [],
        hb_next, zl, arrived, *spike_next,
        flops=product_flops(height, width),
    )
    return tip


def pick(use_new, new, old):
    def body(new_ref, old_ref, out):
        @pl.when(use_new())
        def _():
            out[...] = new_ref[...]

        @pl.when(jnp.logical_not(use_new()))
        def _():
            out[...] = old_ref[...]

    (out,) = call(body, [jax.ShapeDtypeStruct(old.shape, old.dtype)], [], new, old)
    return out


def tip_update(use_new, state, new_tip, tip, spike):
    height, width = state.shape
    n = len(spike)

    def body(*refs):
        state_ref, new_ref, tip_ref = refs[:3]
        spike_refs, (out, out_b) = refs[3 : 3 + n], refs[3 + n :]

        def update(source):
            for rows, value in each_product(spike_refs, row_starts(height, n, 1), source[...]):
                new = state_ref[rows, :] - value
                out[rows, :] = new
                out_b[rows, :] = new.astype(jnp.bfloat16)

        @pl.when(use_new())
        def _():
            update(new_ref)

        @pl.when(jnp.logical_not(use_new()))
        def _():
            update(tip_ref)

    return call(
        body,
        [jax.ShapeDtypeStruct((height, width), t) for t in (jnp.float32, jnp.bfloat16)],
        [],
        state, new_tip, tip, *spike,
        flops=product_flops(height, width),
    )


def per_device(chunks, rhs, dinv, spikes, merge_inv):
    slabs = lax.axis_size("slab")
    cols = lax.axis_size("col")
    orb_count = lax.axis_size("orb")
    levels = spikes.shape[2]
    height = dinv.shape[3]
    device = lax.axis_index("slab")

    level_of = jnp.int32(0)
    for level in range(1, levels):
        level_of = jnp.where(lax.rem(device, 1 << level) == 0, level, level_of)
    part = height // orb_count // cols
    mine = lax.dynamic_slice(
        spikes,
        (0, 0, level_of, lax.axis_index("col") * part, 0),
        (2, 1, 1, part, height),
    ).reshape(2, part, height)
    backward = [(i, i - 1) for i in range(1, slabs)]
    quarter = lax.ppermute(mine, "slab", backward)

    inverse = ring_gather(dinv[:, 0], "orb")
    states, hbs = start_state(inverse, rhs[:, 0], chunks)
    states, hbs = list(states), list(hbs)
    spike_all = [ring_gather(spikes[:, 0, level], "orb") for level in range(levels)]
    merge = ring_gather(merge_inv[:, 0], "orb")
    spike_next = []
    for piece in ring_gather(quarter, "col"):
        spike_next.append(ring_gather(piece, "orb"))
    spike_next = [spike_next[k][j] for j in range(orb_count) for k in range(cols)]

    early = hbs
    for level in range(levels):
        span = 1 << level
        heads = range(0, slabs, 2 * span)
        spike = spike_all[level]

        def position(span=span):
            return lax.rem(lax.axis_index("slab"), 2 * span)

        def is_left(span=span, position=position):
            return position() == span - 1

        def is_right(span=span, position=position):
            return position() >= span

        down = [(g + span, g + span - 1) for g in heads]
        up = [(g + span - 1, g + span) for g in heads]
        hb_next = [lax.ppermute(early[c], "slab", down) for c in range(chunks)]
        zl = [left_tip(is_left, states[c], hb_next[c], spike, merge) for c in range(chunks)]
        arrived = [lax.ppermute(zl[c], "slab", up) for c in range(chunks)]
        if span == 1:
            for c in range(chunks):
                states[c], hbs[c] = left_update(is_left, states[c], hb_next[c], zl[c], spike, spike_next)
                early = list(hbs)
            for c in range(chunks):
                states[c] = right_update(is_right, states[c], arrived[c], spike)
            continue
        tips = [tip_of(is_left, hb_next[c], zl[c], arrived[c], spike_next, orb_count) for c in range(chunks)]
        reach = 1
        while reach < span:
            route = []
            for g in heads:
                for j in range(reach):
                    if j + reach < span:
                        route.append((g + span + j, g + span + j + reach))
                        route.append((g + span - 1 - j, g + span - 1 - j - reach))
            moved = [lax.ppermute(tips[c], "slab", route) for c in range(chunks)]

            def is_new(span=span, position=position, reach=reach):
                far = jnp.where(position() >= span, position() - span, span - 1 - position())
                return jnp.logical_and(far >= reach, far < 2 * reach)

            if 2 * reach < span:
                tips = [pick(is_new, moved[c], tips[c]) for c in range(chunks)]
            reach *= 2
        for c in range(chunks):
            states[c], hbs[c] = tip_update(is_new, states[c], moved[c], tips[c], spike)
        early = list(hbs)

    half = [s.shape[1] // 2 for s in states]
    real = jnp.concatenate([s[:, :h] for s, h in zip(states, half)], axis=1)
    imag = jnp.concatenate([s[:, h:] for s, h in zip(states, half)], axis=1)
    return jnp.stack([real, imag])[:, None]


def solution(mesh):
    placed = (
        P(None, ("energy", "slab"), None, ("col", "orb")),
        P(None, ("energy", "slab"), "orb", None),
        P(None, ("energy", "slab"), None, "orb", None),
        P(None, ("energy", "slab"), "orb", None),
    )

    def body(rhs, dinv, spikes, merge_inv):
        chunks = 2 if rhs.shape[3] % 256 == 0 else 1
        return per_device(chunks, rhs, dinv, spikes, merge_inv)

    return jax.shard_map(
        body,
        mesh=mesh,
        in_specs=placed,
        out_specs=P(None, ("energy", "slab"), None, ("col", "orb")),
        check_vma=False,
    )
```

time: 200 us -> 60.7 us (0.30)
  waiting for transfers between devices: 141 us -> 34.1 us
  between operations: 13.3 us -> 0.3 us
  matrix products: 9.68 us -> 0 us
  local copies, waits for them, and re-layouts: 10.2 us -> 2.38 us
  Pallas kernels: 0 us -> 6.94 us
  starting transfers between devices: 20.4 us -> 15.6 us
  other arithmetic: 4.16 us -> 1.11 us
    ppermute x8 -> x18, waiting for transfers between devices: 112 us -> 34.1 us  [the longest x2 15.7 us: per_device(): moved = [lax.ppermute(tips[c], 'slab', route) for c in range(chunks)]]
    all_gather x3 -> x0, waiting for transfers between devices: 27.9 us -> none  [the longest x1 10.3 us: per_device(): lax.all_gather(dinv, 'orb', axis=2, tiled=True)]
    dot_general x20 -> x0, matrix products: 9.68 us -> none  [the longest x5 2.73 us: complex_product(): jnp.dot(matrix[0], operand[1], preferred_element_type=jnp.float32)]
    pallas_call x0 -> x13, Pallas kernels: none -> 6.94 us  [call(): pl.pallas_call(body, out_shape=outs, in_specs=[VMEM] * len(args), out_spe...]
    ppermute x8 -> x18, starting transfers between devices: 20.3 us -> 15.6 us  [the longest x4 4.47 us: per_device(): arrived = [lax.ppermute(zl[c], 'slab', up) for c in range(chunks)]]
    cond x13 -> x0, local copies, waits for them, and re-layouts: 3.71 us -> none
    unnamed x7 -> x6, local copies, waits for them, and re-layouts: 3.23 us -> 0.02 us
    select_n x4 -> x0, other arithmetic: 2.31 us -> none  [spread_group(): values = jnp.where(receive_mask, partner, values)]
  transfers between devices with their start and end apart: 11 -> 18, of which waited for: 10 -> 7; matrix products, arithmetic and copies ran while one was open for 4% -> 2% of each run, Pallas kernels for 0% -> 10%
where the time goes in v1:
time: 60.7 us; the launch traced here: 60.4 us
  waiting for transfers between devices  34.1 us (56%)
  starting transfers between devices  15.6 us (26%)
  Pallas kernels  6.94 us (11%)
  local copies, waits for them, and re-layouts  2.38 us (4%)
  other arithmetic  1.11 us (2%)
    ppermute x2, waiting for transfers between devices, per_device(): moved = [lax.ppermute(tips[c], 'slab', route) for c in range(chunks)]  15.7 us
    ppermute x1, waiting for transfers between devices, per_device(): quarter = lax.ppermute(mine, 'slab', backward)  7.53 us
    pallas_call x13, Pallas kernels, call(): pl.pallas_call(body, out_shape=outs, in_specs=[VMEM] * len(args), out_spe...  6.94 us
    ppermute x4, starting transfers between devices, per_device(): arrived = [lax.ppermute(zl[c], 'slab', up) for c in range(chunks)]  4.47 us
    ppermute x4, waiting for transfers between devices, per_device(): hb_next = [lax.ppermute(early[c], 'slab', down) for c in range(chunks)]  4.41 us
    ppermute x4, starting transfers between devices, per_device(): hb_next = [lax.ppermute(early[c], 'slab', down) for c in range(chunks)]  3.93 us
    ppermute x7, waiting for transfers between devices, ring_gather(): lax.ppermute(block, axis, [((i + step) % count, i) for i in range(count)])  3.76 us
    ppermute x7, starting transfers between devices, ring_gather(): lax.ppermute(block, axis, [((i + step) % count, i) for i in range(count)])  3.32 us
  transfers between devices with their start and end apart: 18, of which 7 were waited for; matrix products, arithmetic and copies ran while one was open for 2% of the time, Pallas kernels for 10%

profile of v1, /device:TPU:0, one launch (start us, length us, event | category | flops | bytes accessed | tf_op | source)
XLA Modules:
  0.0 60.4 jit_solution(17915584347485987082)
XLA Ops:
  0.0 1.0 %dynamic-slice_bitcast_fusion = bf16[2,128,512]{2,1,0:T(8,128)(2,1)S(1)} fusion(bf16[2,1,2,256,512]{4,3,2,1,0:T(8,128)(2,1)} %param.6, s32[]{:T(128)S(6)} %select_n.8, s32[]{:T(128)S(6)} %select_n.9), kind=kLoop, calls=%fused_computation.5 | loop fusion | bytes 524296 | tf_op jit(solution)/shard_map/reshape | solution.py:269
  1.0 1.3 %collective-permute-start.4 = (bf16[2,128,512]{2,1,0:T(8,128)(2,1)S(1)}, bf16[2,128,512]{2,1,0:T(8,128)(2,1)S(1)}, u32[]{:S(2)}, u32[]{:S(2)}) collective-permute-start(bf16[2,128,512]{2,1,0:T(8,128)(2,1)S(1)} %dynamic-slice_bitcast_fusion), channel_id=1, source_target_pairs={{4,0},{8,4},{12,8},{5,1},{9,5},{13,9},{6,2},{10,6},{14,10},{7,3},{... | collective-permute-start | bytes 786440 | tf_op jit(solution)/shard_map/ppermute | solution.py:271
  2.4 0.5 collective-permute-start
  2.9 1.3 %slice_bitcast_fusion = (bf16[2,256,512]{2,1,0:T(8,128)(2,1)S(1)}, bf16[2,256,512]{2,1,0:T(8,128)(2,1)S(1)}) fusion(bf16[2,1,2,256,512]{4,3,2,1,0:T(8,128)(2,1)} %param.6), kind=kLoop, calls=%fused_computation.3 | loop fusion | bytes 2097152 | tf_op jit(solution)/shard_map/squeeze | solution.py:276
  4.4 0.4 collective-permute-start.3
  4.7 7.5 %collective-permute-done.4.refs_5_.refs_3_ = bf16[2,128,512]{2,1,0:T(8,128)(2,1)S(1)} collective-permute-done((bf16[2,128,512]{2,1,0:T(8,128)(2,1)S(1)}, bf16[2,128,512]{2,1,0:T(8,128)(2,1)S(1)}, u32[]{:S(2)}, u32[]{:S(2)}) %collective-permute-start.4) | collective-permute-done | bytes 262176 | tf_op jit(solution)/shard_map/ppermute | solution.py:271
  12.3 1.6 %collective-permute-start.5 = (bf16[2,128,512]{2,1,0:T(8,128)(2,1)S(1)}, bf16[2,128,512]{2,1,0:T(8,128)(2,1)S(1)}, u32[]{:S(2)}, u32[]{:S(2)}) collective-permute-start(bf16[2,128,512]{2,1,0:T(8,128)(2,1)S(1)} %collective-permute-done.4.refs_5_.refs_3_), channel_id=1, source_target_pairs={{2,0},{0,2},{3,1},{1,3},{6,4},{4,6},{7,5},{5,7},{10,8},{8,10},{11,... | collective-permute-start | bytes 786440 | tf_op jit(solution)/shard_map/ppermute | solution.py:17
  13.9 0.7 %shard_map.46 = (f32[512,256]{1,0:T(8,128)S(1)}, bf16[512,256]{1,0:T(8,128)(2,1)S(1)}, f32[512,256]{1,0:T(8,128)S(1)}, bf16[512,256]{1,0:T(8,128)(2,1)S(1)}) custom-call(bf16[2,256,512]{2,1,0:T(8,128)(2,1)S(1)} %bitcast.27, bf16[2,256,512]{2,1,0:T(8,128)(2,1)S(1)} %collective-permute-done.refs_1_, bf16[2,512,256]{2,1,0:T(8,128)(2,1)S(1)} %bitcast.28), custom_call_target="tpu_custom_call" | custom-call | flops 536870912 | bytes 3145728 | tf_op jit(solution)/shard_map/pallas_call | solution.py:58
  14.6 1.3 %collective-permute-start.1 = (bf16[512,256]{1,0:T(8,128)(2,1)S(1)}, bf16[512,256]{1,0:T(8,128)(2,1)S(1)}, u32[]{:S(2)}, u32[]{:S(2)}) collective-permute-start(bf16[512,256]{1,0:T(8,128)(2,1)S(1)} %get-tuple-element.16), channel_id=1, source_target_pairs={{4,0},{12,8},{5,1},{13,9},{6,2},{14,10},{7,3},{15,11},{20,16},{28,... | collective-permute-start | bytes 786440 | tf_op jit(solution)/shard_map/ppermute | solution.py:300
  16.0 3.7 %collective-permute-done.5.refs_6_.refs_4_ = bf16[2,128,512]{2,1,0:T(8,128)(2,1)S(1)} collective-permute-done((bf16[2,128,512]{2,1,0:T(8,128)(2,1)S(1)}, bf16[2,128,512]{2,1,0:T(8,128)(2,1)S(1)}, u32[]{:S(2)}, u32[]{:S(2)}) %collective-permute-start.5) | collective-permute-done | bytes 262176 | tf_op jit(solution)/shard_map/ppermute | solution.py:17
  19.8 0.5 collective-permute-start.10
  20.3 1.3 %collective-permute-start.13 = (bf16[512,256]{1,0:T(8,128)(2,1)S(1)}, bf16[512,256]{1,0:T(8,128)(2,1)S(1)}, u32[]{:S(2)}, u32[]{:S(2)}) collective-permute-start(bf16[512,256]{1,0:T(8,128)(2,1)S(1)} %get-tuple-element.21), channel_id=1, source_target_pairs={{4,0},{12,8},{5,1},{13,9},{6,2},{14,10},{7,3},{15,11},{20,16},{28,... | collective-permute-start | bytes 786440 | tf_op jit(solution)/shard_map/ppermute | solution.py:300
  21.6 1.9 %collective-permute-done.1.refs_1_ = bf16[512,256]{1,0:T(8,128)(2,1)S(1)} collective-permute-done((bf16[512,256]{1,0:T(8,128)(2,1)S(1)}, bf16[512,256]{1,0:T(8,128)(2,1)S(1)}, u32[]{:S(2)}, u32[]{:S(2)}) %collective-permute-start.1) | collective-permute-done | bytes 262176 | tf_op jit(solution)/shard_map/ppermute | solution.py:300
  23.4 0.9 %shard_map.47.refs_2_ = bf16[512,256]{1,0:T(8,128)(2,1)S(1)} custom-call(f32[512,256]{1,0:T(8,128)S(1)} %get-tuple-element.15.refs_0_, bf16[512,256]{1,0:T(8,128)(2,1)S(1)} %collective-permute-done.1.refs_1_, bf16[2,256,512]{2,1,0:T(8,128)(2,1)S(1)} %get-tuple-element.26.refs_2_.refs_3_, bf16[2,256,512]{2,1,0:T(8,128)(2,1)S(1)} %collective-permute-done.2.refs_3_.refs_4_, ...), custom_call_target="tpu_custom_call" | custom-call | flops 536870912 | bytes 3145728 | tf_op jit(solution)/shard_map/pallas_call | solution.py:58
  24.4 1.8 %collective-permute-start.8 = (bf16[512,256]{1,0:T(8,128)(2,1)S(1)}, bf16[512,256]{1,0:T(8,128)(2,1)S(1)}, u32[]{:S(2)}, u32[]{:S(2)}) collective-permute-start(bf16[512,256]{1,0:T(8,128)(2,1)S(1)} %shard_map.47.refs_2_), channel_id=1, source_target_pairs={{0,4},{8,12},{1,5},{9,13},{2,6},{10,14},{3,7},{11,15},{16,20},{24,... | collective-permute-start | bytes 786440 | tf_op jit(solution)/shard_map/ppermute | solution.py:302
  26.2 0.9 %shard_map.48 = (f32[512,256]{1,0:T(8,128)S(1)}, bf16[512,256]{1,0:T(8,128)(2,1)S(1)}) custom-call(f32[512,256]{1,0:T(8,128)S(1)} %get-tuple-element.15.refs_0_, bf16[512,256]{1,0:T(8,128)(2,1)S(1)} %collective-permute-done.1.refs_1_, bf16[512,256]{1,0:T(8,128)(2,1)S(1)} %shard_map.47.refs_2_, bf16[2,256,512]{2,1,0:T(8,128)(2,1)S(1)} %get-tuple-element.26.refs_2_.refs_3_, ...), custom_call_target="tpu_custom_call" | custom-call | flops 536870912 | bytes 3932160 | tf_op jit(solution)/shard_map/pallas_call | solution.py:58
  27.1 0.7 %collective-permute-start.9 = (bf16[512,256]{1,0:T(8,128)(2,1)S(1)}, bf16[512,256]{1,0:T(8,128)(2,1)S(1)}, u32[]{:S(2)}, u32[]{:S(2)}) collective-permute-start(bf16[512,256]{1,0:T(8,128)(2,1)S(1)} %get-tuple-element.18), channel_id=1, source_target_pairs={{8,4},{9,5},{10,6},{11,7},{24,20},{25,21},{26,22},{27,23}} | collective-permute-start | bytes 786440 | tf_op jit(solution)/shard_map/ppermute | solution.py:300
  27.8 2.5 %collective-permute-done.13.refs_1_ = bf16[512,256]{1,0:T(8,128)(2,1)S(1)} collective-permute-done((bf16[512,256]{1,0:T(8,128)(2,1)S(1)}, bf16[512,256]{1,0:T(8,128)(2,1)S(1)}, u32[]{:S(2)}, u32[]{:S(2)}) %collective-permute-start.13) | collective-permute-done | bytes 262176 | tf_op jit(solution)/shard_map/ppermute | solution.py:300
  30.4 0.9 %shard_map.53.refs_2_ = bf16[512,256]{1,0:T(8,128)(2,1)S(1)} custom-call(f32[512,256]{1,0:T(8,128)S(1)} %get-tuple-element.20.refs_0_, bf16[512,256]{1,0:T(8,128)(2,1)S(1)} %collective-permute-done.13.refs_1_, bf16[2,256,512]{2,1,0:T(8,128)(2,1)S(1)} %get-tuple-element.26.refs_2_.refs_3_, bf16[2,256,512]{2,1,0:T(8,128)(2,1)S(1)} %collective-permute-done.2.refs_3_.refs_4_, ...), custom_call_target="tpu_custom_call" | custom-call | flops 536870912 | bytes 3145728 | tf_op jit(solution)/shard_map/pallas_call | solution.py:58
  31.3 1.3 %collective-permute-start.14 = (bf16[512,256]{1,0:T(8,128)(2,1)S(1)}, bf16[512,256]{1,0:T(8,128)(2,1)S(1)}, u32[]{:S(2)}, u32[]{:S(2)}) collective-permute-start(bf16[512,256]{1,0:T(8,128)(2,1)S(1)} %shard_map.53.refs_2_), channel_id=1, source_target_pairs={{0,4},{8,12},{1,5},{9,13},{2,6},{10,14},{3,7},{11,15},{16,20},{24,... | collective-permute-start | bytes 786440 | tf_op jit(solution)/shard_map/ppermute | solution.py:302
  32.6 0.9 %shard_map.54 = (f32[512,256]{1,0:T(8,128)S(1)}, bf16[512,256]{1,0:T(8,128)(2,1)S(1)}) custom-call(f32[512,256]{1,0:T(8,128)S(1)} %get-tuple-element.20.refs_0_, bf16[512,256]{1,0:T(8,128)(2,1)S(1)} %collective-permute-done.13.refs_1_, bf16[512,256]{1,0:T(8,128)(2,1)S(1)} %shard_map.53.refs_2_, bf16[2,256,512]{2,1,0:T(8,128)(2,1)S(1)} %get-tuple-element.26.refs_2_.refs_3_, ...), custom_call_target="tpu_custom_call" | custom-call | flops 536870912 | bytes 3932160 | tf_op jit(solution)/shard_map/pallas_call | solution.py:58
  33.6 0.7 %collective-permute-start.15 = (bf16[512,256]{1,0:T(8,128)(2,1)S(1)}, bf16[512,256]{1,0:T(8,128)(2,1)S(1)}, u32[]{:S(2)}, u32[]{:S(2)}) collective-permute-start(bf16[512,256]{1,0:T(8,128)(2,1)S(1)} %get-tuple-element.23), channel_id=1, source_target_pairs={{8,4},{9,5},{10,6},{11,7},{24,20},{25,21},{26,22},{27,23}} | collective-permute-start | bytes 786440 | tf_op jit(solution)/shard_map/ppermute | solution.py:300
  34.4 0.7 %collective-permute-start.11 = (bf16[512,256]{1,0:T(8,128)(2,1)S(1)}, bf16[512,256]{1,0:T(8,128)(2,1)S(1)}, u32[]{:S(2)}, u32[]{:S(2)}) collective-permute-start(bf16[512,256]{1,0:T(8,128)(2,1)S(1)} %shard_map.50.refs_1_), channel_id=1, source_target_pairs={{4,8},{5,9},{6,10},{7,11},{20,24},{21,25},{22,26},{23,27}} | collective-permute-start | bytes 786440 | tf_op jit(solution)/shard_map/ppermute | solution.py:302
  35.1 2.7 %collective-permute-done.14.refs_1_ = bf16[512,256]{1,0:T(8,128)(2,1)S(1)} collective-permute-done((bf16[512,256]{1,0:T(8,128)(2,1)S(1)}, bf16[512,256]{1,0:T(8,128)(2,1)S(1)}, u32[]{:S(2)}, u32[]{:S(2)}) %collective-permute-start.14) | collective-permute-done | bytes 262176 | tf_op jit(solution)/shard_map/ppermute | solution.py:302
  37.9 0.7 %collective-permute-start.16 = (bf16[512,256]{1,0:T(8,128)(2,1)S(1)}, bf16[512,256]{1,0:T(8,128)(2,1)S(1)}, u32[]{:S(2)}, u32[]{:S(2)}) collective-permute-start(bf16[512,256]{1,0:T(8,128)(2,1)S(1)} %shard_map.56.refs_1_), channel_id=1, source_target_pairs={{4,8},{5,9},{6,10},{7,11},{20,24},{21,25},{22,26},{23,27}} | collective-permute-start | bytes 786440 | tf_op jit(solution)/shard_map/ppermute | solution.py:302
  38.6 1.3 %collective-permute-start.12 = (bf16[512,256]{1,0:T(8,128)(2,1)S(1)}, bf16[512,256]{1,0:T(8,128)(2,1)S(1)}, u32[]{:S(2)}, u32[]{:S(2)}) collective-permute-start(bf16[512,256]{1,0:T(8,128)(2,1)S(1)} %shard_map.51.refs_2_), channel_id=1, source_target_pairs={{8,12},{4,0},{9,13},{5,1},{10,14},{6,2},{11,15},{7,3},{24,28},{20,... | collective-permute-start | bytes 786440 | tf_op jit(solution)/shard_map/ppermute | solution.py:319
  40.0 1.3 %collective-permute-start.17 = (bf16[512,256]{1,0:T(8,128)(2,1)S(1)}, bf16[512,256]{1,0:T(8,128)(2,1)S(1)}, u32[]{:S(2)}, u32[]{:S(2)}) collective-permute-start(bf16[512,256]{1,0:T(8,128)(2,1)S(1)} %shard_map.57.refs_2_), channel_id=1, source_target_pairs={{8,12},{4,0},{9,13},{5,1},{10,14},{6,2},{11,15},{7,3},{24,28},{20,... | collective-permute-start | bytes 786440 | tf_op jit(solution)/shard_map/ppermute | solution.py:319
  41.3 12.6 %collective-permute-done.12.refs_1_ = bf16[512,256]{1,0:T(8,128)(2,1)S(1)} collective-permute-done((bf16[512,256]{1,0:T(8,128)(2,1)S(1)}, bf16[512,256]{1,0:T(8,128)(2,1)S(1)}, u32[]{:S(2)}, u32[]{:S(2)}) %collective-permute-start.12) | collective-permute-done | bytes 262176 | tf_op jit(solution)/shard_map/ppermute | solution.py:319
  53.9 1.1 %shard_map.52 = (f32[512,256]{1,0:T(8,128)S(1)}, bf16[512,256]{1,0:T(8,128)(2,1)}) custom-call(f32[512,256]{1,0:T(8,128)S(1)} %shard_map.49.refs_0_, bf16[512,256]{1,0:T(8,128)(2,1)S(1)} %collective-permute-done.12.refs_1_, bf16[512,256]{1,0:T(8,128)(2,1)S(1)} %shard_map.51.refs_2_, bf16[2,256,512]{2,1,0:T(8,128)(2,1)S(1)} %get-tuple-element.25.refs_2_.refs_3_, ...), custom_call_target="tpu_custom_call" | custom-call | flops 268435456 | bytes 2883584 | tf_op jit(solution)/shard_map/pallas_call | solution.py:58
  55.1 3.1 %collective-permute-done.17.refs_1_ = bf16[512,256]{1,0:T(8,128)(2,1)S(1)} collective-permute-done((bf16[512,256]{1,0:T(8,128)(2,1)S(1)}, bf16[512,256]{1,0:T(8,128)(2,1)S(1)}, u32[]{:S(2)}, u32[]{:S(2)}) %collective-permute-start.17) | collective-permute-done | bytes 262176 | tf_op jit(solution)/shard_map/ppermute | solution.py:319
  58.1 1.1 %shard_map.58 = (f32[512,256]{1,0:T(8,128)S(1)}, bf16[512,256]{1,0:T(8,128)(2,1)}) custom-call(f32[512,256]{1,0:T(8,128)S(1)} %shard_map.55.refs_0_, bf16[512,256]{1,0:T(8,128)(2,1)S(1)} %collective-permute-done.17.refs_1_, bf16[512,256]{1,0:T(8,128)(2,1)S(1)} %shard_map.57.refs_2_, bf16[2,256,512]{2,1,0:T(8,128)(2,1)S(1)} %get-tuple-element.25.refs_2_.refs_3_, ...), custom_call_target="tpu_custom_call" | custom-call | flops 268435456 | bytes 2883584 | tf_op jit(solution)/shard_map/pallas_call | solution.py:58
  59.4 1.0 %maximum_bitcast_fusion = f32[2,1,512,256]{3,2,1,0:T(8,128)} fusion(f32[1,512,256]{2,1,0:T(8,128)S(1)} %get-tuple-element.32, f32[1,512,256]{2,1,0:T(8,128)S(1)} %get-tuple-element.31), kind=kLoop, calls=%fused_computation | loop fusion | flops 262144 | bytes 2097152 | tf_op jit(solution)/shard_map/broadcast_in_dim | solution.py:335
  (29 shorter events, 0.7 us)
Async XLA Ops:
  0.0 2.3 %copy-start.1 = (bf16[2,1,256,512]{3,2,1,0:T(8,128)(2,1)S(1)}, bf16[2,1,256,512]{3,2,1,0:T(8,128)(2,1)}, u32[]{:S(2)}) copy-start(bf16[2,1,256,512]{3,2,1,0:T(8,128)(2,1)} %param.5) | copy-start | bytes 1572868
  1.0 11.2 %collective-permute-start.4 = (bf16[2,128,512]{2,1,0:T(8,128)(2,1)S(1)}, bf16[2,128,512]{2,1,0:T(8,128)(2,1)S(1)}, u32[]{:S(2)}, u32[]{:S(2)}) collective-permute-start(bf16[2,128,512]{2,1,0:T(8,128)(2,1)S(1)} %dynamic-slice_bitcast_fusion), channel_id=1, source_target_pairs={{4,0},{8,4},{12,8},{5,1},{9,5},{13,9},{6,2},{10,6},{14,10},{7,3},{... | collective-permute-start | bytes 786440 | tf_op jit(solution)/shard_map/ppermute | solution.py:271
  2.3 2.0 %copy-start = (bf16[2,1,256,512]{3,2,1,0:T(8,128)(2,1)S(1)}, bf16[2,1,256,512]{3,2,1,0:T(8,128)(2,1)}, u32[]{:S(2)}) copy-start(bf16[2,1,256,512]{3,2,1,0:T(8,128)(2,1)} %param.7) | copy-start | bytes 1572868
  2.4 11.6 %copy-start.2 = (bf16[2,1,512,256]{3,2,1,0:T(8,128)(2,1)S(1)}, bf16[2,1,512,256]{3,2,1,0:T(8,128)(2,1)}, u32[]{:S(2)}) copy-start(bf16[2,1,512,256]{3,2,1,0:T(8,128)(2,1)} %param.4) | copy-start | bytes 1572868
  2.4 11.5 %collective-permute-start = (bf16[2,256,512]{2,1,0:T(8,128)(2,1)S(1)}, bf16[2,256,512]{2,1,0:T(8,128)(2,1)S(1)}, u32[]{:S(2)}, u32[]{:S(2)}) collective-permute-start(bf16[2,256,512]{2,1,0:T(8,128)(2,1)S(1)} %bitcast.26), channel_id=1, source_target_pairs={{1,0},{0,1},{3,2},{2,3},{5,4},{4,5},{7,6},{6,7},{9,8},{8,9},{11,10... | collective-permute-start | bytes 1572872 | tf_op jit(solution)/shard_map/ppermute | solution.py:17
  4.2 15.6 %collective-permute-start.2 = (bf16[2,256,512]{2,1,0:T(8,128)(2,1)S(1)}, bf16[2,256,512]{2,1,0:T(8,128)(2,1)S(1)}, u32[]{:S(2)}, u32[]{:S(2)}) collective-permute-start(bf16[2,256,512]{2,1,0:T(8,128)(2,1)S(1)} %get-tuple-element.26.refs_2_.refs_3_), channel_id=1, source_target_pairs={{1,0},{0,1},{3,2},{2,3},{5,4},{4,5},{7,6},{6,7},{9,8},{8,9},{11,10... | collective-permute-start | bytes 1572872 | tf_op jit(solution)/shard_map/ppermute | solution.py:17
  4.4 15.9 %collective-permute-start.3 = (bf16[2,256,512]{2,1,0:T(8,128)(2,1)S(1)}, bf16[2,256,512]{2,1,0:T(8,128)(2,1)S(1)}, u32[]{:S(2)}, u32[]{:S(2)}) collective-permute-start(bf16[2,256,512]{2,1,0:T(8,128)(2,1)S(1)} %bitcast.21), channel_id=1, source_target_pairs={{1,0},{0,1},{3,2},{2,3},{5,4},{4,5},{7,6},{6,7},{9,8},{8,9},{11,10... | collective-permute-start | bytes 1572872 | tf_op jit(solution)/shard_map/ppermute | solution.py:17
  12.3 7.5 %collective-permute-start.5 = (bf16[2,128,512]{2,1,0:T(8,128)(2,1)S(1)}, bf16[2,128,512]{2,1,0:T(8,128)(2,1)S(1)}, u32[]{:S(2)}, u32[]{:S(2)}) collective-permute-start(bf16[2,128,512]{2,1,0:T(8,128)(2,1)S(1)} %collective-permute-done.4.refs_5_.refs_3_), channel_id=1, source_target_pairs={{2,0},{0,2},{3,1},{1,3},{6,4},{4,6},{7,5},{5,7},{10,8},{8,10},{11,... | collective-permute-start | bytes 786440 | tf_op jit(solution)/shard_map/ppermute | solution.py:17
  14.6 8.8 %collective-permute-start.1 = (bf16[512,256]{1,0:T(8,128)(2,1)S(1)}, bf16[512,256]{1,0:T(8,128)(2,1)S(1)}, u32[]{:S(2)}, u32[]{:S(2)}) collective-permute-start(bf16[512,256]{1,0:T(8,128)(2,1)S(1)} %get-tuple-element.16), channel_id=1, source_target_pairs={{4,0},{12,8},{5,1},{13,9},{6,2},{14,10},{7,3},{15,11},{20,16},{28,... | collective-permute-start | bytes 786440 | tf_op jit(solution)/shard_map/ppermute | solution.py:300
  15.9 10.3 %collective-permute-start.6 = (bf16[2,128,512]{2,1,0:T(8,128)(2,1)S(1)}, bf16[2,128,512]{2,1,0:T(8,128)(2,1)S(1)}, u32[]{:S(2)}, u32[]{:S(2)}) collective-permute-start(bf16[2,128,512]{2,1,0:T(8,128)(2,1)S(1)} %collective-permute-done.4.refs_5_.refs_3_), channel_id=1, source_target_pairs={{1,0},{0,1},{3,2},{2,3},{5,4},{4,5},{7,6},{6,7},{9,8},{8,9},{11,10... | collective-permute-start | bytes 786440 | tf_op jit(solution)/shard_map/ppermute | solution.py:17
  19.8 6.4 %collective-permute-start.7 = (bf16[2,128,512]{2,1,0:T(8,128)(2,1)S(1)}, bf16[2,128,512]{2,1,0:T(8,128)(2,1)S(1)}, u32[]{:S(2)}, u32[]{:S(2)}) collective-permute-start(bf16[2,128,512]{2,1,0:T(8,128)(2,1)S(1)} %collective-permute-done.5.refs_6_.refs_4_), channel_id=1, source_target_pairs={{1,0},{0,1},{3,2},{2,3},{5,4},{4,5},{7,6},{6,7},{9,8},{8,9},{11,10... | collective-permute-start | bytes 786440 | tf_op jit(solution)/shard_map/ppermute | solution.py:17
  19.8 14.6 %collective-permute-start.10 = (bf16[2,256,512]{2,1,0:T(8,128)(2,1)S(1)}, bf16[2,256,512]{2,1,0:T(8,128)(2,1)S(1)}, u32[]{:S(2)}, u32[]{:S(2)}) collective-permute-start(bf16[2,256,512]{2,1,0:T(8,128)(2,1)S(1)} %get-tuple-element.25.refs_2_.refs_3_), channel_id=1, source_target_pairs={{1,0},{0,1},{3,2},{2,3},{5,4},{4,5},{7,6},{6,7},{9,8},{8,9},{11,10... | collective-permute-start | bytes 1572872 | tf_op jit(solution)/shard_map/ppermute | solution.py:17
  20.3 10.1 %collective-permute-start.13 = (bf16[512,256]{1,0:T(8,128)(2,1)S(1)}, bf16[512,256]{1,0:T(8,128)(2,1)S(1)}, u32[]{:S(2)}, u32[]{:S(2)}) collective-permute-start(bf16[512,256]{1,0:T(8,128)(2,1)S(1)} %get-tuple-element.21), channel_id=1, source_target_pairs={{4,0},{12,8},{5,1},{13,9},{6,2},{14,10},{7,3},{15,11},{20,16},{28,... | collective-permute-start | bytes 786440 | tf_op jit(solution)/shard_map/ppermute | solution.py:300
  24.4 9.9 %collective-permute-start.8 = (bf16[512,256]{1,0:T(8,128)(2,1)S(1)}, bf16[512,256]{1,0:T(8,128)(2,1)S(1)}, u32[]{:S(2)}, u32[]{:S(2)}) collective-permute-start(bf16[512,256]{1,0:T(8,128)(2,1)S(1)} %shard_map.47.refs_2_), channel_id=1, source_target_pairs={{0,4},{8,12},{1,5},{9,13},{2,6},{10,14},{3,7},{11,15},{16,20},{24,... | collective-permute-start | bytes 786440 | tf_op jit(solution)/shard_map/ppermute | solution.py:302
  27.1 7.2 %collective-permute-start.9 = (bf16[512,256]{1,0:T(8,128)(2,1)S(1)}, bf16[512,256]{1,0:T(8,128)(2,1)S(1)}, u32[]{:S(2)}, u32[]{:S(2)}) collective-permute-start(bf16[512,256]{1,0:T(8,128)(2,1)S(1)} %get-tuple-element.18), channel_id=1, source_target_pairs={{8,4},{9,5},{10,6},{11,7},{24,20},{25,21},{26,22},{27,23}} | collective-permute-start | bytes 786440 | tf_op jit(solution)/shard_map/ppermute | solution.py:300
  31.3 6.5 %collective-permute-start.14 = (bf16[512,256]{1,0:T(8,128)(2,1)S(1)}, bf16[512,256]{1,0:T(8,128)(2,1)S(1)}, u32[]{:S(2)}, u32[]{:S(2)}) collective-permute-start(bf16[512,256]{1,0:T(8,128)(2,1)S(1)} %shard_map.53.refs_2_), channel_id=1, source_target_pairs={{0,4},{8,12},{1,5},{9,13},{2,6},{10,14},{3,7},{11,15},{16,20},{24,... | collective-permute-start | bytes 786440 | tf_op jit(solution)/shard_map/ppermute | solution.py:302
  33.6 4.2 %collective-permute-start.15 = (bf16[512,256]{1,0:T(8,128)(2,1)S(1)}, bf16[512,256]{1,0:T(8,128)(2,1)S(1)}, u32[]{:S(2)}, u32[]{:S(2)}) collective-permute-start(bf16[512,256]{1,0:T(8,128)(2,1)S(1)} %get-tuple-element.23), channel_id=1, source_target_pairs={{8,4},{9,5},{10,6},{11,7},{24,20},{25,21},{26,22},{27,23}} | collective-permute-start | bytes 786440 | tf_op jit(solution)/shard_map/ppermute | solution.py:300
  34.4 4.2 %collective-permute-start.11 = (bf16[512,256]{1,0:T(8,128)(2,1)S(1)}, bf16[512,256]{1,0:T(8,128)(2,1)S(1)}, u32[]{:S(2)}, u32[]{:S(2)}) collective-permute-start(bf16[512,256]{1,0:T(8,128)(2,1)S(1)} %shard_map.50.refs_1_), channel_id=1, source_target_pairs={{4,8},{5,9},{6,10},{7,11},{20,24},{21,25},{22,26},{23,27}} | collective-permute-start | bytes 786440 | tf_op jit(solution)/shard_map/ppermute | solution.py:302
  37.9 2.0 %collective-permute-start.16 = (bf16[512,256]{1,0:T(8,128)(2,1)S(1)}, bf16[512,256]{1,0:T(8,128)(2,1)S(1)}, u32[]{:S(2)}, u32[]{:S(2)}) collective-permute-start(bf16[512,256]{1,0:T(8,128)(2,1)S(1)} %shard_map.56.refs_1_), channel_id=1, source_target_pairs={{4,8},{5,9},{6,10},{7,11},{20,24},{21,25},{22,26},{23,27}} | collective-permute-start | bytes 786440 | tf_op jit(solution)/shard_map/ppermute | solution.py:302
  38.6 15.3 %collective-permute-start.12 = (bf16[512,256]{1,0:T(8,128)(2,1)S(1)}, bf16[512,256]{1,0:T(8,128)(2,1)S(1)}, u32[]{:S(2)}, u32[]{:S(2)}) collective-permute-start(bf16[512,256]{1,0:T(8,128)(2,1)S(1)} %shard_map.51.refs_2_), channel_id=1, source_target_pairs={{8,12},{4,0},{9,13},{5,1},{10,14},{6,2},{11,15},{7,3},{24,28},{20,... | collective-permute-start | bytes 786440 | tf_op jit(solution)/shard_map/ppermute | solution.py:319
  40.0 18.2 %collective-permute-start.17 = (bf16[512,256]{1,0:T(8,128)(2,1)S(1)}, bf16[512,256]{1,0:T(8,128)(2,1)S(1)}, u32[]{:S(2)}, u32[]{:S(2)}) collective-permute-start(bf16[512,256]{1,0:T(8,128)(2,1)S(1)} %shard_map.57.refs_2_), channel_id=1, source_target_pairs={{8,12},{4,0},{9,13},{5,1},{10,14},{6,2},{11,15},{7,3},{24,28},{20,... | collective-permute-start | bytes 786440 | tf_op jit(solution)/shard_map/ppermute | solution.py:319

commit v2 on v1

v2 whole, which is shorter than its diff:
```python
import jax
import jax.numpy as jnp
from jax import lax
from jax.experimental import pallas as pl
from jax.experimental.pallas import tpu as pltpu
from jax.sharding import PartitionSpec as P

VMEM = pl.BlockSpec(memory_space=pltpu.VMEM)
SHARES = (1, 1)


def ring_gather(block, axis):
    count = lax.axis_size(axis)
    blocks = [block]
    for step in range(1, count):
        blocks.append(lax.ppermute(block, axis, [((i + step) % count, i) for i in range(count)]))
    return blocks


def row_starts(height, orb_count, col_parts):
    orb = lax.axis_index("orb")
    per_orb = height // orb_count
    starts = []
    for j in range(orb_count):
        base = lax.rem(orb + j, orb_count) * per_orb
        if col_parts == 1:
            starts.append(base)
            continue
        col = lax.axis_index("col")
        for k in range(col_parts):
            starts.append(base + lax.rem(col + k, col_parts) * (per_orb // col_parts))
    return starts


def rows_of(start, size):
    return pl.ds(pl.multiple_of(start, size), size)


def turned(field):
    half = field.shape[1] // 2
    return jnp.concatenate([-field[:, half:], field[:, :half]], axis=1)


def at_level(spikes, level):
    return [tuple(lambda s=s, p=p: s[p, level] for p in range(2)) for s in spikes]


def parts_of(pieces):
    return [tuple(lambda m=m, p=p: m[p] for p in range(2)) for m in pieces]


def packed(refs, height, width):
    blocks = height // width
    size = (refs[0].shape[0] - height) // (2 * blocks)

    def load(ref, part):
        first = height + part * blocks * size
        return jnp.concatenate([ref[pl.ds(first + k * size, size), :] for k in range(blocks)], axis=1)

    return [tuple(lambda r=r, p=p: load(r, p) for p in range(2)) for r in refs]


def each_product(pieces, starts, field):
    field_i = turned(field)
    for (real, imag), start in zip(pieces, starts):
        value = jnp.dot(real(), field, preferred_element_type=jnp.float32)
        value += jnp.dot(imag(), field_i, preferred_element_type=jnp.float32)
        yield rows_of(start, value.shape[0]), value


def call(body, outs, scratch, *args, flops=0, aliases=None):
    nbytes = sum(a.size * a.dtype.itemsize for a in args) + sum(o.size * o.dtype.itemsize for o in outs)
    return pl.pallas_call(
        body,
        out_shape=outs,
        in_specs=[VMEM] * len(args),
        out_specs=[VMEM] * len(outs),
        scratch_shapes=scratch,
        compiler_params=pltpu.CompilerParams(vmem_limit_bytes=24 * 2**20),
        cost_estimate=pl.CostEstimate(flops=flops, bytes_accessed=nbytes, transcendentals=0),
    )(*args)


def product_flops(height, width):
    return 2 * 2 * height * height * width


def is_even():
    return lax.rem(lax.axis_index("slab"), 2) == 0


def lowest_bit(number, levels):
    found = jnp.int32(0)
    for level in range(1, levels):
        found = jnp.where(lax.rem(number, 1 << level) == 0, level, found)
    return found


def start_state(pieces, rhs, first, width):
    height = rhs.shape[1]
    n = len(pieces)

    def body(*refs):
        mats, rhs_ref, (out, out_b) = refs[:n], refs[n], refs[n + 1 :]
        window = pl.ds(first, width)
        field = jnp.concatenate([rhs_ref[0, :, window], rhs_ref[1, :, window]], axis=1)
        for rows, value in each_product(parts_of(mats), row_starts(height, n, 1), field):
            out[rows, :] = value
            out_b[rows, :] = value.astype(jnp.bfloat16)

    outs = [jax.ShapeDtypeStruct((height, 2 * width), t) for t in (jnp.float32, jnp.bfloat16)]
    return call(body, outs, [], *pieces, rhs, flops=product_flops(height, 2 * width))


def send_field(odd_sends_product, merge_refs, height, hb_ref, store):
    n = len(merge_refs)
    left = jnp.logical_xor(is_even(), odd_sends_product)

    @pl.when(left)
    def _():
        for rows, value in each_product(parts_of(merge_refs), row_starts(height, n, 1), hb_ref[...]):
            store(rows, value.astype(jnp.bfloat16))

    @pl.when(jnp.logical_not(left))
    def _():
        store(pl.ds(0, height), hb_ref[...])


def first_sends(spikes, merge, hb, levels):
    height, width = hb.shape
    n = len(spikes)
    size = height // n
    blocks = height // width
    cut = min(128, width)

    def body(*refs):
        spike_refs, merge_refs, hb_ref = refs[:n], refs[n : 2 * n], refs[2 * n]
        q_out, pay, later = refs[2 * n + 1 :]
        device = lax.axis_index("slab")
        level_left = lowest_bit(device + 1, levels)
        level_right = lowest_bit(device, levels)
        starts = row_starts(height, n, 1)

        def columns(k, carry):
            window = pl.ds(pl.multiple_of(k * cut, cut), cut)
            order = [jnp.concatenate([s[p, level_left, :, window] for s in spike_refs], axis=0) for p in range(2)]
            if n > 1:
                first = lax.axis_index("orb")
                order = [in_place(x, first, n) for x in order]
            field = jnp.concatenate(order, axis=1)
            for _, value in each_product(parts_of(merge_refs[:1]), starts[:1], field):
                q_out[0, :, window] = value[:, :cut].astype(jnp.bfloat16)
                q_out[1, :, window] = value[:, cut:].astype(jnp.bfloat16)
            return carry

        lax.fori_loop(0, height // cut, columns, 0)

        def pack(source):
            for p in range(2):
                for k in range(blocks):
                    pay[pl.ds(height + (p * blocks + k) * size, size), :] = source(p, pl.ds(k * width, width))

        @pl.when(is_even())
        def _():
            pack(lambda p, window: q_out[p, :, window])
            for p in range(2):
                later[p] = spike_refs[0][p, level_right]

        @pl.when(jnp.logical_not(is_even()))
        def _():
            pack(lambda p, window: spike_refs[0][p, 0, :, window])
            later[...] = q_out[...]

        def store(rows, value):
            pay[rows, :] = value

        send_field(False, merge_refs, height, hb_ref, store)

    return call(
        body,
        [
            jax.ShapeDtypeStruct((2, size, height), jnp.bfloat16),
            jax.ShapeDtypeStruct((height + 2 * blocks * size, width), jnp.bfloat16),
            jax.ShapeDtypeStruct((2, size, height), jnp.bfloat16),
        ],
        [],
        *spikes, *merge, hb,
        flops=2 * product_flops(height, width),
    )


def in_place(rows, first, count):
    size = rows.shape[0] // count
    out = rows
    for shift in range(1, count):
        rolled = jnp.concatenate([rows[rows.shape[0] - shift * size :], rows[: rows.shape[0] - shift * size]], axis=0)
        out = jnp.where(first == shift, rolled, out)
    return out


def next_sends(merge, hb):
    height, width = hb.shape
    n = len(merge)

    def body(*refs):
        merge_refs, hb_ref, out = refs[:n], refs[n], refs[n + 1]

        def store(rows, value):
            out[rows, :] = value

        send_field(False, merge_refs, height, hb_ref, store)

    (out,) = call(
        body, [jax.ShapeDtypeStruct(hb.shape, jnp.bfloat16)], [], *merge, hb, flops=product_flops(height, width)
    )
    return out


def merge_tip(left, q_refs, mats, height, mine, got, source, store):
    n = len(q_refs)
    starts = row_starts(height, n, 1)

    @pl.when(left)
    def _():
        for rows, value in each_product(parts_of(q_refs), starts, got[pl.ds(0, height), :]):
            source[rows, :] = (mine[rows, :].astype(jnp.float32) - value).astype(jnp.bfloat16)

    @pl.when(jnp.logical_not(left))
    def _():
        source[...] = mine[pl.ds(0, height), :]

    for rows, value in each_product(mats, starts, source[...]):
        store(rows, (got[rows, :].astype(jnp.float32) - value).astype(jnp.bfloat16))


def first_level(state, mine, got, payloads, q, spikes, merge):
    height, width = state.shape
    n = len(q)

    def body(*refs):
        state_ref, mine_ref, got_ref = refs[:3]
        pay_refs, q_refs, spike_refs, merge_refs = (refs[3 + k * n : 3 + (k + 1) * n] for k in range(4))
        out, send, source, tip = refs[3 + 4 * n :]

        def store_tip(rows, value):
            tip[rows, :] = value

        merge_tip(is_even(), q_refs, packed(pay_refs, height, width), height, mine_ref, got_ref, source, store_tip)
        for rows, value in each_product(at_level(spike_refs, 0), row_starts(height, n, 1), tip[...]):
            new = state_ref[rows, :] - value
            out[rows, :] = new
            source[rows, :] = new.astype(jnp.bfloat16)

        def store(rows, value):
            send[rows, :] = value

        send_field(True, merge_refs, height, source, store)

    return call(
        body,
        [jax.ShapeDtypeStruct((height, width), t) for t in (jnp.float32, jnp.bfloat16)],
        [pltpu.VMEM((height, width), jnp.bfloat16)] * 2,
        state, mine, got, *payloads, *q, *spikes, *merge,
        flops=4 * product_flops(height, width),
    )


def later_tip(position, span, mine, got, mats, q):
    height, width = mine.shape
    n = len(q)

    def body(*refs):
        mine_ref, got_ref = refs[:2]
        mat_refs, q_refs = refs[2 : 2 + n], refs[2 + n : 2 + 2 * n]
        out, source = refs[2 + 2 * n :]
        place = position()

        def store(rows, value):
            out[rows, :] = value

        @pl.when(jnp.logical_or(place == span - 1, place == span))
        def _():
            merge_tip(place == span - 1, q_refs, parts_of(mat_refs), height, mine_ref, got_ref, source, store)

    (tip,) = call(
        body,
        [jax.ShapeDtypeStruct((height, width), jnp.bfloat16)],
        [pltpu.VMEM((height, width), jnp.bfloat16)],
        mine, got, *mats, *q,
        flops=2 * product_flops(height, width),
    )
    return tip


def pick(use_new, new, old):
    def body(new_ref, old_ref, out):
        @pl.when(use_new())
        def _():
            out[...] = new_ref[...]

        @pl.when(jnp.logical_not(use_new()))
        def _():
            out[...] = old_ref[...]

    (out,) = call(body, [jax.ShapeDtypeStruct(old.shape, old.dtype)], [], new, old)
    return out


def tip_update(use_new, state, new_tip, tip, spikes, level, merge=()):
    height, width = state.shape
    n = len(spikes)
    kinds = (jnp.float32, jnp.bfloat16) if merge else (jnp.float32,)

    def body(*refs):
        state_ref, new_ref, tip_ref = refs[:3]
        spike_refs, merge_refs = refs[3 : 3 + n], refs[3 + n : 3 + n + len(merge)]
        outs, source = refs[3 + n + len(merge) : -1], refs[-1]

        @pl.when(use_new())
        def _():
            source[...] = new_ref[...]

        @pl.when(jnp.logical_not(use_new()))
        def _():
            source[...] = tip_ref[...]

        starts = row_starts(height, n, 1)
        for rows, value in each_product(at_level(spike_refs, level), starts, source[...]):
            outs[0][rows, :] = state_ref[rows, :] - value
        if not merge:
            return
        source[...] = outs[0][...].astype(jnp.bfloat16)

        def store(rows, value):
            outs[1][rows, :] = value

        send_field(True, merge_refs, height, source, store)

    return call(
        body,
        [jax.ShapeDtypeStruct((height, width), t) for t in kinds],
        [pltpu.VMEM((height, width), jnp.bfloat16)],
        state, new_tip, tip, *spikes, *merge,
        flops=product_flops(height, width),
    )


def last_update(use_new, done, state, new_tip, tip, spikes, level):
    height, width = state.shape
    n, k = len(spikes), len(done)
    own = width // 2
    before = sum(d.shape[1] // 2 for d in done)
    columns = before + own
    split = before - before % 128

    def body(*refs):
        done_refs = refs[:k]
        state_ref, new_ref, tip_ref = refs[k : k + 3]
        spike_refs = refs[k + 3 : k + 3 + n]
        out, source, whole, sems = refs[k + 3 + n :]

        first = 0
        for d in done_refs:
            w = d.shape[1] // 2
            whole[0, :, pl.ds(first, w)] = d[:, :w]
            whole[1, :, pl.ds(first, w)] = d[:, w:]
            first += w
        copies = []
        if split:
            window = pl.ds(0, split)
            copies.append(pltpu.make_async_copy(whole.at[:, :, window], out.at[:, :, window], sems.at[0]))
            copies[0].start()

        @pl.when(use_new())
        def _():
            source[...] = new_ref[...]

        @pl.when(jnp.logical_not(use_new()))
        def _():
            source[...] = tip_ref[...]

        starts = row_starts(height, n, 1)
        for rows, value in each_product(at_level(spike_refs, level), starts, source[...]):
            new = state_ref[rows, :] - value
            whole[0, rows, pl.ds(before, own)] = new[:, :own]
            whole[1, rows, pl.ds(before, own)] = new[:, own:]
        window = pl.ds(split, columns - split)
        copies.append(pltpu.make_async_copy(whole.at[:, :, window], out.at[:, :, window], sems.at[1]))
        copies[-1].start()
        for copy in copies:
            copy.wait()

    return pl.pallas_call(
        body,
        out_shape=jax.ShapeDtypeStruct((2, height, columns), jnp.float32),
        in_specs=[VMEM] * (k + 3 + n),
        out_specs=pl.BlockSpec(memory_space=pl.ANY),
        scratch_shapes=[
            pltpu.VMEM((height, width), jnp.bfloat16),
            pltpu.VMEM((2, height, columns), jnp.float32),
            pltpu.SemaphoreType.DMA((2,)),
        ],
        compiler_params=pltpu.CompilerParams(vmem_limit_bytes=24 * 2**20),
        cost_estimate=pl.CostEstimate(
            flops=product_flops(height, width), bytes_accessed=12 * height * columns, transcendentals=0
        ),
    )(*done, state, new_tip, tip, *spikes)


def swap(block, pairs):
    return lax.ppermute(block, "slab", pairs + [(b, a) for a, b in pairs])


def per_device(widths, rhs, dinv, spikes, merge_inv):
    slabs = lax.axis_size("slab")
    levels = spikes.shape[2]
    chunks = range(len(widths))

    inverse = ring_gather(dinv[:, 0], "orb")
    spike_all = ring_gather(spikes[:, 0], "orb")
    merge = ring_gather(merge_inv[:, 0], "orb")
    states, hbs = [], []
    for c in chunks:
        state, hb = start_state(inverse, rhs[:, 0], sum(widths[:c]), widths[c])
        states.append(state)
        hbs.append(hb)

    q_own, pay, later = first_sends(spike_all, merge, hbs[0], levels)
    pairs = [(i, i + 1) for i in range(0, slabs, 2)]
    pay_got = swap(pay, pairs)
    mats = ring_gather(swap(later, [(i, i + 1) for i in range(1, slabs - 1, 2)]), "orb")
    q = ring_gather(q_own, "orb")
    sends = [pay] + [next_sends(merge, hbs[c]) for c in chunks[1:]]
    gots = [pay_got] + [swap(sends[c], pairs) for c in chunks[1:]]
    payloads = ring_gather(pay_got, "orb")
    for c in chunks:
        states[c], sends[c] = first_level(states[c], sends[c], gots[c], payloads, q, spike_all, merge)

    for level in range(1, levels):
        span = 1 << level
        heads = range(0, slabs, 2 * span)

        def position(span=span):
            return lax.rem(lax.axis_index("slab"), 2 * span)

        gots = [swap(sends[c], [(g + span - 1, g + span) for g in heads]) for c in chunks]
        tips = [later_tip(position, span, sends[c], gots[c], mats, q) for c in chunks]
        reach = 1
        while reach < span:
            route = []
            for g in heads:
                for j in range(reach):
                    if j + reach < span:
                        route.append((g + span + j, g + span + j + reach))
                        route.append((g + span - 1 - j, g + span - 1 - j - reach))
            moved = [lax.ppermute(tips[c], "slab", route) for c in chunks]

            def is_new(span=span, position=position, reach=reach):
                far = jnp.where(position() >= span, position() - span, span - 1 - position())
                return jnp.logical_and(far >= reach, far < 2 * reach)

            if 2 * reach < span:
                tips = [pick(is_new, moved[c], tips[c]) for c in chunks]
            reach *= 2
        if level < levels - 1:
            for c in chunks:
                states[c], sends[c] = tip_update(is_new, states[c], moved[c], tips[c], spike_all, level, merge)
            continue
        for c in chunks[:-1]:
            (states[c],) = tip_update(is_new, states[c], moved[c], tips[c], spike_all, level)
        c = chunks[-1]
        whole = last_update(is_new, states[:c], states[c], moved[c], tips[c], spike_all, level)
    return whole[:, None]


def chunk_widths(columns):
    total = sum(SHARES)
    if columns * min(SHARES) // total < 64:
        return [columns]
    return [columns * s // total for s in SHARES]


def solution(mesh):
    placed = (
        P(None, ("energy", "slab"), None, ("col", "orb")),
        P(None, ("energy", "slab"), "orb", None),
        P(None, ("energy", "slab"), None, "orb", None),
        P(None, ("energy", "slab"), "orb", None),
    )

    def body(rhs, dinv, spikes, merge_inv):
        return per_device(chunk_widths(rhs.shape[3]), rhs, dinv, spikes, merge_inv)

    return jax.shard_map(
        body,
        mesh=mesh,
        in_specs=placed,
        out_specs=P(None, ("energy", "slab"), None, ("col", "orb")),
        check_vma=False,
    )
```

time: 60.7 us -> 74.9 us (1.23)
  waiting for transfers between devices: 34.1 us -> 50.9 us
  starting transfers between devices: 15.6 us -> 13.1 us
  other arithmetic: 1.11 us -> 0 us
    ppermute x11 -> x7, waiting for transfers between devices: 30.3 us -> 48.2 us  [the longest x2 25.7 us: per_device(): moved = [lax.ppermute(tips[c], 'slab', route) for c in chunks]]
    unnamed x6 -> x10, local copies, waits for them, and re-layouts: 0.02 us -> 2.66 us
    ppermute x7 -> x6, starting transfers between devices: 3.32 us -> 1.54 us  [ring_gather(): lax.ppermute(block, axis, [((i + step) % count, i) for i in range(count)])]
    pallas_call x0 -> x1, Pallas kernels: none -> 1.3 us  [last_update(): pl.pallas_call(body, out_shape=jax.ShapeDtypeStruct((2, height, columns),...]
    squeeze x1 -> x0, local copies, waits for them, and re-layouts: 1.27 us -> none  [per_device(): spikes[:, 0, level]]
    broadcast_in_dim x1 -> x0, other arithmetic: 1.04 us -> none  [per_device(): return jnp.stack([real, imag])[:, None]]
    reshape x1 -> x0, local copies, waits for them, and re-layouts: 1.03 us -> none  [per_device(): mine = lax.dynamic_slice(spikes, (0, 0, level_of, lax.axis_index('col') *...]
    ppermute x7 -> x6, waiting for transfers between devices: 3.76 us -> 2.75 us  [ring_gather(): lax.ppermute(block, axis, [((i + step) % count, i) for i in range(count)])]
  transfers between devices with their start and end apart: 18 -> 13, of which waited for: 7 -> 5; matrix products, arithmetic and copies ran while one was open for 2% -> 0% of each run, Pallas kernels for 10% -> 6%
where the time goes in v2:
time: 74.9 us; the launch traced here: 74.5 us
  waiting for transfers between devices  50.9 us (68%)
  starting transfers between devices  13.1 us (17%)
  Pallas kernels  7.68 us (10%)
  local copies, waits for them, and re-layouts  2.66 us (4%)
    ppermute x2, waiting for transfers between devices, per_device(): moved = [lax.ppermute(tips[c], 'slab', route) for c in chunks]  25.7 us
    ppermute x5, waiting for transfers between devices, swap(): return lax.ppermute(block, 'slab', pairs + [(b, a) for a, b in pairs])  22.5 us
    ppermute x5, starting transfers between devices, swap(): return lax.ppermute(block, 'slab', pairs + [(b, a) for a, b in pairs])  8.95 us
    pallas_call x9, Pallas kernels, call(): pl.pallas_call(body, out_shape=outs, in_specs=[VMEM] * len(args), out_spe...  6.38 us
    ppermute x6, waiting for transfers between devices, ring_gather(): lax.ppermute(block, axis, [((i + step) % count, i) for i in range(count)])  2.75 us
    unnamed x10, local copies, waits for them, and re-layouts  2.66 us
    ppermute x2, starting transfers between devices, per_device(): moved = [lax.ppermute(tips[c], 'slab', route) for c in chunks]  2.58 us
    ppermute x6, starting transfers between devices, ring_gather(): lax.ppermute(block, axis, [((i + step) % count, i) for i in range(count)])  1.54 us
  transfers between devices with their start and end apart: 13, of which 5 were waited for; matrix products, arithmetic and copies ran while one was open for 0% of the time, Pallas kernels for 6%

profile of v2, /device:TPU:0, one launch (start us, length us, event | category | flops | bytes accessed | tf_op | source)
XLA Modules:
  0.0 74.5 jit_solution(13896699763706077334)
XLA Ops:
  0.0 0.5 collective-permute-start.1
  0.5 0.1 collective-permute-start
  0.5 0.4 collective-permute-start.2
  1.0 2.7 %collective-permute-done.refs_1_ = bf16[2,256,512]{2,1,0:T(8,128)(2,1)S(1)} collective-permute-done((bf16[2,256,512]{2,1,0:T(8,128)(2,1)}, bf16[2,256,512]{2,1,0:T(8,128)(2,1)S(1)}, u32[]{:S(2)}, u32[]{:S(2)}) %collective-permute-start) | collective-permute-done | bytes 524320 | tf_op jit(solution)/shard_map/ppermute | solution.py:16
  3.7 1.0 %copy-done.2 = bf16[2,1,256,512]{3,2,1,0:T(8,128)(2,1)S(1)} copy-done((bf16[2,1,256,512]{3,2,1,0:T(8,128)(2,1)S(1)}, bf16[2,1,256,512]{3,2,1,0:T(8,128)(2,1)}, u32[]{:S(2)}) %copy-start.2) | copy-done | bytes 524312
  4.7 1.0 %copy-done.4 = bf16[2,1,512,256]{3,2,1,0:T(8,128)(2,1)S(1)} copy-done((bf16[2,1,512,256]{3,2,1,0:T(8,128)(2,1)S(1)}, bf16[2,1,512,256]{3,2,1,0:T(8,128)(2,1)}, u32[]{:S(2)}) %copy-start.4) | copy-done | bytes 524312
  5.8 0.4 shard_map.46
  6.2 0.0 collective-permute-done.2.refs_3_.refs_10_.refs_1_
  6.3 0.6 copy-done.1
  6.8 1.8 %shard_map.47 = (bf16[2,256,512]{2,1,0:T(8,128)(2,1)S(1)}, bf16[1536,256]{1,0:T(8,128)(2,1)S(1)}, bf16[2,256,512]{2,1,0:T(8,128)(2,1)S(1)}) custom-call(bf16[2,2,256,512]{3,2,1,0:T(8,128)(2,1)S(1)} %bitcast.8, bf16[2,2,256,512]{3,2,1,0:T(8,128)(2,1)S(1)} %collective-permute-done.1.refs_1_.refs_8_.refs_4_.refs_5_, bf16[2,256,512]{2,1,0:T(8,128)(2,1)S(1)} %bitcast.14, ...), custom_call_target="tpu_custom_call" | custom-call | flops 536870912 | bytes 5242880 | tf_op jit(solution)/shard_map/pallas_call | solution.py:73
  8.6 2.6 %collective-permute-start.3 = (bf16[1536,256]{1,0:T(8,128)(2,1)S(1)}, bf16[1536,256]{1,0:T(8,128)(2,1)S(1)}, u32[]{:S(2)}, u32[]{:S(2)}) collective-permute-start(bf16[1536,256]{1,0:T(8,128)(2,1)S(1)} %get-tuple-element.18.refs_1_), channel_id=1, source_target_pairs={{0,4},{8,12},{4,0},{12,8},{1,5},{9,13},{5,1},{13,9},{2,6},{10,14},... | collective-permute-start | bytes 2359304 | tf_op jit(solution)/shard_map/ppermute | solution.py:411
  11.2 17.8 %collective-permute-done.3.refs_2_.refs_3_ = bf16[1536,256]{1,0:T(8,128)(2,1)S(1)} collective-permute-done((bf16[1536,256]{1,0:T(8,128)(2,1)S(1)}, bf16[1536,256]{1,0:T(8,128)(2,1)S(1)}, u32[]{:S(2)}, u32[]{:S(2)}) %collective-permute-start.3) | collective-permute-done | bytes 786464 | tf_op jit(solution)/shard_map/ppermute | solution.py:411
  29.0 0.7 collective-permute-start.7
  29.7 0.6 collective-permute-start.5
  30.3 0.4 shard_map.51
  30.7 0.5 shard_map.52.refs_1_
  31.2 4.3 %collective-permute-start.10 = (bf16[512,256]{1,0:T(8,128)(2,1)S(1)}, bf16[512,256]{1,0:T(8,128)(2,1)S(1)}, u32[]{:S(2)}, u32[]{:S(2)}) collective-permute-start(bf16[512,256]{1,0:T(8,128)(2,1)S(1)} %shard_map.52.refs_1_), channel_id=1, source_target_pairs={{0,4},{8,12},{4,0},{12,8},{1,5},{9,13},{5,1},{13,9},{2,6},{10,14},... | collective-permute-start | bytes 786440 | tf_op jit(solution)/shard_map/ppermute | solution.py:411
  35.5 0.0 collective-permute-done.7.refs_2_
  35.5 0.0 collective-permute-start.8
  35.5 0.0 collective-permute-done.5.refs_6_.refs_5_
  35.5 1.4 %shard_map.48 = (f32[512,256]{1,0:T(8,128)S(1)}, bf16[512,256]{1,0:T(8,128)(2,1)S(1)}) custom-call(f32[512,256]{1,0:T(8,128)S(1)} %get-tuple-element.16.refs_0_, bf16[1536,256]{1,0:T(8,128)(2,1)S(1)} %get-tuple-element.18.refs_1_, bf16[1536,256]{1,0:T(8,128)(2,1)S(1)} %collective-permute-done.3.refs_2_.refs_3_, ...), custom_call_target="tpu_custom_call" | custom-call | flops 1073741824 | bytes 8650752 | tf_op jit(solution)/shard_map/pallas_call | solution.py:73
  37.0 0.7 collective-permute-start.6
  37.6 4.6 %collective-permute-done.10.refs_2_ = bf16[512,256]{1,0:T(8,128)(2,1)S(1)} collective-permute-done((bf16[512,256]{1,0:T(8,128)(2,1)S(1)}, bf16[512,256]{1,0:T(8,128)(2,1)S(1)}, u32[]{:S(2)}, u32[]{:S(2)}) %collective-permute-start.10) | collective-permute-done | bytes 262176 | tf_op jit(solution)/shard_map/ppermute | solution.py:411
  42.3 1.4 %shard_map.53 = (f32[512,256]{1,0:T(8,128)S(1)}, bf16[512,256]{1,0:T(8,128)(2,1)S(1)}) custom-call(f32[512,256]{1,0:T(8,128)S(1)} %get-tuple-element.23.refs_0_, bf16[512,256]{1,0:T(8,128)(2,1)S(1)} %shard_map.52.refs_1_, bf16[512,256]{1,0:T(8,128)(2,1)S(1)} %collective-permute-done.10.refs_2_, bf16[1536,256]{1,0:T(8,128)(2,1)S(1)} %collective-permute-done.3.refs_2_.refs_3_, ...), custom_call_target="tpu_custom_call" | custom-call | flops 1073741824 | bytes 7602176 | tf_op jit(solution)/shard_map/pallas_call | solution.py:73
  43.7 0.7 collective-permute-start.11
  44.4 0.0 collective-permute-done.6.refs_1_
  44.4 1.3 %collective-permute-start.9 = (bf16[512,256]{1,0:T(8,128)(2,1)S(1)}, bf16[512,256]{1,0:T(8,128)(2,1)S(1)}, u32[]{:S(2)}, u32[]{:S(2)}) collective-permute-start(bf16[512,256]{1,0:T(8,128)(2,1)S(1)} %shard_map.49.refs_2_), channel_id=1, source_target_pairs={{8,12},{4,0},{9,13},{5,1},{10,14},{6,2},{11,15},{7,3},{24,28},{20,... | collective-permute-start | bytes 786440 | tf_op jit(solution)/shard_map/ppermute | solution.py:456
  45.7 1.3 %collective-permute-start.12 = (bf16[512,256]{1,0:T(8,128)(2,1)S(1)}, bf16[512,256]{1,0:T(8,128)(2,1)S(1)}, u32[]{:S(2)}, u32[]{:S(2)}) collective-permute-start(bf16[512,256]{1,0:T(8,128)(2,1)S(1)} %shard_map.54.refs_3_), channel_id=1, source_target_pairs={{8,12},{4,0},{9,13},{5,1},{10,14},{6,2},{11,15},{7,3},{24,28},{20,... | collective-permute-start | bytes 786440 | tf_op jit(solution)/shard_map/ppermute | solution.py:456
  47.0 20.6 %collective-permute-done.9.refs_1_ = bf16[512,256]{1,0:T(8,128)(2,1)S(1)} collective-permute-done((bf16[512,256]{1,0:T(8,128)(2,1)S(1)}, bf16[512,256]{1,0:T(8,128)(2,1)S(1)}, u32[]{:S(2)}, u32[]{:S(2)}) %collective-permute-start.9) | collective-permute-done | bytes 262176 | tf_op jit(solution)/shard_map/ppermute | solution.py:456
  67.6 0.5 shard_map.50.refs_0_
  68.1 5.2 %collective-permute-done.12.refs_2_ = bf16[512,256]{1,0:T(8,128)(2,1)S(1)} collective-permute-done((bf16[512,256]{1,0:T(8,128)(2,1)S(1)}, bf16[512,256]{1,0:T(8,128)(2,1)S(1)}, u32[]{:S(2)}, u32[]{:S(2)}) %collective-permute-start.12) | collective-permute-done | bytes 262176 | tf_op jit(solution)/shard_map/ppermute | solution.py:456
  73.2 1.3 %shard_map.55 = f32[2,512,256]{2,1,0:T(8,128)} custom-call(f32[512,256]{1,0:T(8,128)S(1)} %shard_map.50.refs_0_, f32[512,256]{1,0:T(8,128)S(1)} %get-tuple-element.25.refs_1_, bf16[512,256]{1,0:T(8,128)(2,1)S(1)} %collective-permute-done.12.refs_2_, bf16[512,256]{1,0:T(8,128)(2,1)S(1)} %shard_map.54.refs_3_, bf16[2,2,256,512]{3,2,1,0:T(8,128)(2,1)S(1)} %bitcast.12, ...), custom_call_target="tpu_custom_call" | custom-call | flops 268435456 | bytes 1572864 | tf_op jit(solution)/shard_map/pallas_call | solution.py:393
  (14 shorter events, 0.1 us)
Async XLA Ops:
  0.0 6.3 %copy-start = (bf16[2,1,2,256,512]{4,3,2,1,0:T(8,128)(2,1)S(1)}, bf16[2,1,2,256,512]{4,3,2,1,0:T(8,128)(2,1)}, u32[]{:S(2)}) copy-start(bf16[2,1,2,256,512]{4,3,2,1,0:T(8,128)(2,1)} %param.6) | copy-start | bytes 3145732
  0.0 6.2 %collective-permute-start.1 = (bf16[2,2,256,512]{3,2,1,0:T(8,128)(2,1)}, bf16[2,2,256,512]{3,2,1,0:T(8,128)(2,1)S(1)}, u32[]{:S(2)}, u32[]{:S(2)}) collective-permute-start(bf16[2,2,256,512]{3,2,1,0:T(8,128)(2,1)} %bitcast.7), channel_id=1, source_target_pairs={{1,0},{0,1},{3,2},{2,3},{5,4},{4,5},{7,6},{6,7},{9,8},{8,9},{11,10... | collective-permute-start | bytes 3145736 | tf_op jit(solution)/shard_map/ppermute | solution.py:16
  0.5 3.2 %collective-permute-start = (bf16[2,256,512]{2,1,0:T(8,128)(2,1)}, bf16[2,256,512]{2,1,0:T(8,128)(2,1)S(1)}, u32[]{:S(2)}, u32[]{:S(2)}) collective-permute-start(bf16[2,256,512]{2,1,0:T(8,128)(2,1)} %bitcast.18), channel_id=1, source_target_pairs={{1,0},{0,1},{3,2},{2,3},{5,4},{4,5},{7,6},{6,7},{9,8},{8,9},{11,10... | collective-permute-start | bytes 1572872 | tf_op jit(solution)/shard_map/ppermute | solution.py:16
  0.5 5.7 %collective-permute-start.2 = (bf16[2,256,512]{2,1,0:T(8,128)(2,1)}, bf16[2,256,512]{2,1,0:T(8,128)(2,1)S(1)}, u32[]{:S(2)}, u32[]{:S(2)}) collective-permute-start(bf16[2,256,512]{2,1,0:T(8,128)(2,1)} %bitcast.13), channel_id=1, source_target_pairs={{1,0},{0,1},{3,2},{2,3},{5,4},{4,5},{7,6},{6,7},{9,8},{8,9},{11,10... | collective-permute-start | bytes 1572872 | tf_op jit(solution)/shard_map/ppermute | solution.py:16
  3.7 1.0 %copy-start.2 = (bf16[2,1,256,512]{3,2,1,0:T(8,128)(2,1)S(1)}, bf16[2,1,256,512]{3,2,1,0:T(8,128)(2,1)}, u32[]{:S(2)}) copy-start(bf16[2,1,256,512]{3,2,1,0:T(8,128)(2,1)} %param.5) | copy-start | bytes 1572868
  4.7 1.0 %copy-start.4 = (bf16[2,1,512,256]{3,2,1,0:T(8,128)(2,1)S(1)}, bf16[2,1,512,256]{3,2,1,0:T(8,128)(2,1)}, u32[]{:S(2)}) copy-start(bf16[2,1,512,256]{3,2,1,0:T(8,128)(2,1)} %param.4) | copy-start | bytes 1572868
  5.8 1.0 %copy-start.1 = (bf16[2,1,256,512]{3,2,1,0:T(8,128)(2,1)S(1)}, bf16[2,1,256,512]{3,2,1,0:T(8,128)(2,1)}, u32[]{:S(2)}) copy-start(bf16[2,1,256,512]{3,2,1,0:T(8,128)(2,1)} %param.7) | copy-start | bytes 1572868
  6.8 23.5 %copy-start.3 = (bf16[2,1,256,512]{3,2,1,0:T(8,128)(2,1)S(1)}, bf16[2,1,256,512]{3,2,1,0:T(8,128)(2,1)}, u32[]{:S(2)}) copy-start(bf16[2,1,256,512]{3,2,1,0:T(8,128)(2,1)} %param.5) | copy-start | bytes 1572868
  8.6 20.4 %collective-permute-start.3 = (bf16[1536,256]{1,0:T(8,128)(2,1)S(1)}, bf16[1536,256]{1,0:T(8,128)(2,1)S(1)}, u32[]{:S(2)}, u32[]{:S(2)}) collective-permute-start(bf16[1536,256]{1,0:T(8,128)(2,1)S(1)} %get-tuple-element.18.refs_1_), channel_id=1, source_target_pairs={{0,4},{8,12},{4,0},{12,8},{1,5},{9,13},{5,1},{13,9},{2,6},{10,14},... | collective-permute-start | bytes 2359304 | tf_op jit(solution)/shard_map/ppermute | solution.py:411
  29.0 6.5 %collective-permute-start.4 = (bf16[1536,256]{1,0:T(8,128)(2,1)S(1)}, bf16[1536,256]{1,0:T(8,128)(2,1)S(1)}, u32[]{:S(2)}, u32[]{:S(2)}) collective-permute-start(bf16[1536,256]{1,0:T(8,128)(2,1)S(1)} %collective-permute-done.3.refs_2_.refs_3_), channel_id=1, source_target_pairs={{1,0},{0,1},{3,2},{2,3},{5,4},{4,5},{7,6},{6,7},{9,8},{8,9},{11,10... | collective-permute-start | bytes 2359304 | tf_op jit(solution)/shard_map/ppermute | solution.py:16
  29.0 6.5 %collective-permute-start.7 = (bf16[2,256,512]{2,1,0:T(8,128)(2,1)S(1)}, bf16[2,256,512]{2,1,0:T(8,128)(2,1)S(1)}, u32[]{:S(2)}, u32[]{:S(2)}) collective-permute-start(bf16[2,256,512]{2,1,0:T(8,128)(2,1)S(1)} %get-tuple-element.22), channel_id=1, source_target_pairs={{4,8},{8,4},{5,9},{9,5},{6,10},{10,6},{7,11},{11,7},{20,24},{24,20... | collective-permute-start | bytes 1572872 | tf_op jit(solution)/shard_map/ppermute | solution.py:411
  29.7 5.8 %collective-permute-start.5 = (bf16[2,256,512]{2,1,0:T(8,128)(2,1)S(1)}, bf16[2,256,512]{2,1,0:T(8,128)(2,1)S(1)}, u32[]{:S(2)}, u32[]{:S(2)}) collective-permute-start(bf16[2,256,512]{2,1,0:T(8,128)(2,1)S(1)} %get-tuple-element.19.refs_5_.refs_4_), channel_id=1, source_target_pairs={{1,0},{0,1},{3,2},{2,3},{5,4},{4,5},{7,6},{6,7},{9,8},{8,9},{11,10... | collective-permute-start | bytes 1572872 | tf_op jit(solution)/shard_map/ppermute | solution.py:16
  31.2 11.1 %collective-permute-start.10 = (bf16[512,256]{1,0:T(8,128)(2,1)S(1)}, bf16[512,256]{1,0:T(8,128)(2,1)S(1)}, u32[]{:S(2)}, u32[]{:S(2)}) collective-permute-start(bf16[512,256]{1,0:T(8,128)(2,1)S(1)} %shard_map.52.refs_1_), channel_id=1, source_target_pairs={{0,4},{8,12},{4,0},{12,8},{1,5},{9,13},{5,1},{13,9},{2,6},{10,14},... | collective-permute-start | bytes 786440 | tf_op jit(solution)/shard_map/ppermute | solution.py:411
  35.5 8.8 %collective-permute-start.8 = (bf16[2,256,512]{2,1,0:T(8,128)(2,1)S(1)}, bf16[2,256,512]{2,1,0:T(8,128)(2,1)S(1)}, u32[]{:S(2)}, u32[]{:S(2)}) collective-permute-start(bf16[2,256,512]{2,1,0:T(8,128)(2,1)S(1)} %collective-permute-done.7.refs_2_), channel_id=1, source_target_pairs={{1,0},{0,1},{3,2},{2,3},{5,4},{4,5},{7,6},{6,7},{9,8},{8,9},{11,10... | collective-permute-start | bytes 1572872 | tf_op jit(solution)/shard_map/ppermute | solution.py:16
  37.0 7.4 %collective-permute-start.6 = (bf16[512,256]{1,0:T(8,128)(2,1)S(1)}, bf16[512,256]{1,0:T(8,128)(2,1)S(1)}, u32[]{:S(2)}, u32[]{:S(2)}) collective-permute-start(bf16[512,256]{1,0:T(8,128)(2,1)S(1)} %get-tuple-element.21.refs_0_), channel_id=1, source_target_pairs={{4,8},{8,4},{5,9},{9,5},{6,10},{10,6},{7,11},{11,7},{20,24},{24,20... | collective-permute-start | bytes 786440 | tf_op jit(solution)/shard_map/ppermute | solution.py:411
  43.7 2.0 %collective-permute-start.11 = (bf16[512,256]{1,0:T(8,128)(2,1)S(1)}, bf16[512,256]{1,0:T(8,128)(2,1)S(1)}, u32[]{:S(2)}, u32[]{:S(2)}) collective-permute-start(bf16[512,256]{1,0:T(8,128)(2,1)S(1)} %get-tuple-element.26.refs_0_), channel_id=1, source_target_pairs={{4,8},{8,4},{5,9},{9,5},{6,10},{10,6},{7,11},{11,7},{20,24},{24,20... | collective-permute-start | bytes 786440 | tf_op jit(solution)/shard_map/ppermute | solution.py:411
  44.4 23.2 %collective-permute-start.9 = (bf16[512,256]{1,0:T(8,128)(2,1)S(1)}, bf16[512,256]{1,0:T(8,128)(2,1)S(1)}, u32[]{:S(2)}, u32[]{:S(2)}) collective-permute-start(bf16[512,256]{1,0:T(8,128)(2,1)S(1)} %shard_map.49.refs_2_), channel_id=1, source_target_pairs={{8,12},{4,0},{9,13},{5,1},{10,14},{6,2},{11,15},{7,3},{24,28},{20,... | collective-permute-start | bytes 786440 | tf_op jit(solution)/shard_map/ppermute | solution.py:456
  45.7 27.5 %collective-permute-start.12 = (bf16[512,256]{1,0:T(8,128)(2,1)S(1)}, bf16[512,256]{1,0:T(8,128)(2,1)S(1)}, u32[]{:S(2)}, u32[]{:S(2)}) collective-permute-start(bf16[512,256]{1,0:T(8,128)(2,1)S(1)} %shard_map.54.refs_3_), channel_id=1, source_target_pairs={{8,12},{4,0},{9,13},{5,1},{10,14},{6,2},{11,15},{7,3},{24,28},{20,... | collective-permute-start | bytes 786440 | tf_op jit(solution)/shard_map/ppermute | solution.py:456

commit v3 on v2

--- a/solution.py
+++ b/solution.py
@@ -49,17 +49,6 @@
     return [tuple(lambda m=m, p=p: m[p] for p in range(2)) for m in pieces]
 
 
-def packed(refs, height, width):
-    blocks = height // width
-    size = (refs[0].shape[0] - height) // (2 * blocks)
-
-    def load(ref, part):
-        first = height + part * blocks * size
-        return jnp.concatenate([ref[pl.ds(first + k * size, size), :] for k in range(blocks)], axis=1)
-
-    return [tuple(lambda r=r, p=p: load(r, p) for p in range(2)) for r in refs]
-
-
 def each_product(pieces, starts, field):
     field_i = turned(field)
     for (real, imag), start in zip(pieces, starts):
@@ -96,6 +85,28 @@
     return found
 
 
+def fetch(*arrays):
+    n = len(arrays)
+
+    def body(*refs):
+        sems = refs[-1]
+        copies = [pltpu.make_async_copy(refs[k], refs[n + k], sems.at[k]) for k in range(n)]
+        for copy in copies:
+            copy.start()
+        for copy in copies:
+            copy.wait()
+
+    return pl.pallas_call(
+        body,
+        out_shape=[jax.ShapeDtypeStruct(a.shape, a.dtype) for a in arrays],
+        in_specs=[pl.BlockSpec(memory_space=pl.ANY)] * n,
+        out_specs=[VMEM] * n,
+        scratch_shapes=[pltpu.SemaphoreType.DMA((n,))],
+        compiler_params=pltpu.CompilerParams(vmem_limit_bytes=48 * 2**20),
+        cost_estimate=pl.CostEstimate(flops=0, bytes_accessed=2 * sum(a.size * 2 for a in arrays), transcendentals=0),
+    )(*arrays)
+
+
 def start_state(pieces, rhs, first, width):
     height = rhs.shape[1]
     n = len(pieces)
@@ -126,79 +137,55 @@
         store(pl.ds(0, height), hb_ref[...])
 
 
-def first_sends(spikes, merge, hb, levels):
-    height, width = hb.shape
+def first_sends(spikes, merge_own, levels, cols):
     n = len(spikes)
-    size = height // n
-    blocks = height // width
-    cut = min(128, width)
-
-    def body(*refs):
-        spike_refs, merge_refs, hb_ref = refs[:n], refs[n : 2 * n], refs[2 * n]
-        q_out, pay, later = refs[2 * n + 1 :]
+    size, height = merge_own.shape[1:]
+    cut = min(128, height)
+
+    def body(*refs):
+        spike_refs, merge_ref = refs[:n], refs[n]
+        q_out, first, later = refs[n + 1 :]
         device = lax.axis_index("slab")
         level_left = lowest_bit(device + 1, levels)
         level_right = lowest_bit(device, levels)
+
         starts = row_starts(height, n, 1)
-
-        def columns(k, carry):
-            window = pl.ds(pl.multiple_of(k * cut, cut), cut)
-            order = [jnp.concatenate([s[p, level_left, :, window] for s in spike_refs], axis=0) for p in range(2)]
-            if n > 1:
-                first = lax.axis_index("orb")
-                order = [in_place(x, first, n) for x in order]
-            field = jnp.concatenate(order, axis=1)
-            for _, value in each_product(parts_of(merge_refs[:1]), starts[:1], field):
-                q_out[0, :, window] = value[:, :cut].astype(jnp.bfloat16)
-                q_out[1, :, window] = value[:, cut:].astype(jnp.bfloat16)
-            return carry
-
-        lax.fori_loop(0, height // cut, columns, 0)
-
-        def pack(source):
-            for p in range(2):
-                for k in range(blocks):
-                    pay[pl.ds(height + (p * blocks + k) * size, size), :] = source(p, pl.ds(k * width, width))
+        for k in range(height // cut):
+            window = pl.ds(k * cut, cut)
+            value = 0.0
+            for spike, start in zip(spike_refs, starts):
+                field = jnp.concatenate([spike[p, level_left, :, window] for p in range(2)], axis=1)
+                piece = tuple(lambda p=p, start=start: merge_ref[p, :, rows_of(start, size)] for p in range(2))
+                for _, part in each_product([piece], [0], field):
+                    value += part
+            q_out[0, :, window] = value[:, :cut].astype(jnp.bfloat16)
+            q_out[1, :, window] = value[:, cut:].astype(jnp.bfloat16)
+
+        share = size // cols
+        rows = rows_of(lax.axis_index("col") * share, share) if cols > 1 else pl.ds(0, size)
 
         @pl.when(is_even())
         def _():
-            pack(lambda p, window: q_out[p, :, window])
+            first[...] = q_out[:, rows, :]
             for p in range(2):
                 later[p] = spike_refs[0][p, level_right]
 
         @pl.when(jnp.logical_not(is_even()))
         def _():
-            pack(lambda p, window: spike_refs[0][p, 0, :, window])
+            for p in range(2):
+                first[p] = spike_refs[0][p, 0, rows, :]
             later[...] = q_out[...]
 
-        def store(rows, value):
-            pay[rows, :] = value
-
-        send_field(False, merge_refs, height, hb_ref, store)
-
     return call(
         body,
-        [
-            jax.ShapeDtypeStruct((2, size, height), jnp.bfloat16),
-            jax.ShapeDtypeStruct((height + 2 * blocks * size, width), jnp.bfloat16),
-            jax.ShapeDtypeStruct((2, size, height), jnp.bfloat16),
-        ],
+        [jax.ShapeDtypeStruct((2, rows, height), jnp.bfloat16) for rows in (size, size // cols, size)],
         [],
-        *spikes, *merge, hb,
-        flops=2 * product_flops(height, width),
-    )
-
-
-def in_place(rows, first, count):
-    size = rows.shape[0] // count
-    out = rows
-    for shift in range(1, count):
-        rolled = jnp.concatenate([rows[rows.shape[0] - shift * size :], rows[: rows.shape[0] - shift * size]], axis=0)
-        out = jnp.where(first == shift, rolled, out)
-    return out
-
-
-def next_sends(merge, hb):
+        *spikes, merge_own,
+        flops=product_flops(height, height),
+    )
+
+
+def first_field(merge, hb):
     height, width = hb.shape
     n = len(merge)
 
@@ -229,23 +216,25 @@
     def _():
         source[...] = mine[pl.ds(0, height), :]
 
+    starts = row_starts(height, n, len(mats) // n)
     for rows, value in each_product(mats, starts, source[...]):
         store(rows, (got[rows, :].astype(jnp.float32) - value).astype(jnp.bfloat16))
 
 
-def first_level(state, mine, got, payloads, q, spikes, merge):
+def first_level(state, mine, got, mats, q, spikes, merge):
     height, width = state.shape
     n = len(q)
 
     def body(*refs):
         state_ref, mine_ref, got_ref = refs[:3]
-        pay_refs, q_refs, spike_refs, merge_refs = (refs[3 + k * n : 3 + (k + 1) * n] for k in range(4))
-        out, send, source, tip = refs[3 + 4 * n :]
+        mat_refs, rest = refs[3 : 3 + len(mats)], refs[3 + len(mats) :]
+        q_refs, spike_refs, merge_refs = (rest[k * n : (k + 1) * n] for k in range(3))
+        out, send, source, tip = rest[3 * n :]
 
         def store_tip(rows, value):
             tip[rows, :] = value
 
-        merge_tip(is_even(), q_refs, packed(pay_refs, height, width), height, mine_ref, got_ref, source, store_tip)
+        merge_tip(is_even(), q_refs, parts_of(mat_refs), height, mine_ref, got_ref, source, store_tip)
         for rows, value in each_product(at_level(spike_refs, 0), row_starts(height, n, 1), tip[...]):
             new = state_ref[rows, :] - value
             out[rows, :] = new
@@ -260,7 +249,7 @@
         body,
         [jax.ShapeDtypeStruct((height, width), t) for t in (jnp.float32, jnp.bfloat16)],
         [pltpu.VMEM((height, width), jnp.bfloat16)] * 2,
-        state, mine, got, *payloads, *q, *spikes, *merge,
+        state, mine, got, *mats, *q, *spikes, *merge,
         flops=4 * product_flops(height, width),
     )
 
@@ -416,25 +405,30 @@
     levels = spikes.shape[2]
     chunks = range(len(widths))
 
+    cols = lax.axis_size("col")
+    spike_all = ring_gather(spikes[:, 0], "orb")
+    spike_own, merge_own = fetch(spikes[:, 0], merge_inv[:, 0])
+    spike_all[0] = spike_own
+    q_own, first, later = first_sends(spike_all, merge_own, levels, cols)
+    pairs = [(i, i + 1) for i in range(0, slabs, 2)]
+    first = swap(first, pairs)
+    later = swap(later, [(i, i + 1) for i in range(1, slabs - 1, 2)])
+    q = ring_gather(q_own, "orb")
+    dinv, merge_inv, _ = lax.optimization_barrier((dinv, merge_inv, q_own))
     inverse = ring_gather(dinv[:, 0], "orb")
-    spike_all = ring_gather(spikes[:, 0], "orb")
-    merge = ring_gather(merge_inv[:, 0], "orb")
-    states, hbs = [], []
+    merge = [merge_own] + ring_gather(merge_inv[:, 0], "orb")[1:]
+    states, sends, gots = [], [], []
     for c in chunks:
         state, hb = start_state(inverse, rhs[:, 0], sum(widths[:c]), widths[c])
         states.append(state)
-        hbs.append(hb)
-
-    q_own, pay, later = first_sends(spike_all, merge, hbs[0], levels)
-    pairs = [(i, i + 1) for i in range(0, slabs, 2)]
-    pay_got = swap(pay, pairs)
-    mats = ring_gather(swap(later, [(i, i + 1) for i in range(1, slabs - 1, 2)]), "orb")
-    q = ring_gather(q_own, "orb")
-    sends = [pay] + [next_sends(merge, hbs[c]) for c in chunks[1:]]
-    gots = [pay_got] + [swap(sends[c], pairs) for c in chunks[1:]]
-    payloads = ring_gather(pay_got, "orb")
+        sends.append(first_field(merge, hb))
+        gots.append(swap(sends[c], pairs))
+    first, _ = lax.optimization_barrier((first, sends[-1]))
+    across = [ring_gather(p, "orb") for p in ring_gather(first, "col")]
+    first = [across[k][j] for j in range(len(q)) for k in range(cols)]
+    later = ring_gather(later, "orb")
     for c in chunks:
-        states[c], sends[c] = first_level(states[c], sends[c], gots[c], payloads, q, spike_all, merge)
+        states[c], sends[c] = first_level(states[c], sends[c], gots[c], first, q, spike_all, merge)
 
     for level in range(1, levels):
         span = 1 << level
@@ -444,7 +438,7 @@
             return lax.rem(lax.axis_index("slab"), 2 * span)
 
         gots = [swap(sends[c], [(g + span - 1, g + span) for g in heads]) for c in chunks]
-        tips = [later_tip(position, span, sends[c], gots[c], mats, q) for c in chunks]
+        tips = [later_tip(position, span, sends[c], gots[c], later, q) for c in chunks]
         reach = 1
         while reach < span:
             route = []

time: 74.9 us -> 52.9 us (0.71)
  waiting for transfers between devices: 50.9 us -> 29.6 us
    ppermute x5 -> x6, waiting for transfers between devices: 22.5 us -> 10.4 us  [swap(): return lax.ppermute(block, 'slab', pairs + [(b, a) for a, b in pairs])]
    ppermute x2, waiting for transfers between devices: 25.7 us -> 15.1 us  [per_device(): moved = [lax.ppermute(tips[c], 'slab', route) for c in chunks]]
    ppermute x6 -> x8, waiting for transfers between devices: 2.75 us -> 4.16 us  [ring_gather(): lax.ppermute(block, axis, [((i + step) % count, i) for i in range(count)])]
    ppermute x5 -> x6, starting transfers between devices: 8.95 us -> 7.63 us  [swap(): return lax.ppermute(block, 'slab', pairs + [(b, a) for a, b in pairs])]
    ppermute x6 -> x8, starting transfers between devices: 1.54 us -> 2.86 us  [ring_gather(): lax.ppermute(block, axis, [((i + step) % count, i) for i in range(count)])]
    pallas_call x9 -> x10, Pallas kernels: 6.38 us -> 5.78 us  [call(): pl.pallas_call(body, out_shape=outs, in_specs=[VMEM] * len(args), out_spe...]
    unnamed x10 -> x8, local copies, waits for them, and re-layouts: 2.66 us -> 2.54 us
  transfers between devices with their start and end apart: 13 -> 16, of which waited for: 5 -> 7; matrix products, arithmetic and copies ran while one was open for 0% -> 0% of each run, Pallas kernels for 6% -> 10%
where the time goes in v3:
time: 52.9 us; the launch traced here: 52.6 us
  waiting for transfers between devices  29.6 us (56%)
  starting transfers between devices  13.1 us (25%)
  Pallas kernels  7.21 us (14%)
  local copies, waits for them, and re-layouts  2.54 us (5%)
    ppermute x2, waiting for transfers between devices, per_device(): moved = [lax.ppermute(tips[c], 'slab', route) for c in chunks]  15.1 us
    ppermute x6, waiting for transfers between devices, swap(): return lax.ppermute(block, 'slab', pairs + [(b, a) for a, b in pairs])  10.4 us
    ppermute x6, starting transfers between devices, swap(): return lax.ppermute(block, 'slab', pairs + [(b, a) for a, b in pairs])  7.63 us
    pallas_call x10, Pallas kernels, call(): pl.pallas_call(body, out_shape=outs, in_specs=[VMEM] * len(args), out_spe...  5.78 us
    ppermute x8, waiting for transfers between devices, ring_gather(): lax.ppermute(block, axis, [((i + step) % count, i) for i in range(count)])  4.16 us
    ppermute x8, starting transfers between devices, ring_gather(): lax.ppermute(block, axis, [((i + step) % count, i) for i in range(count)])  2.86 us
    ppermute x2, starting transfers between devices, per_device(): moved = [lax.ppermute(tips[c], 'slab', route) for c in chunks]  2.58 us
    unnamed x8, local copies, waits for them, and re-layouts  2.54 us
  transfers between devices with their start and end apart: 16, of which 7 were waited for; matrix products, arithmetic and copies ran while one was open for 0% of the time, Pallas kernels for 10%

profile of v3, /device:TPU:0, one launch (start us, length us, event | category | flops | bytes accessed | tf_op | source)
XLA Modules:
  0.0 52.6 jit_solution(14664276484391257735)
XLA Ops:
  0.0 0.5 collective-permute-start
  0.5 1.2 %copy-done.2 = bf16[2,1,2,256,512]{4,3,2,1,0:T(8,128)(2,1)S(1)} copy-done((bf16[2,1,2,256,512]{4,3,2,1,0:T(8,128)(2,1)S(1)}, bf16[2,1,2,256,512]{4,3,2,1,0:T(8,128)(2,1)}, u32[]{:S(2)}) %copy-start.2) | copy-done | bytes 1048600
  1.7 1.0 %copy-done.3 = bf16[2,1,256,512]{3,2,1,0:T(8,128)(2,1)S(1)} copy-done((bf16[2,1,256,512]{3,2,1,0:T(8,128)(2,1)S(1)}, bf16[2,1,256,512]{3,2,1,0:T(8,128)(2,1)}, u32[]{:S(2)}) %copy-start.3) | copy-done | bytes 524312
  2.7 0.1 shard_map.46
  3.0 0.8 %shard_map.47 = (bf16[2,256,512]{2,1,0:T(8,128)(2,1)S(1)}, bf16[2,128,512]{2,1,0:T(8,128)(2,1)S(1)}, bf16[2,256,512]{2,1,0:T(8,128)(2,1)S(1)}) custom-call(bf16[2,2,256,512]{3,2,1,0:T(8,128)(2,1)S(1)} %get-tuple-element.21.refs_0_.refs_9_.refs_3_.refs_4_, bf16[2,2,256,512]{3,2,1,0:T(8,128)(2,1)S(1)} %collective-permute-done.refs_1_.refs_10_.refs_4_.refs_5_, ...), custom_call_target="tpu_custom_call" | custom-call | flops 536870912 | bytes 3932160 | tf_op jit(solution)/shard_map/pallas_call | solution.py:62
  3.7 0.3 copy-done
  4.0 0.4 collective-permute-start.1
  4.4 0.1 collective-permute-start.2
  4.5 2.9 %collective-permute-start.4 = (bf16[2,128,512]{2,1,0:T(8,128)(2,1)S(1)}, bf16[2,128,512]{2,1,0:T(8,128)(2,1)S(1)}, u32[]{:S(2)}, u32[]{:S(2)}) collective-permute-start(bf16[2,128,512]{2,1,0:T(8,128)(2,1)S(1)} %get-tuple-element.28), channel_id=1, source_target_pairs={{0,4},{8,12},{4,0},{12,8},{1,5},{9,13},{5,1},{13,9},{2,6},{10,14},... | collective-permute-start | bytes 786440 | tf_op jit(solution)/shard_map/ppermute | solution.py:400
  7.5 0.7 %collective-permute-start.10 = (bf16[2,256,512]{2,1,0:T(8,128)(2,1)S(1)}, bf16[2,256,512]{2,1,0:T(8,128)(2,1)S(1)}, u32[]{:S(2)}, u32[]{:S(2)}) collective-permute-start(bf16[2,256,512]{2,1,0:T(8,128)(2,1)S(1)} %get-tuple-element.33), channel_id=1, source_target_pairs={{4,8},{8,4},{5,9},{9,5},{6,10},{10,6},{7,11},{11,7},{20,24},{24,20... | collective-permute-start | bytes 1572872 | tf_op jit(solution)/shard_map/ppermute | solution.py:400
  8.2 0.4 shard_map.50
  8.6 0.5 shard_map.51.refs_1_
  9.1 5.0 %collective-permute-done.4.refs_3_ = bf16[2,128,512]{2,1,0:T(8,128)(2,1)S(1)} collective-permute-done((bf16[2,128,512]{2,1,0:T(8,128)(2,1)S(1)}, bf16[2,128,512]{2,1,0:T(8,128)(2,1)S(1)}, u32[]{:S(2)}, u32[]{:S(2)}) %collective-permute-start.4) | collective-permute-done | bytes 262176 | tf_op jit(solution)/shard_map/ppermute | solution.py:400
  14.1 1.7 %collective-permute-start.5 = (bf16[2,128,512]{2,1,0:T(8,128)(2,1)S(1)}, bf16[2,128,512]{2,1,0:T(8,128)(2,1)S(1)}, u32[]{:S(2)}, u32[]{:S(2)}) collective-permute-start(bf16[2,128,512]{2,1,0:T(8,128)(2,1)S(1)} %collective-permute-done.4.refs_3_), channel_id=1, source_target_pairs={{2,0},{0,2},{3,1},{1,3},{6,4},{4,6},{7,5},{5,7},{10,8},{8,10},{11,... | collective-permute-start | bytes 786440 | tf_op jit(solution)/shard_map/ppermute | solution.py:16
  15.7 0.4 shard_map.48
  16.2 0.5 shard_map.49.refs_1_
  16.6 1.2 %collective-permute-start.3 = (bf16[512,256]{1,0:T(8,128)(2,1)S(1)}, bf16[512,256]{1,0:T(8,128)(2,1)S(1)}, u32[]{:S(2)}, u32[]{:S(2)}) collective-permute-start(bf16[512,256]{1,0:T(8,128)(2,1)S(1)} %shard_map.49.refs_1_), channel_id=1, source_target_pairs={{0,4},{8,12},{4,0},{12,8},{1,5},{9,13},{5,1},{13,9},{2,6},{10,14},... | collective-permute-start | bytes 786440 | tf_op jit(solution)/shard_map/ppermute | solution.py:400
  17.8 4.0 %collective-permute-done.5.refs_4_ = bf16[2,128,512]{2,1,0:T(8,128)(2,1)S(1)} collective-permute-done((bf16[2,128,512]{2,1,0:T(8,128)(2,1)S(1)}, bf16[2,128,512]{2,1,0:T(8,128)(2,1)S(1)}, u32[]{:S(2)}, u32[]{:S(2)}) %collective-permute-start.5) | collective-permute-done | bytes 262176 | tf_op jit(solution)/shard_map/ppermute | solution.py:16
  21.9 1.4 %collective-permute-start.13 = (bf16[512,256]{1,0:T(8,128)(2,1)S(1)}, bf16[512,256]{1,0:T(8,128)(2,1)S(1)}, u32[]{:S(2)}, u32[]{:S(2)}) collective-permute-start(bf16[512,256]{1,0:T(8,128)(2,1)S(1)} %shard_map.51.refs_1_), channel_id=1, source_target_pairs={{0,4},{8,12},{4,0},{12,8},{1,5},{9,13},{5,1},{13,9},{2,6},{10,14},... | collective-permute-start | bytes 786440 | tf_op jit(solution)/shard_map/ppermute | solution.py:400
  23.3 0.2 collective-permute-start.11
  23.6 2.2 %collective-permute-done.3.refs_2_ = bf16[512,256]{1,0:T(8,128)(2,1)S(1)} collective-permute-done((bf16[512,256]{1,0:T(8,128)(2,1)S(1)}, bf16[512,256]{1,0:T(8,128)(2,1)S(1)}, u32[]{:S(2)}, u32[]{:S(2)}) %collective-permute-start.3) | collective-permute-done | bytes 262176 | tf_op jit(solution)/shard_map/ppermute | solution.py:400
  25.8 1.4 %shard_map.52 = (f32[512,256]{1,0:T(8,128)S(1)}, bf16[512,256]{1,0:T(8,128)(2,1)S(1)}) custom-call(f32[512,256]{1,0:T(8,128)S(1)} %get-tuple-element.25.refs_0_, bf16[512,256]{1,0:T(8,128)(2,1)S(1)} %shard_map.49.refs_1_, bf16[512,256]{1,0:T(8,128)(2,1)S(1)} %collective-permute-done.3.refs_2_, bf16[2,128,512]{2,1,0:T(8,128)(2,1)S(1)} %collective-permute-done.4.refs_3_, ...), custom_call_target="tpu_custom_call" | custom-call | flops 1073741824 | bytes 7077888 | tf_op jit(solution)/shard_map/pallas_call | solution.py:62
  27.2 0.7 %collective-permute-start.9 = (bf16[512,256]{1,0:T(8,128)(2,1)S(1)}, bf16[512,256]{1,0:T(8,128)(2,1)S(1)}, u32[]{:S(2)}, u32[]{:S(2)}) collective-permute-start(bf16[512,256]{1,0:T(8,128)(2,1)S(1)} %get-tuple-element.32.refs_0_), channel_id=1, source_target_pairs={{4,8},{8,4},{5,9},{9,5},{6,10},{10,6},{7,11},{11,7},{20,24},{24,20... | collective-permute-start | bytes 786440 | tf_op jit(solution)/shard_map/ppermute | solution.py:400
  27.9 3.2 %collective-permute-done.13.refs_2_ = bf16[512,256]{1,0:T(8,128)(2,1)S(1)} collective-permute-done((bf16[512,256]{1,0:T(8,128)(2,1)S(1)}, bf16[512,256]{1,0:T(8,128)(2,1)S(1)}, u32[]{:S(2)}, u32[]{:S(2)}) %collective-permute-start.13) | collective-permute-done | bytes 262176 | tf_op jit(solution)/shard_map/ppermute | solution.py:400
  31.0 1.4 %shard_map.55 = (f32[512,256]{1,0:T(8,128)S(1)}, bf16[512,256]{1,0:T(8,128)(2,1)S(1)}) custom-call(f32[512,256]{1,0:T(8,128)S(1)} %get-tuple-element.34.refs_0_, bf16[512,256]{1,0:T(8,128)(2,1)S(1)} %shard_map.51.refs_1_, bf16[512,256]{1,0:T(8,128)(2,1)S(1)} %collective-permute-done.13.refs_2_, bf16[2,128,512]{2,1,0:T(8,128)(2,1)S(1)} %collective-permute-done.4.refs_3_, ...), custom_call_target="tpu_custom_call" | custom-call | flops 1073741824 | bytes 7077888 | tf_op jit(solution)/shard_map/pallas_call | solution.py:62
  32.4 0.7 %collective-permute-start.14 = (bf16[512,256]{1,0:T(8,128)(2,1)S(1)}, bf16[512,256]{1,0:T(8,128)(2,1)S(1)}, u32[]{:S(2)}, u32[]{:S(2)}) collective-permute-start(bf16[512,256]{1,0:T(8,128)(2,1)S(1)} %get-tuple-element.36.refs_0_), channel_id=1, source_target_pairs={{4,8},{8,4},{5,9},{9,5},{6,10},{10,6},{7,11},{11,7},{20,24},{24,20... | collective-permute-start | bytes 786440 | tf_op jit(solution)/shard_map/ppermute | solution.py:400
  33.1 1.3 %collective-permute-start.12 = (bf16[512,256]{1,0:T(8,128)(2,1)S(1)}, bf16[512,256]{1,0:T(8,128)(2,1)S(1)}, u32[]{:S(2)}, u32[]{:S(2)}) collective-permute-start(bf16[512,256]{1,0:T(8,128)(2,1)S(1)} %shard_map.53.refs_2_), channel_id=1, source_target_pairs={{8,12},{4,0},{9,13},{5,1},{10,14},{6,2},{11,15},{7,3},{24,28},{20,... | collective-permute-start | bytes 786440 | tf_op jit(solution)/shard_map/ppermute | solution.py:450
  34.5 1.3 %collective-permute-start.15 = (bf16[512,256]{1,0:T(8,128)(2,1)S(1)}, bf16[512,256]{1,0:T(8,128)(2,1)S(1)}, u32[]{:S(2)}, u32[]{:S(2)}) collective-permute-start(bf16[512,256]{1,0:T(8,128)(2,1)S(1)} %shard_map.56.refs_3_), channel_id=1, source_target_pairs={{8,12},{4,0},{9,13},{5,1},{10,14},{6,2},{11,15},{7,3},{24,28},{20,... | collective-permute-start | bytes 786440 | tf_op jit(solution)/shard_map/ppermute | solution.py:450
  35.8 9.8 %collective-permute-done.12.refs_1_ = bf16[512,256]{1,0:T(8,128)(2,1)S(1)} collective-permute-done((bf16[512,256]{1,0:T(8,128)(2,1)S(1)}, bf16[512,256]{1,0:T(8,128)(2,1)S(1)}, u32[]{:S(2)}, u32[]{:S(2)}) %collective-permute-start.12) | collective-permute-done | bytes 262176 | tf_op jit(solution)/shard_map/ppermute | solution.py:450
  45.6 0.5 shard_map.54.refs_0_
  46.0 5.3 %collective-permute-done.15.refs_2_ = bf16[512,256]{1,0:T(8,128)(2,1)S(1)} collective-permute-done((bf16[512,256]{1,0:T(8,128)(2,1)S(1)}, bf16[512,256]{1,0:T(8,128)(2,1)S(1)}, u32[]{:S(2)}, u32[]{:S(2)}) %collective-permute-start.15) | collective-permute-done | bytes 262176 | tf_op jit(solution)/shard_map/ppermute | solution.py:450
  51.3 1.3 %shard_map.57 = f32[2,512,256]{2,1,0:T(8,128)} custom-call(f32[512,256]{1,0:T(8,128)S(1)} %shard_map.54.refs_0_, f32[512,256]{1,0:T(8,128)S(1)} %get-tuple-element.35.refs_1_, bf16[512,256]{1,0:T(8,128)(2,1)S(1)} %collective-permute-done.15.refs_2_, bf16[512,256]{1,0:T(8,128)(2,1)S(1)} %shard_map.56.refs_3_, ...), custom_call_target="tpu_custom_call" | custom-call | flops 268435456 | bytes 1572864 | tf_op jit(solution)/shard_map/pallas_call | solution.py:382
  (20 shorter events, 0.2 us)
Async XLA Ops:
  0.0 3.0 %collective-permute-start = (bf16[2,2,256,512]{3,2,1,0:T(8,128)(2,1)}, bf16[2,2,256,512]{3,2,1,0:T(8,128)(2,1)S(1)}, u32[]{:S(2)}, u32[]{:S(2)}) collective-permute-start(bf16[2,2,256,512]{3,2,1,0:T(8,128)(2,1)} %bitcast.13), channel_id=1, source_target_pairs={{1,0},{0,1},{3,2},{2,3},{5,4},{4,5},{7,6},{6,7},{9,8},{8,9},{11,10... | collective-permute-start | bytes 3145736 | tf_op jit(solution)/shard_map/ppermute | solution.py:16
  0.5 1.2 %copy-start.2 = (bf16[2,1,2,256,512]{4,3,2,1,0:T(8,128)(2,1)S(1)}, bf16[2,1,2,256,512]{4,3,2,1,0:T(8,128)(2,1)}, u32[]{:S(2)}) copy-start(bf16[2,1,2,256,512]{4,3,2,1,0:T(8,128)(2,1)} %param.6) | copy-start | bytes 3145732
  1.7 1.0 %copy-start.3 = (bf16[2,1,256,512]{3,2,1,0:T(8,128)(2,1)S(1)}, bf16[2,1,256,512]{3,2,1,0:T(8,128)(2,1)}, u32[]{:S(2)}) copy-start(bf16[2,1,256,512]{3,2,1,0:T(8,128)(2,1)} %param.7) | copy-start | bytes 1572868
  3.0 1.0 %copy-start = (bf16[2,1,256,512]{3,2,1,0:T(8,128)(2,1)S(1)}, bf16[2,1,256,512]{3,2,1,0:T(8,128)(2,1)}, u32[]{:S(2)}) copy-start(bf16[2,1,256,512]{3,2,1,0:T(8,128)(2,1)} %param.5) | copy-start | bytes 1572868
  3.0 5.2 %copy-start.1 = (bf16[2,1,512,256]{3,2,1,0:T(8,128)(2,1)S(1)}, bf16[2,1,512,256]{3,2,1,0:T(8,128)(2,1)}, u32[]{:S(2)}) copy-start(bf16[2,1,512,256]{3,2,1,0:T(8,128)(2,1)} %param.4) | copy-start | bytes 1572868
  4.0 4.2 %collective-permute-start.1 = (bf16[2,256,512]{2,1,0:T(8,128)(2,1)S(1)}, bf16[2,256,512]{2,1,0:T(8,128)(2,1)S(1)}, u32[]{:S(2)}, u32[]{:S(2)}) collective-permute-start(bf16[2,256,512]{2,1,0:T(8,128)(2,1)S(1)} %bitcast.8), channel_id=1, source_target_pairs={{1,0},{0,1},{3,2},{2,3},{5,4},{4,5},{7,6},{6,7},{9,8},{8,9},{11,10... | collective-permute-start | bytes 1572872 | tf_op jit(solution)/shard_map/ppermute | solution.py:16
  4.4 4.2 %collective-permute-start.2 = (bf16[2,256,512]{2,1,0:T(8,128)(2,1)S(1)}, bf16[2,256,512]{2,1,0:T(8,128)(2,1)S(1)}, u32[]{:S(2)}, u32[]{:S(2)}) collective-permute-start(bf16[2,256,512]{2,1,0:T(8,128)(2,1)S(1)} %bitcast.16), channel_id=1, source_target_pairs={{1,0},{0,1},{3,2},{2,3},{5,4},{4,5},{7,6},{6,7},{9,8},{8,9},{11,10... | collective-permute-start | bytes 1572872 | tf_op jit(solution)/shard_map/ppermute | solution.py:16
  4.5 9.5 %collective-permute-start.4 = (bf16[2,128,512]{2,1,0:T(8,128)(2,1)S(1)}, bf16[2,128,512]{2,1,0:T(8,128)(2,1)S(1)}, u32[]{:S(2)}, u32[]{:S(2)}) collective-permute-start(bf16[2,128,512]{2,1,0:T(8,128)(2,1)S(1)} %get-tuple-element.28), channel_id=1, source_target_pairs={{0,4},{8,12},{4,0},{12,8},{1,5},{9,13},{5,1},{13,9},{2,6},{10,14},... | collective-permute-start | bytes 786440 | tf_op jit(solution)/shard_map/ppermute | solution.py:400
  7.5 14.4 %collective-permute-start.8 = (bf16[2,256,512]{2,1,0:T(8,128)(2,1)S(1)}, bf16[2,256,512]{2,1,0:T(8,128)(2,1)S(1)}, u32[]{:S(2)}, u32[]{:S(2)}) collective-permute-start(bf16[2,256,512]{2,1,0:T(8,128)(2,1)S(1)} %get-tuple-element.23.refs_7_.refs_4_), channel_id=1, source_target_pairs={{1,0},{0,1},{3,2},{2,3},{5,4},{4,5},{7,6},{6,7},{9,8},{8,9},{11,10... | collective-permute-start | bytes 1572872 | tf_op jit(solution)/shard_map/ppermute | solution.py:16
  7.5 15.9 %collective-permute-start.10 = (bf16[2,256,512]{2,1,0:T(8,128)(2,1)S(1)}, bf16[2,256,512]{2,1,0:T(8,128)(2,1)S(1)}, u32[]{:S(2)}, u32[]{:S(2)}) collective-permute-start(bf16[2,256,512]{2,1,0:T(8,128)(2,1)S(1)} %get-tuple-element.33), channel_id=1, source_target_pairs={{4,8},{8,4},{5,9},{9,5},{6,10},{10,6},{7,11},{11,7},{20,24},{24,20... | collective-permute-start | bytes 1572872 | tf_op jit(solution)/shard_map/ppermute | solution.py:400
  14.1 7.8 %collective-permute-start.5 = (bf16[2,128,512]{2,1,0:T(8,128)(2,1)S(1)}, bf16[2,128,512]{2,1,0:T(8,128)(2,1)S(1)}, u32[]{:S(2)}, u32[]{:S(2)}) collective-permute-start(bf16[2,128,512]{2,1,0:T(8,128)(2,1)S(1)} %collective-permute-done.4.refs_3_), channel_id=1, source_target_pairs={{2,0},{0,2},{3,1},{1,3},{6,4},{4,6},{7,5},{5,7},{10,8},{8,10},{11,... | collective-permute-start | bytes 786440 | tf_op jit(solution)/shard_map/ppermute | solution.py:16
  15.7 10.1 %collective-permute-start.6 = (bf16[2,128,512]{2,1,0:T(8,128)(2,1)S(1)}, bf16[2,128,512]{2,1,0:T(8,128)(2,1)S(1)}, u32[]{:S(2)}, u32[]{:S(2)}) collective-permute-start(bf16[2,128,512]{2,1,0:T(8,128)(2,1)S(1)} %collective-permute-done.4.refs_3_), channel_id=1, source_target_pairs={{1,0},{0,1},{3,2},{2,3},{5,4},{4,5},{7,6},{6,7},{9,8},{8,9},{11,10... | collective-permute-start | bytes 786440 | tf_op jit(solution)/shard_map/ppermute | solution.py:16
  16.6 9.2 %collective-permute-start.3 = (bf16[512,256]{1,0:T(8,128)(2,1)S(1)}, bf16[512,256]{1,0:T(8,128)(2,1)S(1)}, u32[]{:S(2)}, u32[]{:S(2)}) collective-permute-start(bf16[512,256]{1,0:T(8,128)(2,1)S(1)} %shard_map.49.refs_1_), channel_id=1, source_target_pairs={{0,4},{8,12},{4,0},{12,8},{1,5},{9,13},{5,1},{13,9},{2,6},{10,14},... | collective-permute-start | bytes 786440 | tf_op jit(solution)/shard_map/ppermute | solution.py:400
  21.9 3.9 %collective-permute-start.7 = (bf16[2,128,512]{2,1,0:T(8,128)(2,1)S(1)}, bf16[2,128,512]{2,1,0:T(8,128)(2,1)S(1)}, u32[]{:S(2)}, u32[]{:S(2)}) collective-permute-start(bf16[2,128,512]{2,1,0:T(8,128)(2,1)S(1)} %collective-permute-done.5.refs_4_), channel_id=1, source_target_pairs={{1,0},{0,1},{3,2},{2,3},{5,4},{4,5},{7,6},{6,7},{9,8},{8,9},{11,10... | collective-permute-start | bytes 786440 | tf_op jit(solution)/shard_map/ppermute | solution.py:16
  21.9 9.1 %collective-permute-start.13 = (bf16[512,256]{1,0:T(8,128)(2,1)S(1)}, bf16[512,256]{1,0:T(8,128)(2,1)S(1)}, u32[]{:S(2)}, u32[]{:S(2)}) collective-permute-start(bf16[512,256]{1,0:T(8,128)(2,1)S(1)} %shard_map.51.refs_1_), channel_id=1, source_target_pairs={{0,4},{8,12},{4,0},{12,8},{1,5},{9,13},{5,1},{13,9},{2,6},{10,14},... | collective-permute-start | bytes 786440 | tf_op jit(solution)/shard_map/ppermute | solution.py:400
  23.3 9.8 %collective-permute-start.11 = (bf16[2,256,512]{2,1,0:T(8,128)(2,1)S(1)}, bf16[2,256,512]{2,1,0:T(8,128)(2,1)S(1)}, u32[]{:S(2)}, u32[]{:S(2)}) collective-permute-start(bf16[2,256,512]{2,1,0:T(8,128)(2,1)S(1)} %collective-permute-done.10.refs_2_), channel_id=1, source_target_pairs={{1,0},{0,1},{3,2},{2,3},{5,4},{4,5},{7,6},{6,7},{9,8},{8,9},{11,10... | collective-permute-start | bytes 1572872 | tf_op jit(solution)/shard_map/ppermute | solution.py:16
  27.2 5.9 %collective-permute-start.9 = (bf16[512,256]{1,0:T(8,128)(2,1)S(1)}, bf16[512,256]{1,0:T(8,128)(2,1)S(1)}, u32[]{:S(2)}, u32[]{:S(2)}) collective-permute-start(bf16[512,256]{1,0:T(8,128)(2,1)S(1)} %get-tuple-element.32.refs_0_), channel_id=1, source_target_pairs={{4,8},{8,4},{5,9},{9,5},{6,10},{10,6},{7,11},{11,7},{20,24},{24,20... | collective-permute-start | bytes 786440 | tf_op jit(solution)/shard_map/ppermute | solution.py:400
  32.4 2.0 %collective-permute-start.14 = (bf16[512,256]{1,0:T(8,128)(2,1)S(1)}, bf16[512,256]{1,0:T(8,128)(2,1)S(1)}, u32[]{:S(2)}, u32[]{:S(2)}) collective-permute-start(bf16[512,256]{1,0:T(8,128)(2,1)S(1)} %get-tuple-element.36.refs_0_), channel_id=1, source_target_pairs={{4,8},{8,4},{5,9},{9,5},{6,10},{10,6},{7,11},{11,7},{20,24},{24,20... | collective-permute-start | bytes 786440 | tf_op jit(solution)/shard_map/ppermute | solution.py:400
  33.1 12.4 %collective-permute-start.12 = (bf16[512,256]{1,0:T(8,128)(2,1)S(1)}, bf16[512,256]{1,0:T(8,128)(2,1)S(1)}, u32[]{:S(2)}, u32[]{:S(2)}) collective-permute-start(bf16[512,256]{1,0:T(8,128)(2,1)S(1)} %shard_map.53.refs_2_), channel_id=1, source_target_pairs={{8,12},{4,0},{9,13},{5,1},{10,14},{6,2},{11,15},{7,3},{24,28},{20,... | collective-permute-start | bytes 786440 | tf_op jit(solution)/shard_map/ppermute | solution.py:450
  34.5 16.9 %collective-permute-start.15 = (bf16[512,256]{1,0:T(8,128)(2,1)S(1)}, bf16[512,256]{1,0:T(8,128)(2,1)S(1)}, u32[]{:S(2)}, u32[]{:S(2)}) collective-permute-start(bf16[512,256]{1,0:T(8,128)(2,1)S(1)} %shard_map.56.refs_3_), channel_id=1, source_target_pairs={{8,12},{4,0},{9,13},{5,1},{10,14},{6,2},{11,15},{7,3},{24,28},{20,... | collective-permute-start | bytes 786440 | tf_op jit(solution)/shard_map/ppermute | solution.py:450

commit v4 on v3

--- a/solution.py
+++ b/solution.py
@@ -203,12 +203,10 @@
     return out
 
 
-def merge_tip(left, q_refs, mats, height, mine, got, source, store):
-    n = len(q_refs)
-    starts = row_starts(height, n, 1)
-
+def source_of(left, q_refs, height, mine, got, source):
     @pl.when(left)
     def _():
+        starts = row_starts(height, len(q_refs), 1)
         for rows, value in each_product(parts_of(q_refs), starts, got[pl.ds(0, height), :]):
             source[rows, :] = (mine[rows, :].astype(jnp.float32) - value).astype(jnp.bfloat16)
 
@@ -216,41 +214,66 @@
     def _():
         source[...] = mine[pl.ds(0, height), :]
 
-    starts = row_starts(height, n, len(mats) // n)
+
+def tip_from(mats, orb_count, height, source, got, store):
+    starts = row_starts(height, orb_count, len(mats) // orb_count)
     for rows, value in each_product(mats, starts, source[...]):
         store(rows, (got[rows, :].astype(jnp.float32) - value).astype(jnp.bfloat16))
 
 
-def first_level(state, mine, got, mats, q, spikes, merge):
+def first_source(mine, got, q):
+    height, width = mine.shape
+    n = len(q)
+
+    def body(*refs):
+        mine_ref, got_ref = refs[:2]
+        source_of(is_even(), refs[2 : 2 + n], height, mine_ref, got_ref, refs[2 + n])
+
+    (source,) = call(
+        body,
+        [jax.ShapeDtypeStruct((height, width), jnp.bfloat16)],
+        [],
+        mine, got, *q,
+        flops=product_flops(height, width),
+    )
+    return source
+
+
+def merge_tip(left, q_refs, mats, height, mine, got, source, store):
+    source_of(left, q_refs, height, mine, got, source)
+    tip_from(mats, len(q_refs), height, source, got, store)
+
+
+def first_level(state, source, got, mats, spikes, merge):
     height, width = state.shape
-    n = len(q)
-
-    def body(*refs):
-        state_ref, mine_ref, got_ref = refs[:3]
+    n = len(spikes)
+
+    def body(*refs):
+        state_ref, source_ref, got_ref = refs[:3]
         mat_refs, rest = refs[3 : 3 + len(mats)], refs[3 + len(mats) :]
-        q_refs, spike_refs, merge_refs = (rest[k * n : (k + 1) * n] for k in range(3))
-        out, send, source, tip = rest[3 * n :]
+        spike_refs, merge_refs = rest[:n], rest[n : 2 * n]
+        out, send, rounded, tip = rest[2 * n :]
 
         def store_tip(rows, value):
             tip[rows, :] = value
 
-        merge_tip(is_even(), q_refs, parts_of(mat_refs), height, mine_ref, got_ref, source, store_tip)
+        tip_from(parts_of(mat_refs), n, height, source_ref, got_ref, store_tip)
         for rows, value in each_product(at_level(spike_refs, 0), row_starts(height, n, 1), tip[...]):
             new = state_ref[rows, :] - value
             out[rows, :] = new
-            source[rows, :] = new.astype(jnp.bfloat16)
+            rounded[rows, :] = new.astype(jnp.bfloat16)
 
         def store(rows, value):
             send[rows, :] = value
 
-        send_field(True, merge_refs, height, source, store)
+        send_field(True, merge_refs, height, rounded, store)
 
     return call(
         body,
         [jax.ShapeDtypeStruct((height, width), t) for t in (jnp.float32, jnp.bfloat16)],
         [pltpu.VMEM((height, width), jnp.bfloat16)] * 2,
-        state, mine, got, *mats, *q, *spikes, *merge,
-        flops=4 * product_flops(height, width),
+        state, source, got, *mats, *spikes, *merge,
+        flops=3 * product_flops(height, width),
     )
 
 
@@ -424,11 +447,16 @@
         sends.append(first_field(merge, hb))
         gots.append(swap(sends[c], pairs))
     first, _ = lax.optimization_barrier((first, sends[-1]))
-    across = [ring_gather(p, "orb") for p in ring_gather(first, "col")]
+    sources = [first_source(sends[0], gots[0], q)]
+    *across, _ = lax.optimization_barrier((*ring_gather(first, "col"), sources[0]))
+    across = [ring_gather(p, "orb") for p in across]
     first = [across[k][j] for j in range(len(q)) for k in range(cols)]
     later = ring_gather(later, "orb")
     for c in chunks:
-        states[c], sends[c] = first_level(states[c], sends[c], gots[c], first, q, spike_all, merge)
+        if c:
+            mine, _ = lax.optimization_barrier((sends[c], across[-1][-1]))
+            sources.append(first_source(mine, gots[c], q))
+        states[c], sends[c] = first_level(states[c], sources[c], gots[c], first, spike_all, merge)
 
     for level in range(1, levels):
         span = 1 << level

time: 52.9 us -> 52.6 us (level)
  waiting for transfers between devices: 29.6 us -> 25.8 us
  starting transfers between devices: 13.1 us -> 16.6 us
    ppermute x6, starting transfers between devices: 7.63 us -> 10.3 us  [swap(): return lax.ppermute(block, 'slab', pairs + [(b, a) for a, b in pairs])]
    ppermute x8, waiting for transfers between devices: 4.16 us -> 2.05 us  [ring_gather(): lax.ppermute(block, axis, [((i + step) % count, i) for i in range(count)])]
    ppermute x6, waiting for transfers between devices: 10.4 us -> 9.06 us  [swap(): return lax.ppermute(block, 'slab', pairs + [(b, a) for a, b in pairs])]
    ppermute x8, starting transfers between devices: 2.86 us -> 3.75 us  [ring_gather(): lax.ppermute(block, axis, [((i + step) % count, i) for i in range(count)])]
    pallas_call x10 -> x12, Pallas kernels: 5.78 us -> 5.79 us  [call(): pl.pallas_call(body, out_shape=outs, in_specs=[VMEM] * len(args), out_spe...]
where the time goes in v4:
time: 52.6 us; the launch traced here: 52.3 us
  waiting for transfers between devices  25.8 us (49%)
  starting transfers between devices  16.6 us (32%)
  Pallas kernels  7.22 us (14%)
  local copies, waits for them, and re-layouts  2.54 us (5%)
    ppermute x2, waiting for transfers between devices, per_device(): moved = [lax.ppermute(tips[c], 'slab', route) for c in chunks]  14.6 us
    ppermute x6, starting transfers between devices, swap(): return lax.ppermute(block, 'slab', pairs + [(b, a) for a, b in pairs])  10.3 us
    ppermute x6, waiting for transfers between devices, swap(): return lax.ppermute(block, 'slab', pairs + [(b, a) for a, b in pairs])  9.06 us
    pallas_call x12, Pallas kernels, call(): pl.pallas_call(body, out_shape=outs, in_specs=[VMEM] * len(args), out_spe...  5.79 us
    ppermute x8, starting transfers between devices, ring_gather(): lax.ppermute(block, axis, [((i + step) % count, i) for i in range(count)])  3.75 us
    ppermute x2, starting transfers between devices, per_device(): moved = [lax.ppermute(tips[c], 'slab', route) for c in chunks]  2.58 us
    unnamed x8, local copies, waits for them, and re-layouts  2.54 us
    ppermute x8, waiting for transfers between devices, ring_gather(): lax.ppermute(block, axis, [((i + step) % count, i) for i in range(count)])  2.05 us
  transfers between devices with their start and end apart: 16, of which 7 were waited for; matrix products, arithmetic and copies ran while one was open for 0% of the time, Pallas kernels for 10%

profile of v4, /device:TPU:0, one launch (start us, length us, event | category | flops | bytes accessed | tf_op | source)
XLA Modules:
  0.0 52.3 jit_solution(8749540023591895535)
XLA Ops:
  0.0 0.5 collective-permute-start
  0.5 1.2 %copy-done.2 = bf16[2,1,2,256,512]{4,3,2,1,0:T(8,128)(2,1)S(1)} copy-done((bf16[2,1,2,256,512]{4,3,2,1,0:T(8,128)(2,1)S(1)}, bf16[2,1,2,256,512]{4,3,2,1,0:T(8,128)(2,1)}, u32[]{:S(2)}) %copy-start.2) | copy-done | bytes 1048600
  1.7 1.0 %copy-done.3 = bf16[2,1,256,512]{3,2,1,0:T(8,128)(2,1)S(1)} copy-done((bf16[2,1,256,512]{3,2,1,0:T(8,128)(2,1)S(1)}, bf16[2,1,256,512]{3,2,1,0:T(8,128)(2,1)}, u32[]{:S(2)}) %copy-start.3) | copy-done | bytes 524312
  3.0 0.8 %shard_map.47 = (bf16[2,256,512]{2,1,0:T(8,128)(2,1)S(1)}, bf16[2,128,512]{2,1,0:T(8,128)(2,1)S(1)}, bf16[2,256,512]{2,1,0:T(8,128)(2,1)S(1)}) custom-call(bf16[2,2,256,512]{3,2,1,0:T(8,128)(2,1)S(1)} %get-tuple-element.24.refs_0_.refs_7_.refs_3_.refs_4_, bf16[2,2,256,512]{3,2,1,0:T(8,128)(2,1)S(1)} %collective-permute-done.refs_1_.refs_8_.refs_4_.refs_5_, ...), custom_call_target="tpu_custom_call" | custom-call | flops 536870912 | bytes 3932160 | tf_op jit(solution)/shard_map/pallas_call | solution.py:62
  4.0 0.4 collective-permute-start.1
  4.5 0.4 collective-permute-start.4
  4.9 2.7 %collective-permute-start.5 = (bf16[2,128,512]{2,1,0:T(8,128)(2,1)S(1)}, bf16[2,128,512]{2,1,0:T(8,128)(2,1)S(1)}, u32[]{:S(2)}, u32[]{:S(2)}) collective-permute-start(bf16[2,128,512]{2,1,0:T(8,128)(2,1)S(1)} %get-tuple-element.31), channel_id=1, source_target_pairs={{0,4},{8,12},{4,0},{12,8},{1,5},{9,13},{5,1},{13,9},{2,6},{10,14},... | collective-permute-start | bytes 786440 | tf_op jit(solution)/shard_map/ppermute | solution.py:423
  7.6 0.7 %collective-permute-start.10 = (bf16[2,256,512]{2,1,0:T(8,128)(2,1)S(1)}, bf16[2,256,512]{2,1,0:T(8,128)(2,1)S(1)}, u32[]{:S(2)}, u32[]{:S(2)}) collective-permute-start(bf16[2,256,512]{2,1,0:T(8,128)(2,1)S(1)} %get-tuple-element.38), channel_id=1, source_target_pairs={{4,8},{8,4},{5,9},{9,5},{6,10},{10,6},{7,11},{11,7},{20,24},{24,20... | collective-permute-start | bytes 1572872 | tf_op jit(solution)/shard_map/ppermute | solution.py:423
  8.3 0.4 shard_map.48
  8.8 0.5 shard_map.49.refs_0_
  9.2 4.0 %collective-permute-start.3 = (bf16[512,256]{1,0:T(8,128)(2,1)S(1)}, bf16[512,256]{1,0:T(8,128)(2,1)S(1)}, u32[]{:S(2)}, u32[]{:S(2)}) collective-permute-start(bf16[512,256]{1,0:T(8,128)(2,1)S(1)} %shard_map.49.refs_0_), channel_id=1, source_target_pairs={{0,4},{8,12},{4,0},{12,8},{1,5},{9,13},{5,1},{13,9},{2,6},{10,14},... | collective-permute-start | bytes 786440 | tf_op jit(solution)/shard_map/ppermute | solution.py:423
  13.2 0.4 shard_map.51
  13.7 0.5 shard_map.52.refs_0_
  14.2 0.6 %collective-permute-done.5.refs_3_ = bf16[2,128,512]{2,1,0:T(8,128)(2,1)S(1)} collective-permute-done((bf16[2,128,512]{2,1,0:T(8,128)(2,1)S(1)}, bf16[2,128,512]{2,1,0:T(8,128)(2,1)S(1)}, u32[]{:S(2)}, u32[]{:S(2)}) %collective-permute-start.5) | collective-permute-done | bytes 262176 | tf_op jit(solution)/shard_map/ppermute | solution.py:423
  14.7 1.9 %collective-permute-start.6 = (bf16[2,128,512]{2,1,0:T(8,128)(2,1)S(1)}, bf16[2,128,512]{2,1,0:T(8,128)(2,1)S(1)}, u32[]{:S(2)}, u32[]{:S(2)}) collective-permute-start(bf16[2,128,512]{2,1,0:T(8,128)(2,1)S(1)} %collective-permute-done.5.refs_3_), channel_id=1, source_target_pairs={{2,0},{0,2},{3,1},{1,3},{6,4},{4,6},{7,5},{5,7},{10,8},{8,10},{11,... | collective-permute-start | bytes 786440 | tf_op jit(solution)/shard_map/ppermute | solution.py:16
  16.6 3.4 %collective-permute-done.3.refs_1_.refs_2_ = bf16[512,256]{1,0:T(8,128)(2,1)S(1)} collective-permute-done((bf16[512,256]{1,0:T(8,128)(2,1)S(1)}, bf16[512,256]{1,0:T(8,128)(2,1)S(1)}, u32[]{:S(2)}, u32[]{:S(2)}) %collective-permute-start.3) | collective-permute-done | bytes 262176 | tf_op jit(solution)/shard_map/ppermute | solution.py:423
  20.0 0.4 shard_map.50.refs_1_
  20.5 1.9 %collective-permute-done.6.refs_4_ = bf16[2,128,512]{2,1,0:T(8,128)(2,1)S(1)} collective-permute-done((bf16[2,128,512]{2,1,0:T(8,128)(2,1)S(1)}, bf16[2,128,512]{2,1,0:T(8,128)(2,1)S(1)}, u32[]{:S(2)}, u32[]{:S(2)}) %collective-permute-start.6) | collective-permute-done | bytes 262176 | tf_op jit(solution)/shard_map/ppermute | solution.py:16
  22.4 0.5 collective-permute-start.8
  22.9 1.5 %collective-permute-start.13 = (bf16[512,256]{1,0:T(8,128)(2,1)S(1)}, bf16[512,256]{1,0:T(8,128)(2,1)S(1)}, u32[]{:S(2)}, u32[]{:S(2)}) collective-permute-start(bf16[512,256]{1,0:T(8,128)(2,1)S(1)} %shard_map.52.refs_0_), channel_id=1, source_target_pairs={{0,4},{8,12},{4,0},{12,8},{1,5},{9,13},{5,1},{13,9},{2,6},{10,14},... | collective-permute-start | bytes 786440 | tf_op jit(solution)/shard_map/ppermute | solution.py:423
  24.5 0.9 %shard_map.53 = (f32[512,256]{1,0:T(8,128)S(1)}, bf16[512,256]{1,0:T(8,128)(2,1)S(1)}) custom-call(f32[512,256]{1,0:T(8,128)S(1)} %get-tuple-element.28.refs_0_, bf16[512,256]{1,0:T(8,128)(2,1)S(1)} %shard_map.50.refs_1_, bf16[512,256]{1,0:T(8,128)(2,1)S(1)} %collective-permute-done.3.refs_1_.refs_2_, ...), custom_call_target="tpu_custom_call" | custom-call | flops 805306368 | bytes 6029312 | tf_op jit(solution)/shard_map/pallas_call | solution.py:62
  25.4 0.7 %collective-permute-start.9 = (bf16[512,256]{1,0:T(8,128)(2,1)S(1)}, bf16[512,256]{1,0:T(8,128)(2,1)S(1)}, u32[]{:S(2)}, u32[]{:S(2)}) collective-permute-start(bf16[512,256]{1,0:T(8,128)(2,1)S(1)} %get-tuple-element.37.refs_0_), channel_id=1, source_target_pairs={{4,8},{8,4},{5,9},{9,5},{6,10},{10,6},{7,11},{11,7},{20,24},{24,20... | collective-permute-start | bytes 786440 | tf_op jit(solution)/shard_map/ppermute | solution.py:423
  26.1 5.1 %collective-permute-done.13.refs_1_.refs_2_ = bf16[512,256]{1,0:T(8,128)(2,1)S(1)} collective-permute-done((bf16[512,256]{1,0:T(8,128)(2,1)S(1)}, bf16[512,256]{1,0:T(8,128)(2,1)S(1)}, u32[]{:S(2)}, u32[]{:S(2)}) %collective-permute-start.13) | collective-permute-done | bytes 262176 | tf_op jit(solution)/shard_map/ppermute | solution.py:423
  31.2 0.4 shard_map.56.refs_1_
  31.6 0.9 %shard_map.57 = (f32[512,256]{1,0:T(8,128)S(1)}, bf16[512,256]{1,0:T(8,128)(2,1)S(1)}) custom-call(f32[512,256]{1,0:T(8,128)S(1)} %get-tuple-element.39.refs_0_, bf16[512,256]{1,0:T(8,128)(2,1)S(1)} %shard_map.56.refs_1_, bf16[512,256]{1,0:T(8,128)(2,1)S(1)} %collective-permute-done.13.refs_1_.refs_2_, ...), custom_call_target="tpu_custom_call" | custom-call | flops 805306368 | bytes 6029312 | tf_op jit(solution)/shard_map/pallas_call | solution.py:62
  32.6 0.7 %collective-permute-start.14 = (bf16[512,256]{1,0:T(8,128)(2,1)S(1)}, bf16[512,256]{1,0:T(8,128)(2,1)S(1)}, u32[]{:S(2)}, u32[]{:S(2)}) collective-permute-start(bf16[512,256]{1,0:T(8,128)(2,1)S(1)} %get-tuple-element.42.refs_0_), channel_id=1, source_target_pairs={{4,8},{8,4},{5,9},{9,5},{6,10},{10,6},{7,11},{11,7},{20,24},{24,20... | collective-permute-start | bytes 786440 | tf_op jit(solution)/shard_map/ppermute | solution.py:423
  33.3 1.3 %collective-permute-start.12 = (bf16[512,256]{1,0:T(8,128)(2,1)S(1)}, bf16[512,256]{1,0:T(8,128)(2,1)S(1)}, u32[]{:S(2)}, u32[]{:S(2)}) collective-permute-start(bf16[512,256]{1,0:T(8,128)(2,1)S(1)} %shard_map.54.refs_2_), channel_id=1, source_target_pairs={{8,12},{4,0},{9,13},{5,1},{10,14},{6,2},{11,15},{7,3},{24,28},{20,... | collective-permute-start | bytes 786440 | tf_op jit(solution)/shard_map/ppermute | solution.py:478
  34.6 1.3 %collective-permute-start.15 = (bf16[512,256]{1,0:T(8,128)(2,1)S(1)}, bf16[512,256]{1,0:T(8,128)(2,1)S(1)}, u32[]{:S(2)}, u32[]{:S(2)}) collective-permute-start(bf16[512,256]{1,0:T(8,128)(2,1)S(1)} %shard_map.58.refs_3_), channel_id=1, source_target_pairs={{8,12},{4,0},{9,13},{5,1},{10,14},{6,2},{11,15},{7,3},{24,28},{20,... | collective-permute-start | bytes 786440 | tf_op jit(solution)/shard_map/ppermute | solution.py:478
  35.9 10.3 %collective-permute-done.12.refs_1_ = bf16[512,256]{1,0:T(8,128)(2,1)S(1)} collective-permute-done((bf16[512,256]{1,0:T(8,128)(2,1)S(1)}, bf16[512,256]{1,0:T(8,128)(2,1)S(1)}, u32[]{:S(2)}, u32[]{:S(2)}) %collective-permute-start.12) | collective-permute-done | bytes 262176 | tf_op jit(solution)/shard_map/ppermute | solution.py:478
  46.2 0.5 shard_map.55.refs_0_
  46.7 4.3 %collective-permute-done.15.refs_2_ = bf16[512,256]{1,0:T(8,128)(2,1)S(1)} collective-permute-done((bf16[512,256]{1,0:T(8,128)(2,1)S(1)}, bf16[512,256]{1,0:T(8,128)(2,1)S(1)}, u32[]{:S(2)}, u32[]{:S(2)}) %collective-permute-start.15) | collective-permute-done | bytes 262176 | tf_op jit(solution)/shard_map/ppermute | solution.py:478
  51.0 1.3 %shard_map.59 = f32[2,512,256]{2,1,0:T(8,128)} custom-call(f32[512,256]{1,0:T(8,128)S(1)} %shard_map.55.refs_0_, f32[512,256]{1,0:T(8,128)S(1)} %get-tuple-element.41.refs_1_, bf16[512,256]{1,0:T(8,128)(2,1)S(1)} %collective-permute-done.15.refs_2_, bf16[512,256]{1,0:T(8,128)(2,1)S(1)} %shard_map.58.refs_3_, ...), custom_call_target="tpu_custom_call" | custom-call | flops 268435456 | bytes 1572864 | tf_op jit(solution)/shard_map/pallas_call | solution.py:405
  (22 shorter events, 0.7 us)
Async XLA Ops:
  0.0 3.0 %collective-permute-start = (bf16[2,2,256,512]{3,2,1,0:T(8,128)(2,1)}, bf16[2,2,256,512]{3,2,1,0:T(8,128)(2,1)S(1)}, u32[]{:S(2)}, u32[]{:S(2)}) collective-permute-start(bf16[2,2,256,512]{3,2,1,0:T(8,128)(2,1)} %bitcast.13), channel_id=1, source_target_pairs={{1,0},{0,1},{3,2},{2,3},{5,4},{4,5},{7,6},{6,7},{9,8},{8,9},{11,10... | collective-permute-start | bytes 3145736 | tf_op jit(solution)/shard_map/ppermute | solution.py:16
  0.5 1.2 %copy-start.2 = (bf16[2,1,2,256,512]{4,3,2,1,0:T(8,128)(2,1)S(1)}, bf16[2,1,2,256,512]{4,3,2,1,0:T(8,128)(2,1)}, u32[]{:S(2)}) copy-start(bf16[2,1,2,256,512]{4,3,2,1,0:T(8,128)(2,1)} %param.6) | copy-start | bytes 3145732
  1.7 1.0 %copy-start.3 = (bf16[2,1,256,512]{3,2,1,0:T(8,128)(2,1)S(1)}, bf16[2,1,256,512]{3,2,1,0:T(8,128)(2,1)}, u32[]{:S(2)}) copy-start(bf16[2,1,256,512]{3,2,1,0:T(8,128)(2,1)} %param.7) | copy-start | bytes 1572868
  3.0 1.0 %copy-start = (bf16[2,1,256,512]{3,2,1,0:T(8,128)(2,1)S(1)}, bf16[2,1,256,512]{3,2,1,0:T(8,128)(2,1)}, u32[]{:S(2)}) copy-start(bf16[2,1,256,512]{3,2,1,0:T(8,128)(2,1)} %param.5) | copy-start | bytes 1572868
  3.0 5.3 %copy-start.1 = (bf16[2,1,512,256]{3,2,1,0:T(8,128)(2,1)S(1)}, bf16[2,1,512,256]{3,2,1,0:T(8,128)(2,1)}, u32[]{:S(2)}) copy-start(bf16[2,1,512,256]{3,2,1,0:T(8,128)(2,1)} %param.4) | copy-start | bytes 1572868
  4.0 4.3 %collective-permute-start.1 = (bf16[2,256,512]{2,1,0:T(8,128)(2,1)S(1)}, bf16[2,256,512]{2,1,0:T(8,128)(2,1)S(1)}, u32[]{:S(2)}, u32[]{:S(2)}) collective-permute-start(bf16[2,256,512]{2,1,0:T(8,128)(2,1)S(1)} %bitcast.8), channel_id=1, source_target_pairs={{1,0},{0,1},{3,2},{2,3},{5,4},{4,5},{7,6},{6,7},{9,8},{8,9},{11,10... | collective-permute-start | bytes 1572872 | tf_op jit(solution)/shard_map/ppermute | solution.py:16
  4.4 4.4 %collective-permute-start.2 = (bf16[2,256,512]{2,1,0:T(8,128)(2,1)S(1)}, bf16[2,256,512]{2,1,0:T(8,128)(2,1)S(1)}, u32[]{:S(2)}, u32[]{:S(2)}) collective-permute-start(bf16[2,256,512]{2,1,0:T(8,128)(2,1)S(1)} %bitcast.16), channel_id=1, source_target_pairs={{1,0},{0,1},{3,2},{2,3},{5,4},{4,5},{7,6},{6,7},{9,8},{8,9},{11,10... | collective-permute-start | bytes 1572872 | tf_op jit(solution)/shard_map/ppermute | solution.py:16
  4.5 12.1 %collective-permute-start.4 = (bf16[2,256,512]{2,1,0:T(8,128)(2,1)S(1)}, bf16[2,256,512]{2,1,0:T(8,128)(2,1)S(1)}, u32[]{:S(2)}, u32[]{:S(2)}) collective-permute-start(bf16[2,256,512]{2,1,0:T(8,128)(2,1)S(1)} %get-tuple-element.26.refs_2_.refs_4_), channel_id=1, source_target_pairs={{1,0},{0,1},{3,2},{2,3},{5,4},{4,5},{7,6},{6,7},{9,8},{8,9},{11,10... | collective-permute-start | bytes 1572872 | tf_op jit(solution)/shard_map/ppermute | solution.py:16
  4.9 9.9 %collective-permute-start.5 = (bf16[2,128,512]{2,1,0:T(8,128)(2,1)S(1)}, bf16[2,128,512]{2,1,0:T(8,128)(2,1)S(1)}, u32[]{:S(2)}, u32[]{:S(2)}) collective-permute-start(bf16[2,128,512]{2,1,0:T(8,128)(2,1)S(1)} %get-tuple-element.31), channel_id=1, source_target_pairs={{0,4},{8,12},{4,0},{12,8},{1,5},{9,13},{5,1},{13,9},{2,6},{10,14},... | collective-permute-start | bytes 786440 | tf_op jit(solution)/shard_map/ppermute | solution.py:423
  7.6 16.9 %collective-permute-start.10 = (bf16[2,256,512]{2,1,0:T(8,128)(2,1)S(1)}, bf16[2,256,512]{2,1,0:T(8,128)(2,1)S(1)}, u32[]{:S(2)}, u32[]{:S(2)}) collective-permute-start(bf16[2,256,512]{2,1,0:T(8,128)(2,1)S(1)} %get-tuple-element.38), channel_id=1, source_target_pairs={{4,8},{8,4},{5,9},{9,5},{6,10},{10,6},{7,11},{11,7},{20,24},{24,20... | collective-permute-start | bytes 1572872 | tf_op jit(solution)/shard_map/ppermute | solution.py:423
  9.2 10.8 %collective-permute-start.3 = (bf16[512,256]{1,0:T(8,128)(2,1)S(1)}, bf16[512,256]{1,0:T(8,128)(2,1)S(1)}, u32[]{:S(2)}, u32[]{:S(2)}) collective-permute-start(bf16[512,256]{1,0:T(8,128)(2,1)S(1)} %shard_map.49.refs_0_), channel_id=1, source_target_pairs={{0,4},{8,12},{4,0},{12,8},{1,5},{9,13},{5,1},{13,9},{2,6},{10,14},... | collective-permute-start | bytes 786440 | tf_op jit(solution)/shard_map/ppermute | solution.py:423
  14.7 7.7 %collective-permute-start.6 = (bf16[2,128,512]{2,1,0:T(8,128)(2,1)S(1)}, bf16[2,128,512]{2,1,0:T(8,128)(2,1)S(1)}, u32[]{:S(2)}, u32[]{:S(2)}) collective-permute-start(bf16[2,128,512]{2,1,0:T(8,128)(2,1)S(1)} %collective-permute-done.5.refs_3_), channel_id=1, source_target_pairs={{2,0},{0,2},{3,1},{1,3},{6,4},{4,6},{7,5},{5,7},{10,8},{8,10},{11,... | collective-permute-start | bytes 786440 | tf_op jit(solution)/shard_map/ppermute | solution.py:16
  22.4 2.0 %collective-permute-start.7 = (bf16[2,128,512]{2,1,0:T(8,128)(2,1)S(1)}, bf16[2,128,512]{2,1,0:T(8,128)(2,1)S(1)}, u32[]{:S(2)}, u32[]{:S(2)}) collective-permute-start(bf16[2,128,512]{2,1,0:T(8,128)(2,1)S(1)} %collective-permute-done.5.refs_3_), channel_id=1, source_target_pairs={{1,0},{0,1},{3,2},{2,3},{5,4},{4,5},{7,6},{6,7},{9,8},{8,9},{11,10... | collective-permute-start | bytes 786440 | tf_op jit(solution)/shard_map/ppermute | solution.py:16
  22.4 2.0 %collective-permute-start.8 = (bf16[2,128,512]{2,1,0:T(8,128)(2,1)S(1)}, bf16[2,128,512]{2,1,0:T(8,128)(2,1)S(1)}, u32[]{:S(2)}, u32[]{:S(2)}) collective-permute-start(bf16[2,128,512]{2,1,0:T(8,128)(2,1)S(1)} %collective-permute-done.6.refs_4_), channel_id=1, source_target_pairs={{1,0},{0,1},{3,2},{2,3},{5,4},{4,5},{7,6},{6,7},{9,8},{8,9},{11,10... | collective-permute-start | bytes 786440 | tf_op jit(solution)/shard_map/ppermute | solution.py:16
  22.9 8.2 %collective-permute-start.13 = (bf16[512,256]{1,0:T(8,128)(2,1)S(1)}, bf16[512,256]{1,0:T(8,128)(2,1)S(1)}, u32[]{:S(2)}, u32[]{:S(2)}) collective-permute-start(bf16[512,256]{1,0:T(8,128)(2,1)S(1)} %shard_map.52.refs_0_), channel_id=1, source_target_pairs={{0,4},{8,12},{4,0},{12,8},{1,5},{9,13},{5,1},{13,9},{2,6},{10,14},... | collective-permute-start | bytes 786440 | tf_op jit(solution)/shard_map/ppermute | solution.py:423
  24.5 8.8 %collective-permute-start.11 = (bf16[2,256,512]{2,1,0:T(8,128)(2,1)S(1)}, bf16[2,256,512]{2,1,0:T(8,128)(2,1)S(1)}, u32[]{:S(2)}, u32[]{:S(2)}) collective-permute-start(bf16[2,256,512]{2,1,0:T(8,128)(2,1)S(1)} %collective-permute-done.10.refs_2_), channel_id=1, source_target_pairs={{1,0},{0,1},{3,2},{2,3},{5,4},{4,5},{7,6},{6,7},{9,8},{8,9},{11,10... | collective-permute-start | bytes 1572872 | tf_op jit(solution)/shard_map/ppermute | solution.py:16
  25.4 7.8 %collective-permute-start.9 = (bf16[512,256]{1,0:T(8,128)(2,1)S(1)}, bf16[512,256]{1,0:T(8,128)(2,1)S(1)}, u32[]{:S(2)}, u32[]{:S(2)}) collective-permute-start(bf16[512,256]{1,0:T(8,128)(2,1)S(1)} %get-tuple-element.37.refs_0_), channel_id=1, source_target_pairs={{4,8},{8,4},{5,9},{9,5},{6,10},{10,6},{7,11},{11,7},{20,24},{24,20... | collective-permute-start | bytes 786440 | tf_op jit(solution)/shard_map/ppermute | solution.py:423
  32.6 2.0 %collective-permute-start.14 = (bf16[512,256]{1,0:T(8,128)(2,1)S(1)}, bf16[512,256]{1,0:T(8,128)(2,1)S(1)}, u32[]{:S(2)}, u32[]{:S(2)}) collective-permute-start(bf16[512,256]{1,0:T(8,128)(2,1)S(1)} %get-tuple-element.42.refs_0_), channel_id=1, source_target_pairs={{4,8},{8,4},{5,9},{9,5},{6,10},{10,6},{7,11},{11,7},{20,24},{24,20... | collective-permute-start | bytes 786440 | tf_op jit(solution)/shard_map/ppermute | solution.py:423
  33.3 12.9 %collective-permute-start.12 = (bf16[512,256]{1,0:T(8,128)(2,1)S(1)}, bf16[512,256]{1,0:T(8,128)(2,1)S(1)}, u32[]{:S(2)}, u32[]{:S(2)}) collective-permute-start(bf16[512,256]{1,0:T(8,128)(2,1)S(1)} %shard_map.54.refs_2_), channel_id=1, source_target_pairs={{8,12},{4,0},{9,13},{5,1},{10,14},{6,2},{11,15},{7,3},{24,28},{20,... | collective-permute-start | bytes 786440 | tf_op jit(solution)/shard_map/ppermute | solution.py:478
  34.6 16.4 %collective-permute-start.15 = (bf16[512,256]{1,0:T(8,128)(2,1)S(1)}, bf16[512,256]{1,0:T(8,128)(2,1)S(1)}, u32[]{:S(2)}, u32[]{:S(2)}) collective-permute-start(bf16[512,256]{1,0:T(8,128)(2,1)S(1)} %shard_map.58.refs_3_), channel_id=1, source_target_pairs={{8,12},{4,0},{9,13},{5,1},{10,14},{6,2},{11,15},{7,3},{24,28},{20,... | collective-permute-start | bytes 786440 | tf_op jit(solution)/shard_map/ppermute | solution.py:478

commit v5 on v4

--- a/solution.py
+++ b/solution.py
@@ -137,48 +137,76 @@
         store(pl.ds(0, height), hb_ref[...])
 
 
-def first_sends(spikes, merge_own, levels, cols):
+def first_matrix(spikes, merge_own, levels, cols):
+    n = len(spikes)
+    size, height = merge_own.shape[1:]
+    share = size // cols
+    cut = min(128, height)
+
+    def body(*refs):
+        spike_refs, merge_ref, out = refs[:n], refs[n], refs[n + 1]
+        rows = rows_of(lax.axis_index("col") * share, share)
+
+        @pl.when(is_even())
+        def _():
+            own_product(spike_refs, merge_ref, rows, 0, cut, out)
+
+        @pl.when(jnp.logical_not(is_even()))
+        def _():
+            for p in range(2):
+                out[p] = spike_refs[0][p, 0, rows, :]
+
+    (out,) = call(
+        body,
+        [jax.ShapeDtypeStruct((2, share, height), jnp.bfloat16)],
+        [],
+        *spikes, merge_own,
+        flops=product_flops(height, height) // cols,
+    )
+    return out
+
+
+def own_product(spike_refs, merge_ref, rows, level, cut, out):
+    n = len(spike_refs)
+    height = out.shape[2]
+    size = height // n
+    starts = row_starts(height, n, 1)
+    for k in range(height // cut):
+        window = pl.ds(k * cut, cut)
+        value = 0.0
+        for spike, start in zip(spike_refs, starts):
+            field = jnp.concatenate([spike[p, level, :, window] for p in range(2)], axis=1)
+            piece = tuple(lambda p=p, start=start: merge_ref[p, rows, rows_of(start, size)] for p in range(2))
+            for _, part in each_product([piece], [0], field):
+                value += part
+        out[0, :, window] = value[:, :cut].astype(jnp.bfloat16)
+        out[1, :, window] = value[:, cut:].astype(jnp.bfloat16)
+
+
+def own_matrix(spikes, merge_own, levels):
     n = len(spikes)
     size, height = merge_own.shape[1:]
     cut = min(128, height)
 
     def body(*refs):
         spike_refs, merge_ref = refs[:n], refs[n]
-        q_out, first, later = refs[n + 1 :]
+        q_out, later = refs[n + 1 :]
         device = lax.axis_index("slab")
-        level_left = lowest_bit(device + 1, levels)
+        own_product(spike_refs, merge_ref, pl.ds(0, size), lowest_bit(device + 1, levels), cut, q_out)
         level_right = lowest_bit(device, levels)
 
-        starts = row_starts(height, n, 1)
-        for k in range(height // cut):
-            window = pl.ds(k * cut, cut)
-            value = 0.0
-            for spike, start in zip(spike_refs, starts):
-                field = jnp.concatenate([spike[p, level_left, :, window] for p in range(2)], axis=1)
-                piece = tuple(lambda p=p, start=start: merge_ref[p, :, rows_of(start, size)] for p in range(2))
-                for _, part in each_product([piece], [0], field):
-                    value += part
-            q_out[0, :, window] = value[:, :cut].astype(jnp.bfloat16)
-            q_out[1, :, window] = value[:, cut:].astype(jnp.bfloat16)
-
-        share = size // cols
-        rows = rows_of(lax.axis_index("col") * share, share) if cols > 1 else pl.ds(0, size)
-
         @pl.when(is_even())
         def _():
-            first[...] = q_out[:, rows, :]
             for p in range(2):
                 later[p] = spike_refs[0][p, level_right]
 
         @pl.when(jnp.logical_not(is_even()))
         def _():
-            for p in range(2):
-                first[p] = spike_refs[0][p, 0, rows, :]
             later[...] = q_out[...]
 
     return call(
         body,
-        [jax.ShapeDtypeStruct((2, rows, height), jnp.bfloat16) for rows in (size, size // cols, size)],
+        [jax.ShapeDtypeStruct((2, size, height), jnp.bfloat16)] * 2,
         [],
         *spikes, merge_own,
         flops=product_flops(height, height),
@@ -432,14 +460,13 @@
     spike_all = ring_gather(spikes[:, 0], "orb")
     spike_own, merge_own = fetch(spikes[:, 0], merge_inv[:, 0])
     spike_all[0] = spike_own
-    q_own, first, later = first_sends(spike_all, merge_own, levels, cols)
     pairs = [(i, i + 1) for i in range(0, slabs, 2)]
-    first = swap(first, pairs)
+    first = swap(first_matrix(spike_all, merge_own, levels, cols), pairs)
+    inverse = ring_gather(dinv[:, 0], "orb")
+    merge = [merge_own] + ring_gather(merge_inv[:, 0], "orb")[1:]
+    q_own, later = own_matrix(spike_all, merge_own, levels)
     later = swap(later, [(i, i + 1) for i in range(1, slabs - 1, 2)])
     q = ring_gather(q_own, "orb")
-    dinv, merge_inv, _ = lax.optimization_barrier((dinv, merge_inv, q_own))
-    inverse = ring_gather(dinv[:, 0], "orb")
-    merge = [merge_own] + ring_gather(merge_inv[:, 0], "orb")[1:]
     states, sends, gots = [], [], []
     for c in chunks:
         state, hb = start_state(inverse, rhs[:, 0], sum(widths[:c]), widths[c])

time: 52.6 us -> 51.8 us (0.985)
  waiting for transfers between devices: 25.8 us -> 24.5 us
    ppermute x6, waiting for transfers between devices: 9.06 us -> 8.18 us  [swap(): return lax.ppermute(block, 'slab', pairs + [(b, a) for a, b in pairs])]
    pallas_call x12 -> x13, Pallas kernels: 5.79 us -> 6.23 us  [call(): pl.pallas_call(body, out_shape=outs, in_specs=[VMEM] * len(args), out_spe...]
  transfers between devices with their start and end apart: 16 -> 16, of which waited for: 7 -> 6; matrix products, arithmetic and copies ran while one was open for 0% -> 0% of each run, Pallas kernels for 10% -> 12%
where the time goes in v5:
time: 51.8 us; the launch traced here: 51.5 us
  waiting for transfers between devices  24.5 us (47%)
  starting transfers between devices  16.8 us (32%)
  Pallas kernels  7.66 us (15%)
  local copies, waits for them, and re-layouts  2.28 us (4%)
    ppermute x2, waiting for transfers between devices, per_device(): moved = [lax.ppermute(tips[c], 'slab', route) for c in chunks]  14.6 us
    ppermute x6, starting transfers between devices, swap(): return lax.ppermute(block, 'slab', pairs + [(b, a) for a, b in pairs])  10.1 us
    ppermute x6, waiting for transfers between devices, swap(): return lax.ppermute(block, 'slab', pairs + [(b, a) for a, b in pairs])  8.18 us
    pallas_call x13, Pallas kernels, call(): pl.pallas_call(body, out_shape=outs, in_specs=[VMEM] * len(args), out_spe...  6.23 us
    ppermute x8, starting transfers between devices, ring_gather(): lax.ppermute(block, axis, [((i + step) % count, i) for i in range(count)])  4.14 us
    ppermute x2, starting transfers between devices, per_device(): moved = [lax.ppermute(tips[c], 'slab', route) for c in chunks]  2.58 us
    unnamed x8, local copies, waits for them, and re-layouts  2.28 us
    ppermute x8, waiting for transfers between devices, ring_gather(): lax.ppermute(block, axis, [((i + step) % count, i) for i in range(count)])  1.68 us
  transfers between devices with their start and end apart: 16, of which 6 were waited for; matrix products, arithmetic and copies ran while one was open for 0% of the time, Pallas kernels for 12%

profile of v5, /device:TPU:0, one launch (start us, length us, event | category | flops | bytes accessed | tf_op | source)
XLA Modules:
  0.0 51.5 jit_solution(18025726723405015660)
XLA Ops:
  0.0 0.5 collective-permute-start.3
  0.5 0.5 collective-permute-start.1
  1.0 1.2 %copy-done.2 = bf16[2,1,2,256,512]{4,3,2,1,0:T(8,128)(2,1)S(1)} copy-done((bf16[2,1,2,256,512]{4,3,2,1,0:T(8,128)(2,1)S(1)}, bf16[2,1,2,256,512]{4,3,2,1,0:T(8,128)(2,1)}, u32[]{:S(2)}) %copy-start.2) | copy-done | bytes 1048600
  2.2 1.0 %copy-done.3 = bf16[2,1,256,512]{3,2,1,0:T(8,128)(2,1)S(1)} copy-done((bf16[2,1,256,512]{3,2,1,0:T(8,128)(2,1)S(1)}, bf16[2,1,256,512]{3,2,1,0:T(8,128)(2,1)}, u32[]{:S(2)}) %copy-start.3) | copy-done | bytes 524312
  3.4 0.8 %shard_map.49 = (bf16[2,256,512]{2,1,0:T(8,128)(2,1)S(1)}, bf16[2,256,512]{2,1,0:T(8,128)(2,1)S(1)}) custom-call(bf16[2,2,256,512]{3,2,1,0:T(8,128)(2,1)S(1)} %get-tuple-element.24.refs_0_.refs_7_.refs_3_.refs_4_, bf16[2,2,256,512]{3,2,1,0:T(8,128)(2,1)S(1)} %collective-permute-done.3.refs_1_.refs_8_.refs_4_.refs_5_, ...), custom_call_target="tpu_custom_call" | custom-call | flops 536870912 | bytes 3670016 | tf_op jit(solution)/shard_map/pallas_call | solution.py:62
  4.3 0.5 shard_map.51
  4.7 2.7 %collective-permute-start.5 = (bf16[2,128,512]{2,1,0:T(8,128)(2,1)S(1)}, bf16[2,128,512]{2,1,0:T(8,128)(2,1)S(1)}, u32[]{:S(2)}, u32[]{:S(2)}) collective-permute-start(bf16[2,128,512]{2,1,0:T(8,128)(2,1)S(1)} %shard_map.51), channel_id=1, source_target_pairs={{0,4},{8,12},{4,0},{12,8},{1,5},{9,13},{5,1},{13,9},{2,6},{10,14},... | collective-permute-start | bytes 786440 | tf_op jit(solution)/shard_map/ppermute | solution.py:451
  7.4 0.7 %collective-permute-start.10 = (bf16[2,256,512]{2,1,0:T(8,128)(2,1)S(1)}, bf16[2,256,512]{2,1,0:T(8,128)(2,1)S(1)}, u32[]{:S(2)}, u32[]{:S(2)}) collective-permute-start(bf16[2,256,512]{2,1,0:T(8,128)(2,1)S(1)} %get-tuple-element.32), channel_id=1, source_target_pairs={{4,8},{8,4},{5,9},{9,5},{6,10},{10,6},{7,11},{11,7},{20,24},{24,20... | collective-permute-start | bytes 1572872 | tf_op jit(solution)/shard_map/ppermute | solution.py:451
  8.1 0.4 shard_map.46
  8.6 0.5 shard_map.48.refs_0_
  9.0 4.0 %collective-permute-start.2 = (bf16[512,256]{1,0:T(8,128)(2,1)S(1)}, bf16[512,256]{1,0:T(8,128)(2,1)S(1)}, u32[]{:S(2)}, u32[]{:S(2)}) collective-permute-start(bf16[512,256]{1,0:T(8,128)(2,1)S(1)} %shard_map.48.refs_0_), channel_id=1, source_target_pairs={{0,4},{8,12},{4,0},{12,8},{1,5},{9,13},{5,1},{13,9},{2,6},{10,14},... | collective-permute-start | bytes 786440 | tf_op jit(solution)/shard_map/ppermute | solution.py:451
  13.1 0.4 shard_map.52
  13.5 0.5 shard_map.53.refs_0_
  14.0 0.4 collective-permute-done.5.refs_3_
  14.4 2.5 %collective-permute-start.6 = (bf16[2,128,512]{2,1,0:T(8,128)(2,1)S(1)}, bf16[2,128,512]{2,1,0:T(8,128)(2,1)S(1)}, u32[]{:S(2)}, u32[]{:S(2)}) collective-permute-start(bf16[2,128,512]{2,1,0:T(8,128)(2,1)S(1)} %collective-permute-done.5.refs_3_), channel_id=1, source_target_pairs={{2,0},{0,2},{3,1},{1,3},{6,4},{4,6},{7,5},{5,7},{10,8},{8,10},{11,... | collective-permute-start | bytes 786440 | tf_op jit(solution)/shard_map/ppermute | solution.py:16
  16.9 2.6 %collective-permute-done.2.refs_1_.refs_2_ = bf16[512,256]{1,0:T(8,128)(2,1)S(1)} collective-permute-done((bf16[512,256]{1,0:T(8,128)(2,1)S(1)}, bf16[512,256]{1,0:T(8,128)(2,1)S(1)}, u32[]{:S(2)}, u32[]{:S(2)}) %collective-permute-start.2) | collective-permute-done | bytes 262176 | tf_op jit(solution)/shard_map/ppermute | solution.py:451
  19.5 0.4 shard_map.50.refs_1_
  20.0 1.7 %collective-permute-done.6.refs_4_ = bf16[2,128,512]{2,1,0:T(8,128)(2,1)S(1)} collective-permute-done((bf16[2,128,512]{2,1,0:T(8,128)(2,1)S(1)}, bf16[2,128,512]{2,1,0:T(8,128)(2,1)S(1)}, u32[]{:S(2)}, u32[]{:S(2)}) %collective-permute-start.6) | collective-permute-done | bytes 262176 | tf_op jit(solution)/shard_map/ppermute | solution.py:16
  21.6 0.5 collective-permute-start.8
  22.2 1.4 %collective-permute-start.13 = (bf16[512,256]{1,0:T(8,128)(2,1)S(1)}, bf16[512,256]{1,0:T(8,128)(2,1)S(1)}, u32[]{:S(2)}, u32[]{:S(2)}) collective-permute-start(bf16[512,256]{1,0:T(8,128)(2,1)S(1)} %shard_map.53.refs_0_), channel_id=1, source_target_pairs={{0,4},{8,12},{4,0},{12,8},{1,5},{9,13},{5,1},{13,9},{2,6},{10,14},... | collective-permute-start | bytes 786440 | tf_op jit(solution)/shard_map/ppermute | solution.py:451
  23.6 0.9 %shard_map.54 = (f32[512,256]{1,0:T(8,128)S(1)}, bf16[512,256]{1,0:T(8,128)(2,1)S(1)}) custom-call(f32[512,256]{1,0:T(8,128)S(1)} %get-tuple-element.21.refs_0_, bf16[512,256]{1,0:T(8,128)(2,1)S(1)} %shard_map.50.refs_1_, bf16[512,256]{1,0:T(8,128)(2,1)S(1)} %collective-permute-done.2.refs_1_.refs_2_, ...), custom_call_target="tpu_custom_call" | custom-call | flops 805306368 | bytes 6029312 | tf_op jit(solution)/shard_map/pallas_call | solution.py:62
  24.5 0.7 %collective-permute-start.9 = (bf16[512,256]{1,0:T(8,128)(2,1)S(1)}, bf16[512,256]{1,0:T(8,128)(2,1)S(1)}, u32[]{:S(2)}, u32[]{:S(2)}) collective-permute-start(bf16[512,256]{1,0:T(8,128)(2,1)S(1)} %get-tuple-element.31.refs_0_), channel_id=1, source_target_pairs={{4,8},{8,4},{5,9},{9,5},{6,10},{10,6},{7,11},{11,7},{20,24},{24,20... | collective-permute-start | bytes 786440 | tf_op jit(solution)/shard_map/ppermute | solution.py:451
  25.2 5.2 %collective-permute-done.13.refs_1_.refs_2_ = bf16[512,256]{1,0:T(8,128)(2,1)S(1)} collective-permute-done((bf16[512,256]{1,0:T(8,128)(2,1)S(1)}, bf16[512,256]{1,0:T(8,128)(2,1)S(1)}, u32[]{:S(2)}, u32[]{:S(2)}) %collective-permute-start.13) | collective-permute-done | bytes 262176 | tf_op jit(solution)/shard_map/ppermute | solution.py:451
  30.4 0.4 shard_map.57.refs_1_
  30.8 0.9 %shard_map.58 = (f32[512,256]{1,0:T(8,128)S(1)}, bf16[512,256]{1,0:T(8,128)(2,1)S(1)}) custom-call(f32[512,256]{1,0:T(8,128)S(1)} %get-tuple-element.33.refs_0_, bf16[512,256]{1,0:T(8,128)(2,1)S(1)} %shard_map.57.refs_1_, bf16[512,256]{1,0:T(8,128)(2,1)S(1)} %collective-permute-done.13.refs_1_.refs_2_, ...), custom_call_target="tpu_custom_call" | custom-call | flops 805306368 | bytes 6029312 | tf_op jit(solution)/shard_map/pallas_call | solution.py:62
  31.8 0.7 %collective-permute-start.14 = (bf16[512,256]{1,0:T(8,128)(2,1)S(1)}, bf16[512,256]{1,0:T(8,128)(2,1)S(1)}, u32[]{:S(2)}, u32[]{:S(2)}) collective-permute-start(bf16[512,256]{1,0:T(8,128)(2,1)S(1)} %get-tuple-element.36.refs_0_), channel_id=1, source_target_pairs={{4,8},{8,4},{5,9},{9,5},{6,10},{10,6},{7,11},{11,7},{20,24},{24,20... | collective-permute-start | bytes 786440 | tf_op jit(solution)/shard_map/ppermute | solution.py:451
  32.5 1.3 %collective-permute-start.12 = (bf16[512,256]{1,0:T(8,128)(2,1)S(1)}, bf16[512,256]{1,0:T(8,128)(2,1)S(1)}, u32[]{:S(2)}, u32[]{:S(2)}) collective-permute-start(bf16[512,256]{1,0:T(8,128)(2,1)S(1)} %shard_map.55.refs_2_), channel_id=1, source_target_pairs={{8,12},{4,0},{9,13},{5,1},{10,14},{6,2},{11,15},{7,3},{24,28},{20,... | collective-permute-start | bytes 786440 | tf_op jit(solution)/shard_map/ppermute | solution.py:505
  33.8 1.3 %collective-permute-start.15 = (bf16[512,256]{1,0:T(8,128)(2,1)S(1)}, bf16[512,256]{1,0:T(8,128)(2,1)S(1)}, u32[]{:S(2)}, u32[]{:S(2)}) collective-permute-start(bf16[512,256]{1,0:T(8,128)(2,1)S(1)} %shard_map.59.refs_3_), channel_id=1, source_target_pairs={{8,12},{4,0},{9,13},{5,1},{10,14},{6,2},{11,15},{7,3},{24,28},{20,... | collective-permute-start | bytes 786440 | tf_op jit(solution)/shard_map/ppermute | solution.py:505
  35.1 9.9 %collective-permute-done.12.refs_1_ = bf16[512,256]{1,0:T(8,128)(2,1)S(1)} collective-permute-done((bf16[512,256]{1,0:T(8,128)(2,1)S(1)}, bf16[512,256]{1,0:T(8,128)(2,1)S(1)}, u32[]{:S(2)}, u32[]{:S(2)}) %collective-permute-start.12) | collective-permute-done | bytes 262176 | tf_op jit(solution)/shard_map/ppermute | solution.py:505
  45.0 0.5 shard_map.56.refs_0_
  45.5 4.8 %collective-permute-done.15.refs_2_ = bf16[512,256]{1,0:T(8,128)(2,1)S(1)} collective-permute-done((bf16[512,256]{1,0:T(8,128)(2,1)S(1)}, bf16[512,256]{1,0:T(8,128)(2,1)S(1)}, u32[]{:S(2)}, u32[]{:S(2)}) %collective-permute-start.15) | collective-permute-done | bytes 262176 | tf_op jit(solution)/shard_map/ppermute | solution.py:505
  50.2 1.3 %shard_map.60 = f32[2,512,256]{2,1,0:T(8,128)} custom-call(f32[512,256]{1,0:T(8,128)S(1)} %shard_map.56.refs_0_, f32[512,256]{1,0:T(8,128)S(1)} %get-tuple-element.35.refs_1_, bf16[512,256]{1,0:T(8,128)(2,1)S(1)} %collective-permute-done.15.refs_2_, bf16[512,256]{1,0:T(8,128)(2,1)S(1)} %shard_map.59.refs_3_, ...), custom_call_target="tpu_custom_call" | custom-call | flops 268435456 | bytes 1572864 | tf_op jit(solution)/shard_map/pallas_call | solution.py:433
  (23 shorter events, 0.4 us)
Async XLA Ops:
  0.0 3.4 %collective-permute-start.3 = (bf16[2,2,256,512]{3,2,1,0:T(8,128)(2,1)}, bf16[2,2,256,512]{3,2,1,0:T(8,128)(2,1)S(1)}, u32[]{:S(2)}, u32[]{:S(2)}) collective-permute-start(bf16[2,2,256,512]{3,2,1,0:T(8,128)(2,1)} %bitcast.12), channel_id=1, source_target_pairs={{1,0},{0,1},{3,2},{2,3},{5,4},{4,5},{7,6},{6,7},{9,8},{8,9},{11,10... | collective-permute-start | bytes 3145736 | tf_op jit(solution)/shard_map/ppermute | solution.py:16
  0.5 7.6 %collective-permute-start = (bf16[2,256,512]{2,1,0:T(8,128)(2,1)}, bf16[2,256,512]{2,1,0:T(8,128)(2,1)S(1)}, u32[]{:S(2)}, u32[]{:S(2)}) collective-permute-start(bf16[2,256,512]{2,1,0:T(8,128)(2,1)} %bitcast.7), channel_id=1, source_target_pairs={{1,0},{0,1},{3,2},{2,3},{5,4},{4,5},{7,6},{6,7},{9,8},{8,9},{11,10... | collective-permute-start | bytes 1572872 | tf_op jit(solution)/shard_map/ppermute | solution.py:16
  0.5 8.1 %collective-permute-start.1 = (bf16[2,256,512]{2,1,0:T(8,128)(2,1)}, bf16[2,256,512]{2,1,0:T(8,128)(2,1)S(1)}, u32[]{:S(2)}, u32[]{:S(2)}) collective-permute-start(bf16[2,256,512]{2,1,0:T(8,128)(2,1)} %bitcast.14), channel_id=1, source_target_pairs={{1,0},{0,1},{3,2},{2,3},{5,4},{4,5},{7,6},{6,7},{9,8},{8,9},{11,10... | collective-permute-start | bytes 1572872 | tf_op jit(solution)/shard_map/ppermute | solution.py:16
  1.0 1.2 %copy-start.2 = (bf16[2,1,2,256,512]{4,3,2,1,0:T(8,128)(2,1)S(1)}, bf16[2,1,2,256,512]{4,3,2,1,0:T(8,128)(2,1)}, u32[]{:S(2)}) copy-start(bf16[2,1,2,256,512]{4,3,2,1,0:T(8,128)(2,1)} %param.6) | copy-start | bytes 3145732
  2.2 1.0 %copy-start.3 = (bf16[2,1,256,512]{3,2,1,0:T(8,128)(2,1)S(1)}, bf16[2,1,256,512]{3,2,1,0:T(8,128)(2,1)}, u32[]{:S(2)}) copy-start(bf16[2,1,256,512]{3,2,1,0:T(8,128)(2,1)} %param.7) | copy-start | bytes 1572868
  4.1 4.0 %copy-start = (bf16[2,1,256,512]{3,2,1,0:T(8,128)(2,1)S(1)}, bf16[2,1,256,512]{3,2,1,0:T(8,128)(2,1)}, u32[]{:S(2)}) copy-start(bf16[2,1,256,512]{3,2,1,0:T(8,128)(2,1)} %param.5) | copy-start | bytes 1572868
  4.2 4.0 %copy-start.1 = (bf16[2,1,512,256]{3,2,1,0:T(8,128)(2,1)S(1)}, bf16[2,1,512,256]{3,2,1,0:T(8,128)(2,1)}, u32[]{:S(2)}) copy-start(bf16[2,1,512,256]{3,2,1,0:T(8,128)(2,1)} %param.4) | copy-start | bytes 1572868
  4.2 15.4 %collective-permute-start.4 = (bf16[2,256,512]{2,1,0:T(8,128)(2,1)S(1)}, bf16[2,256,512]{2,1,0:T(8,128)(2,1)S(1)}, u32[]{:S(2)}, u32[]{:S(2)}) collective-permute-start(bf16[2,256,512]{2,1,0:T(8,128)(2,1)S(1)} %get-tuple-element.25.refs_2_.refs_4_), channel_id=1, source_target_pairs={{1,0},{0,1},{3,2},{2,3},{5,4},{4,5},{7,6},{6,7},{9,8},{8,9},{11,10... | collective-permute-start | bytes 1572872 | tf_op jit(solution)/shard_map/ppermute | solution.py:16
  4.7 9.6 %collective-permute-start.5 = (bf16[2,128,512]{2,1,0:T(8,128)(2,1)S(1)}, bf16[2,128,512]{2,1,0:T(8,128)(2,1)S(1)}, u32[]{:S(2)}, u32[]{:S(2)}) collective-permute-start(bf16[2,128,512]{2,1,0:T(8,128)(2,1)S(1)} %shard_map.51), channel_id=1, source_target_pairs={{0,4},{8,12},{4,0},{12,8},{1,5},{9,13},{5,1},{13,9},{2,6},{10,14},... | collective-permute-start | bytes 786440 | tf_op jit(solution)/shard_map/ppermute | solution.py:451
  7.4 16.2 %collective-permute-start.10 = (bf16[2,256,512]{2,1,0:T(8,128)(2,1)S(1)}, bf16[2,256,512]{2,1,0:T(8,128)(2,1)S(1)}, u32[]{:S(2)}, u32[]{:S(2)}) collective-permute-start(bf16[2,256,512]{2,1,0:T(8,128)(2,1)S(1)} %get-tuple-element.32), channel_id=1, source_target_pairs={{4,8},{8,4},{5,9},{9,5},{6,10},{10,6},{7,11},{11,7},{20,24},{24,20... | collective-permute-start | bytes 1572872 | tf_op jit(solution)/shard_map/ppermute | solution.py:451
  9.0 10.5 %collective-permute-start.2 = (bf16[512,256]{1,0:T(8,128)(2,1)S(1)}, bf16[512,256]{1,0:T(8,128)(2,1)S(1)}, u32[]{:S(2)}, u32[]{:S(2)}) collective-permute-start(bf16[512,256]{1,0:T(8,128)(2,1)S(1)} %shard_map.48.refs_0_), channel_id=1, source_target_pairs={{0,4},{8,12},{4,0},{12,8},{1,5},{9,13},{5,1},{13,9},{2,6},{10,14},... | collective-permute-start | bytes 786440 | tf_op jit(solution)/shard_map/ppermute | solution.py:451
  14.4 7.3 %collective-permute-start.6 = (bf16[2,128,512]{2,1,0:T(8,128)(2,1)S(1)}, bf16[2,128,512]{2,1,0:T(8,128)(2,1)S(1)}, u32[]{:S(2)}, u32[]{:S(2)}) collective-permute-start(bf16[2,128,512]{2,1,0:T(8,128)(2,1)S(1)} %collective-permute-done.5.refs_3_), channel_id=1, source_target_pairs={{2,0},{0,2},{3,1},{1,3},{6,4},{4,6},{7,5},{5,7},{10,8},{8,10},{11,... | collective-permute-start | bytes 786440 | tf_op jit(solution)/shard_map/ppermute | solution.py:16
  21.6 1.9 %collective-permute-start.7 = (bf16[2,128,512]{2,1,0:T(8,128)(2,1)S(1)}, bf16[2,128,512]{2,1,0:T(8,128)(2,1)S(1)}, u32[]{:S(2)}, u32[]{:S(2)}) collective-permute-start(bf16[2,128,512]{2,1,0:T(8,128)(2,1)S(1)} %collective-permute-done.5.refs_3_), channel_id=1, source_target_pairs={{1,0},{0,1},{3,2},{2,3},{5,4},{4,5},{7,6},{6,7},{9,8},{8,9},{11,10... | collective-permute-start | bytes 786440 | tf_op jit(solution)/shard_map/ppermute | solution.py:16
  21.6 1.9 %collective-permute-start.8 = (bf16[2,128,512]{2,1,0:T(8,128)(2,1)S(1)}, bf16[2,128,512]{2,1,0:T(8,128)(2,1)S(1)}, u32[]{:S(2)}, u32[]{:S(2)}) collective-permute-start(bf16[2,128,512]{2,1,0:T(8,128)(2,1)S(1)} %collective-permute-done.6.refs_4_), channel_id=1, source_target_pairs={{1,0},{0,1},{3,2},{2,3},{5,4},{4,5},{7,6},{6,7},{9,8},{8,9},{11,10... | collective-permute-start | bytes 786440 | tf_op jit(solution)/shard_map/ppermute | solution.py:16
  22.2 8.2 %collective-permute-start.13 = (bf16[512,256]{1,0:T(8,128)(2,1)S(1)}, bf16[512,256]{1,0:T(8,128)(2,1)S(1)}, u32[]{:S(2)}, u32[]{:S(2)}) collective-permute-start(bf16[512,256]{1,0:T(8,128)(2,1)S(1)} %shard_map.53.refs_0_), channel_id=1, source_target_pairs={{0,4},{8,12},{4,0},{12,8},{1,5},{9,13},{5,1},{13,9},{2,6},{10,14},... | collective-permute-start | bytes 786440 | tf_op jit(solution)/shard_map/ppermute | solution.py:451
  23.6 8.9 %collective-permute-start.11 = (bf16[2,256,512]{2,1,0:T(8,128)(2,1)S(1)}, bf16[2,256,512]{2,1,0:T(8,128)(2,1)S(1)}, u32[]{:S(2)}, u32[]{:S(2)}) collective-permute-start(bf16[2,256,512]{2,1,0:T(8,128)(2,1)S(1)} %collective-permute-done.10.refs_2_), channel_id=1, source_target_pairs={{1,0},{0,1},{3,2},{2,3},{5,4},{4,5},{7,6},{6,7},{9,8},{8,9},{11,10... | collective-permute-start | bytes 1572872 | tf_op jit(solution)/shard_map/ppermute | solution.py:16
  24.5 7.9 %collective-permute-start.9 = (bf16[512,256]{1,0:T(8,128)(2,1)S(1)}, bf16[512,256]{1,0:T(8,128)(2,1)S(1)}, u32[]{:S(2)}, u32[]{:S(2)}) collective-permute-start(bf16[512,256]{1,0:T(8,128)(2,1)S(1)} %get-tuple-element.31.refs_0_), channel_id=1, source_target_pairs={{4,8},{8,4},{5,9},{9,5},{6,10},{10,6},{7,11},{11,7},{20,24},{24,20... | collective-permute-start | bytes 786440 | tf_op jit(solution)/shard_map/ppermute | solution.py:451
  31.8 2.0 %collective-permute-start.14 = (bf16[512,256]{1,0:T(8,128)(2,1)S(1)}, bf16[512,256]{1,0:T(8,128)(2,1)S(1)}, u32[]{:S(2)}, u32[]{:S(2)}) collective-permute-start(bf16[512,256]{1,0:T(8,128)(2,1)S(1)} %get-tuple-element.36.refs_0_), channel_id=1, source_target_pairs={{4,8},{8,4},{5,9},{9,5},{6,10},{10,6},{7,11},{11,7},{20,24},{24,20... | collective-permute-start | bytes 786440 | tf_op jit(solution)/shard_map/ppermute | solution.py:451
  32.5 12.5 %collective-permute-start.12 = (bf16[512,256]{1,0:T(8,128)(2,1)S(1)}, bf16[512,256]{1,0:T(8,128)(2,1)S(1)}, u32[]{:S(2)}, u32[]{:S(2)}) collective-permute-start(bf16[512,256]{1,0:T(8,128)(2,1)S(1)} %shard_map.55.refs_2_), channel_id=1, source_target_pairs={{8,12},{4,0},{9,13},{5,1},{10,14},{6,2},{11,15},{7,3},{24,28},{20,... | collective-permute-start | bytes 786440 | tf_op jit(solution)/shard_map/ppermute | solution.py:505
  33.8 16.4 %collective-permute-start.15 = (bf16[512,256]{1,0:T(8,128)(2,1)S(1)}, bf16[512,256]{1,0:T(8,128)(2,1)S(1)}, u32[]{:S(2)}, u32[]{:S(2)}) collective-permute-start(bf16[512,256]{1,0:T(8,128)(2,1)S(1)} %shard_map.59.refs_3_), channel_id=1, source_target_pairs={{8,12},{4,0},{9,13},{5,1},{10,14},{6,2},{11,15},{7,3},{24,28},{20,... | collective-permute-start | bytes 786440 | tf_op jit(solution)/shard_map/ppermute | solution.py:505

commit v6 on v5

--- a/solution.py
+++ b/solution.py
@@ -439,6 +439,66 @@
             pltpu.VMEM((height, width), jnp.bfloat16),
             pltpu.VMEM((2, height, columns), jnp.float32),
             pltpu.SemaphoreType.DMA((2,)),
+        ],
+        compiler_params=pltpu.CompilerParams(vmem_limit_bytes=24 * 2**20),
+        cost_estimate=pl.CostEstimate(
+            flops=product_flops(height, width), bytes_accessed=12 * height * columns, transcendentals=0
+        ),
+    )(*done, state, new_tip, tip, *spikes)
+
+
+def last_update_aligned(use_new, done, state, new_tip, tip, spikes, level):
+    height, width = state.shape
+    n, k = len(spikes), len(done)
+    own = width // 2
+    before = sum(d.shape[1] // 2 for d in done)
+    columns = before + own
+
+    def body(*refs):
+        done_refs = refs[:k]
+        state_ref, new_ref, tip_ref = refs[k : k + 3]
+        spike_refs = refs[k + 3 : k + 3 + n]
+        out, source, whole, sems = refs[k + 3 + n :]
+
+        copies = []
+        first = 0
+        for c, d in enumerate(done_refs):
+            w = d.shape[1] // 2
+            for p in range(2):
+                part = pltpu.make_async_copy(
+                    d.at[:, pl.ds(p * w, w)], out.at[p, :, pl.ds(first, w)], sems.at[2 * c + p]
+                )
+                part.start()
+                copies.append(part)
+            first += w
+
+        @pl.when(use_new())
+        def _():
+            source[...] = new_ref[...]
+
+        @pl.when(jnp.logical_not(use_new()))
+        def _():
+            source[...] = tip_ref[...]
+
+        starts = row_starts(height, n, 1)
+        for rows, value in each_product(at_level(spike_refs, level), starts, source[...]):
+            new = state_ref[rows, :] - value
+            whole[0, rows, :] = new[:, :own]
+            whole[1, rows, :] = new[:, own:]
+        copies.append(pltpu.make_async_copy(whole, out.at[:, :, pl.ds(before, own)], sems.at[2 * k]))
+        copies[-1].start()
+        for copy in copies:
+            copy.wait()
+
+    return pl.pallas_call(
+        body,
+        out_shape=jax.ShapeDtypeStruct((2, height, columns), jnp.float32),
+        in_specs=[VMEM] * (k + 3 + n),
+        out_specs=pl.BlockSpec(memory_space=pl.ANY),
+        scratch_shapes=[
+            pltpu.VMEM((height, width), jnp.bfloat16),
+            pltpu.VMEM((2, height, own), jnp.float32),
+            pltpu.SemaphoreType.DMA((2 * k + 1,)),
         ],
         compiler_params=pltpu.CompilerParams(vmem_limit_bytes=24 * 2**20),
         cost_estimate=pl.CostEstimate(
@@ -518,7 +578,8 @@
         for c in chunks[:-1]:
             (states[c],) = tip_update(is_new, states[c], moved[c], tips[c], spike_all, level)
         c = chunks[-1]
-        whole = last_update(is_new, states[:c], states[c], moved[c], tips[c], spike_all, level)
+        aligned = all(w % 128 == 0 for w in widths)
+        whole = (last_update_aligned if aligned else last_update)(is_new, states[:c], states[c], moved[c], tips[c], spike_all, level)
     return whole[:, None]
 
 

time: 51.8 us -> 51.8 us (level)
  no operation moved by 1% of the time
where the time goes in v6:
time: 51.8 us; the launch traced here: 51.5 us
  waiting for transfers between devices  24.5 us (47%)
  starting transfers between devices  16.8 us (32%)
  Pallas kernels  7.64 us (15%)
  local copies, waits for them, and re-layouts  2.28 us (4%)
    ppermute x2, waiting for transfers between devices, per_device(): moved = [lax.ppermute(tips[c], 'slab', route) for c in chunks]  14.6 us
    ppermute x6, starting transfers between devices, swap(): return lax.ppermute(block, 'slab', pairs + [(b, a) for a, b in pairs])  10.1 us
    ppermute x6, waiting for transfers between devices, swap(): return lax.ppermute(block, 'slab', pairs + [(b, a) for a, b in pairs])  8.18 us
    pallas_call x13, Pallas kernels, call(): pl.pallas_call(body, out_shape=outs, in_specs=[VMEM] * len(args), out_spe...  6.23 us
    ppermute x8, starting transfers between devices, ring_gather(): lax.ppermute(block, axis, [((i + step) % count, i) for i in range(count)])  4.14 us
    ppermute x2, starting transfers between devices, per_device(): moved = [lax.ppermute(tips[c], 'slab', route) for c in chunks]  2.58 us
    unnamed x8, local copies, waits for them, and re-layouts  2.28 us
    ppermute x8, waiting for transfers between devices, ring_gather(): lax.ppermute(block, axis, [((i + step) % count, i) for i in range(count)])  1.68 us
  transfers between devices with their start and end apart: 16, of which 6 were waited for; matrix products, arithmetic and copies ran while one was open for 0% of the time, Pallas kernels for 12%

profile of v6, /device:TPU:0, one launch (start us, length us, event | category | flops | bytes accessed | tf_op | source)
XLA Modules:
  0.0 51.5 jit_solution(3712773452112436369)
XLA Ops:
  0.0 0.5 collective-permute-start.3
  0.5 0.5 collective-permute-start.1
  1.0 1.2 %copy-done.2 = bf16[2,1,2,256,512]{4,3,2,1,0:T(8,128)(2,1)S(1)} copy-done((bf16[2,1,2,256,512]{4,3,2,1,0:T(8,128)(2,1)S(1)}, bf16[2,1,2,256,512]{4,3,2,1,0:T(8,128)(2,1)}, u32[]{:S(2)}) %copy-start.2) | copy-done | bytes 1048600
  2.2 1.0 %copy-done.3 = bf16[2,1,256,512]{3,2,1,0:T(8,128)(2,1)S(1)} copy-done((bf16[2,1,256,512]{3,2,1,0:T(8,128)(2,1)S(1)}, bf16[2,1,256,512]{3,2,1,0:T(8,128)(2,1)}, u32[]{:S(2)}) %copy-start.3) | copy-done | bytes 524312
  3.4 0.8 %shard_map.49 = (bf16[2,256,512]{2,1,0:T(8,128)(2,1)S(1)}, bf16[2,256,512]{2,1,0:T(8,128)(2,1)S(1)}) custom-call(bf16[2,2,256,512]{3,2,1,0:T(8,128)(2,1)S(1)} %get-tuple-element.24.refs_0_.refs_7_.refs_3_.refs_4_, bf16[2,2,256,512]{3,2,1,0:T(8,128)(2,1)S(1)} %collective-permute-done.3.refs_1_.refs_8_.refs_4_.refs_5_, ...), custom_call_target="tpu_custom_call" | custom-call | flops 536870912 | bytes 3670016 | tf_op jit(solution)/shard_map/pallas_call | solution.py:62
  4.3 0.5 shard_map.51
  4.7 2.7 %collective-permute-start.5 = (bf16[2,128,512]{2,1,0:T(8,128)(2,1)S(1)}, bf16[2,128,512]{2,1,0:T(8,128)(2,1)S(1)}, u32[]{:S(2)}, u32[]{:S(2)}) collective-permute-start(bf16[2,128,512]{2,1,0:T(8,128)(2,1)S(1)} %shard_map.51), channel_id=1, source_target_pairs={{0,4},{8,12},{4,0},{12,8},{1,5},{9,13},{5,1},{13,9},{2,6},{10,14},... | collective-permute-start | bytes 786440 | tf_op jit(solution)/shard_map/ppermute | solution.py:511
  7.4 0.7 %collective-permute-start.10 = (bf16[2,256,512]{2,1,0:T(8,128)(2,1)S(1)}, bf16[2,256,512]{2,1,0:T(8,128)(2,1)S(1)}, u32[]{:S(2)}, u32[]{:S(2)}) collective-permute-start(bf16[2,256,512]{2,1,0:T(8,128)(2,1)S(1)} %get-tuple-element.32), channel_id=1, source_target_pairs={{4,8},{8,4},{5,9},{9,5},{6,10},{10,6},{7,11},{11,7},{20,24},{24,20... | collective-permute-start | bytes 1572872 | tf_op jit(solution)/shard_map/ppermute | solution.py:511
  8.1 0.4 shard_map.46
  8.6 0.5 shard_map.48.refs_0_
  9.0 4.0 %collective-permute-start.2 = (bf16[512,256]{1,0:T(8,128)(2,1)S(1)}, bf16[512,256]{1,0:T(8,128)(2,1)S(1)}, u32[]{:S(2)}, u32[]{:S(2)}) collective-permute-start(bf16[512,256]{1,0:T(8,128)(2,1)S(1)} %shard_map.48.refs_0_), channel_id=1, source_target_pairs={{0,4},{8,12},{4,0},{12,8},{1,5},{9,13},{5,1},{13,9},{2,6},{10,14},... | collective-permute-start | bytes 786440 | tf_op jit(solution)/shard_map/ppermute | solution.py:511
  13.1 0.4 shard_map.52
  13.5 0.5 shard_map.53.refs_0_
  14.0 0.4 collective-permute-done.5.refs_3_
  14.4 2.5 %collective-permute-start.6 = (bf16[2,128,512]{2,1,0:T(8,128)(2,1)S(1)}, bf16[2,128,512]{2,1,0:T(8,128)(2,1)S(1)}, u32[]{:S(2)}, u32[]{:S(2)}) collective-permute-start(bf16[2,128,512]{2,1,0:T(8,128)(2,1)S(1)} %collective-permute-done.5.refs_3_), channel_id=1, source_target_pairs={{2,0},{0,2},{3,1},{1,3},{6,4},{4,6},{7,5},{5,7},{10,8},{8,10},{11,... | collective-permute-start | bytes 786440 | tf_op jit(solution)/shard_map/ppermute | solution.py:16
  16.9 2.6 %collective-permute-done.2.refs_1_.refs_2_ = bf16[512,256]{1,0:T(8,128)(2,1)S(1)} collective-permute-done((bf16[512,256]{1,0:T(8,128)(2,1)S(1)}, bf16[512,256]{1,0:T(8,128)(2,1)S(1)}, u32[]{:S(2)}, u32[]{:S(2)}) %collective-permute-start.2) | collective-permute-done | bytes 262176 | tf_op jit(solution)/shard_map/ppermute | solution.py:511
  19.5 0.4 shard_map.50.refs_1_
  20.0 1.7 %collective-permute-done.6.refs_4_ = bf16[2,128,512]{2,1,0:T(8,128)(2,1)S(1)} collective-permute-done((bf16[2,128,512]{2,1,0:T(8,128)(2,1)S(1)}, bf16[2,128,512]{2,1,0:T(8,128)(2,1)S(1)}, u32[]{:S(2)}, u32[]{:S(2)}) %collective-permute-start.6) | collective-permute-done | bytes 262176 | tf_op jit(solution)/shard_map/ppermute | solution.py:16
  21.6 0.5 collective-permute-start.8
  22.2 1.4 %collective-permute-start.13 = (bf16[512,256]{1,0:T(8,128)(2,1)S(1)}, bf16[512,256]{1,0:T(8,128)(2,1)S(1)}, u32[]{:S(2)}, u32[]{:S(2)}) collective-permute-start(bf16[512,256]{1,0:T(8,128)(2,1)S(1)} %shard_map.53.refs_0_), channel_id=1, source_target_pairs={{0,4},{8,12},{4,0},{12,8},{1,5},{9,13},{5,1},{13,9},{2,6},{10,14},... | collective-permute-start | bytes 786440 | tf_op jit(solution)/shard_map/ppermute | solution.py:511
  23.6 0.9 %shard_map.54 = (f32[512,256]{1,0:T(8,128)S(1)}, bf16[512,256]{1,0:T(8,128)(2,1)S(1)}) custom-call(f32[512,256]{1,0:T(8,128)S(1)} %get-tuple-element.21.refs_0_, bf16[512,256]{1,0:T(8,128)(2,1)S(1)} %shard_map.50.refs_1_, bf16[512,256]{1,0:T(8,128)(2,1)S(1)} %collective-permute-done.2.refs_1_.refs_2_, ...), custom_call_target="tpu_custom_call" | custom-call | flops 805306368 | bytes 6029312 | tf_op jit(solution)/shard_map/pallas_call | solution.py:62
  24.5 0.7 %collective-permute-start.9 = (bf16[512,256]{1,0:T(8,128)(2,1)S(1)}, bf16[512,256]{1,0:T(8,128)(2,1)S(1)}, u32[]{:S(2)}, u32[]{:S(2)}) collective-permute-start(bf16[512,256]{1,0:T(8,128)(2,1)S(1)} %get-tuple-element.31.refs_0_), channel_id=1, source_target_pairs={{4,8},{8,4},{5,9},{9,5},{6,10},{10,6},{7,11},{11,7},{20,24},{24,20... | collective-permute-start | bytes 786440 | tf_op jit(solution)/shard_map/ppermute | solution.py:511
  25.2 5.2 %collective-permute-done.13.refs_1_.refs_2_ = bf16[512,256]{1,0:T(8,128)(2,1)S(1)} collective-permute-done((bf16[512,256]{1,0:T(8,128)(2,1)S(1)}, bf16[512,256]{1,0:T(8,128)(2,1)S(1)}, u32[]{:S(2)}, u32[]{:S(2)}) %collective-permute-start.13) | collective-permute-done | bytes 262176 | tf_op jit(solution)/shard_map/ppermute | solution.py:511
  30.4 0.4 shard_map.57.refs_1_
  30.8 0.9 %shard_map.58 = (f32[512,256]{1,0:T(8,128)S(1)}, bf16[512,256]{1,0:T(8,128)(2,1)S(1)}) custom-call(f32[512,256]{1,0:T(8,128)S(1)} %get-tuple-element.33.refs_0_, bf16[512,256]{1,0:T(8,128)(2,1)S(1)} %shard_map.57.refs_1_, bf16[512,256]{1,0:T(8,128)(2,1)S(1)} %collective-permute-done.13.refs_1_.refs_2_, ...), custom_call_target="tpu_custom_call" | custom-call | flops 805306368 | bytes 6029312 | tf_op jit(solution)/shard_map/pallas_call | solution.py:62
  31.8 0.7 %collective-permute-start.14 = (bf16[512,256]{1,0:T(8,128)(2,1)S(1)}, bf16[512,256]{1,0:T(8,128)(2,1)S(1)}, u32[]{:S(2)}, u32[]{:S(2)}) collective-permute-start(bf16[512,256]{1,0:T(8,128)(2,1)S(1)} %get-tuple-element.36.refs_0_), channel_id=1, source_target_pairs={{4,8},{8,4},{5,9},{9,5},{6,10},{10,6},{7,11},{11,7},{20,24},{24,20... | collective-permute-start | bytes 786440 | tf_op jit(solution)/shard_map/ppermute | solution.py:511
  32.5 1.3 %collective-permute-start.12 = (bf16[512,256]{1,0:T(8,128)(2,1)S(1)}, bf16[512,256]{1,0:T(8,128)(2,1)S(1)}, u32[]{:S(2)}, u32[]{:S(2)}) collective-permute-start(bf16[512,256]{1,0:T(8,128)(2,1)S(1)} %shard_map.55.refs_2_), channel_id=1, source_target_pairs={{8,12},{4,0},{9,13},{5,1},{10,14},{6,2},{11,15},{7,3},{24,28},{20,... | collective-permute-start | bytes 786440 | tf_op jit(solution)/shard_map/ppermute | solution.py:565
  33.8 1.3 %collective-permute-start.15 = (bf16[512,256]{1,0:T(8,128)(2,1)S(1)}, bf16[512,256]{1,0:T(8,128)(2,1)S(1)}, u32[]{:S(2)}, u32[]{:S(2)}) collective-permute-start(bf16[512,256]{1,0:T(8,128)(2,1)S(1)} %shard_map.59.refs_3_), channel_id=1, source_target_pairs={{8,12},{4,0},{9,13},{5,1},{10,14},{6,2},{11,15},{7,3},{24,28},{20,... | collective-permute-start | bytes 786440 | tf_op jit(solution)/shard_map/ppermute | solution.py:565
  35.1 9.9 %collective-permute-done.12.refs_1_ = bf16[512,256]{1,0:T(8,128)(2,1)S(1)} collective-permute-done((bf16[512,256]{1,0:T(8,128)(2,1)S(1)}, bf16[512,256]{1,0:T(8,128)(2,1)S(1)}, u32[]{:S(2)}, u32[]{:S(2)}) %collective-permute-start.12) | collective-permute-done | bytes 262176 | tf_op jit(solution)/shard_map/ppermute | solution.py:565
  45.0 0.5 shard_map.56.refs_0_
  45.5 4.8 %collective-permute-done.15.refs_2_ = bf16[512,256]{1,0:T(8,128)(2,1)S(1)} collective-permute-done((bf16[512,256]{1,0:T(8,128)(2,1)S(1)}, bf16[512,256]{1,0:T(8,128)(2,1)S(1)}, u32[]{:S(2)}, u32[]{:S(2)}) %collective-permute-start.15) | collective-permute-done | bytes 262176 | tf_op jit(solution)/shard_map/ppermute | solution.py:565
  50.2 1.3 %shard_map.60 = f32[2,512,256]{2,1,0:T(8,128)} custom-call(f32[512,256]{1,0:T(8,128)S(1)} %shard_map.56.refs_0_, f32[512,256]{1,0:T(8,128)S(1)} %get-tuple-element.35.refs_1_, bf16[512,256]{1,0:T(8,128)(2,1)S(1)} %collective-permute-done.15.refs_2_, bf16[512,256]{1,0:T(8,128)(2,1)S(1)} %shard_map.59.refs_3_, ...), custom_call_target="tpu_custom_call" | custom-call | flops 268435456 | bytes 1572864 | tf_op jit(solution)/shard_map/pallas_call | solution.py:493
  (23 shorter events, 0.4 us)
Async XLA Ops:
  0.0 3.4 %collective-permute-start.3 = (bf16[2,2,256,512]{3,2,1,0:T(8,128)(2,1)}, bf16[2,2,256,512]{3,2,1,0:T(8,128)(2,1)S(1)}, u32[]{:S(2)}, u32[]{:S(2)}) collective-permute-start(bf16[2,2,256,512]{3,2,1,0:T(8,128)(2,1)} %bitcast.12), channel_id=1, source_target_pairs={{1,0},{0,1},{3,2},{2,3},{5,4},{4,5},{7,6},{6,7},{9,8},{8,9},{11,10... | collective-permute-start | bytes 3145736 | tf_op jit(solution)/shard_map/ppermute | solution.py:16
  0.5 7.6 %collective-permute-start = (bf16[2,256,512]{2,1,0:T(8,128)(2,1)}, bf16[2,256,512]{2,1,0:T(8,128)(2,1)S(1)}, u32[]{:S(2)}, u32[]{:S(2)}) collective-permute-start(bf16[2,256,512]{2,1,0:T(8,128)(2,1)} %bitcast.7), channel_id=1, source_target_pairs={{1,0},{0,1},{3,2},{2,3},{5,4},{4,5},{7,6},{6,7},{9,8},{8,9},{11,10... | collective-permute-start | bytes 1572872 | tf_op jit(solution)/shard_map/ppermute | solution.py:16
  0.5 8.1 %collective-permute-start.1 = (bf16[2,256,512]{2,1,0:T(8,128)(2,1)}, bf16[2,256,512]{2,1,0:T(8,128)(2,1)S(1)}, u32[]{:S(2)}, u32[]{:S(2)}) collective-permute-start(bf16[2,256,512]{2,1,0:T(8,128)(2,1)} %bitcast.14), channel_id=1, source_target_pairs={{1,0},{0,1},{3,2},{2,3},{5,4},{4,5},{7,6},{6,7},{9,8},{8,9},{11,10... | collective-permute-start | bytes 1572872 | tf_op jit(solution)/shard_map/ppermute | solution.py:16
  1.0 1.2 %copy-start.2 = (bf16[2,1,2,256,512]{4,3,2,1,0:T(8,128)(2,1)S(1)}, bf16[2,1,2,256,512]{4,3,2,1,0:T(8,128)(2,1)}, u32[]{:S(2)}) copy-start(bf16[2,1,2,256,512]{4,3,2,1,0:T(8,128)(2,1)} %param.6) | copy-start | bytes 3145732
  2.2 1.0 %copy-start.3 = (bf16[2,1,256,512]{3,2,1,0:T(8,128)(2,1)S(1)}, bf16[2,1,256,512]{3,2,1,0:T(8,128)(2,1)}, u32[]{:S(2)}) copy-start(bf16[2,1,256,512]{3,2,1,0:T(8,128)(2,1)} %param.7) | copy-start | bytes 1572868
  4.1 4.0 %copy-start = (bf16[2,1,256,512]{3,2,1,0:T(8,128)(2,1)S(1)}, bf16[2,1,256,512]{3,2,1,0:T(8,128)(2,1)}, u32[]{:S(2)}) copy-start(bf16[2,1,256,512]{3,2,1,0:T(8,128)(2,1)} %param.5) | copy-start | bytes 1572868
  4.2 4.0 %copy-start.1 = (bf16[2,1,512,256]{3,2,1,0:T(8,128)(2,1)S(1)}, bf16[2,1,512,256]{3,2,1,0:T(8,128)(2,1)}, u32[]{:S(2)}) copy-start(bf16[2,1,512,256]{3,2,1,0:T(8,128)(2,1)} %param.4) | copy-start | bytes 1572868
  4.2 15.4 %collective-permute-start.4 = (bf16[2,256,512]{2,1,0:T(8,128)(2,1)S(1)}, bf16[2,256,512]{2,1,0:T(8,128)(2,1)S(1)}, u32[]{:S(2)}, u32[]{:S(2)}) collective-permute-start(bf16[2,256,512]{2,1,0:T(8,128)(2,1)S(1)} %get-tuple-element.25.refs_2_.refs_4_), channel_id=1, source_target_pairs={{1,0},{0,1},{3,2},{2,3},{5,4},{4,5},{7,6},{6,7},{9,8},{8,9},{11,10... | collective-permute-start | bytes 1572872 | tf_op jit(solution)/shard_map/ppermute | solution.py:16
  4.7 9.6 %collective-permute-start.5 = (bf16[2,128,512]{2,1,0:T(8,128)(2,1)S(1)}, bf16[2,128,512]{2,1,0:T(8,128)(2,1)S(1)}, u32[]{:S(2)}, u32[]{:S(2)}) collective-permute-start(bf16[2,128,512]{2,1,0:T(8,128)(2,1)S(1)} %shard_map.51), channel_id=1, source_target_pairs={{0,4},{8,12},{4,0},{12,8},{1,5},{9,13},{5,1},{13,9},{2,6},{10,14},... | collective-permute-start | bytes 786440 | tf_op jit(solution)/shard_map/ppermute | solution.py:511
  7.4 16.2 %collective-permute-start.10 = (bf16[2,256,512]{2,1,0:T(8,128)(2,1)S(1)}, bf16[2,256,512]{2,1,0:T(8,128)(2,1)S(1)}, u32[]{:S(2)}, u32[]{:S(2)}) collective-permute-start(bf16[2,256,512]{2,1,0:T(8,128)(2,1)S(1)} %get-tuple-element.32), channel_id=1, source_target_pairs={{4,8},{8,4},{5,9},{9,5},{6,10},{10,6},{7,11},{11,7},{20,24},{24,20... | collective-permute-start | bytes 1572872 | tf_op jit(solution)/shard_map/ppermute | solution.py:511
  9.0 10.5 %collective-permute-start.2 = (bf16[512,256]{1,0:T(8,128)(2,1)S(1)}, bf16[512,256]{1,0:T(8,128)(2,1)S(1)}, u32[]{:S(2)}, u32[]{:S(2)}) collective-permute-start(bf16[512,256]{1,0:T(8,128)(2,1)S(1)} %shard_map.48.refs_0_), channel_id=1, source_target_pairs={{0,4},{8,12},{4,0},{12,8},{1,5},{9,13},{5,1},{13,9},{2,6},{10,14},... | collective-permute-start | bytes 786440 | tf_op jit(solution)/shard_map/ppermute | solution.py:511
  14.4 7.3 %collective-permute-start.6 = (bf16[2,128,512]{2,1,0:T(8,128)(2,1)S(1)}, bf16[2,128,512]{2,1,0:T(8,128)(2,1)S(1)}, u32[]{:S(2)}, u32[]{:S(2)}) collective-permute-start(bf16[2,128,512]{2,1,0:T(8,128)(2,1)S(1)} %collective-permute-done.5.refs_3_), channel_id=1, source_target_pairs={{2,0},{0,2},{3,1},{1,3},{6,4},{4,6},{7,5},{5,7},{10,8},{8,10},{11,... | collective-permute-start | bytes 786440 | tf_op jit(solution)/shard_map/ppermute | solution.py:16
  21.6 1.9 %collective-permute-start.7 = (bf16[2,128,512]{2,1,0:T(8,128)(2,1)S(1)}, bf16[2,128,512]{2,1,0:T(8,128)(2,1)S(1)}, u32[]{:S(2)}, u32[]{:S(2)}) collective-permute-start(bf16[2,128,512]{2,1,0:T(8,128)(2,1)S(1)} %collective-permute-done.5.refs_3_), channel_id=1, source_target_pairs={{1,0},{0,1},{3,2},{2,3},{5,4},{4,5},{7,6},{6,7},{9,8},{8,9},{11,10... | collective-permute-start | bytes 786440 | tf_op jit(solution)/shard_map/ppermute | solution.py:16
  21.6 1.9 %collective-permute-start.8 = (bf16[2,128,512]{2,1,0:T(8,128)(2,1)S(1)}, bf16[2,128,512]{2,1,0:T(8,128)(2,1)S(1)}, u32[]{:S(2)}, u32[]{:S(2)}) collective-permute-start(bf16[2,128,512]{2,1,0:T(8,128)(2,1)S(1)} %collective-permute-done.6.refs_4_), channel_id=1, source_target_pairs={{1,0},{0,1},{3,2},{2,3},{5,4},{4,5},{7,6},{6,7},{9,8},{8,9},{11,10... | collective-permute-start | bytes 786440 | tf_op jit(solution)/shard_map/ppermute | solution.py:16
  22.2 8.2 %collective-permute-start.13 = (bf16[512,256]{1,0:T(8,128)(2,1)S(1)}, bf16[512,256]{1,0:T(8,128)(2,1)S(1)}, u32[]{:S(2)}, u32[]{:S(2)}) collective-permute-start(bf16[512,256]{1,0:T(8,128)(2,1)S(1)} %shard_map.53.refs_0_), channel_id=1, source_target_pairs={{0,4},{8,12},{4,0},{12,8},{1,5},{9,13},{5,1},{13,9},{2,6},{10,14},... | collective-permute-start | bytes 786440 | tf_op jit(solution)/shard_map/ppermute | solution.py:511
  23.6 8.9 %collective-permute-start.11 = (bf16[2,256,512]{2,1,0:T(8,128)(2,1)S(1)}, bf16[2,256,512]{2,1,0:T(8,128)(2,1)S(1)}, u32[]{:S(2)}, u32[]{:S(2)}) collective-permute-start(bf16[2,256,512]{2,1,0:T(8,128)(2,1)S(1)} %collective-permute-done.10.refs_2_), channel_id=1, source_target_pairs={{1,0},{0,1},{3,2},{2,3},{5,4},{4,5},{7,6},{6,7},{9,8},{8,9},{11,10... | collective-permute-start | bytes 1572872 | tf_op jit(solution)/shard_map/ppermute | solution.py:16
  24.5 7.9 %collective-permute-start.9 = (bf16[512,256]{1,0:T(8,128)(2,1)S(1)}, bf16[512,256]{1,0:T(8,128)(2,1)S(1)}, u32[]{:S(2)}, u32[]{:S(2)}) collective-permute-start(bf16[512,256]{1,0:T(8,128)(2,1)S(1)} %get-tuple-element.31.refs_0_), channel_id=1, source_target_pairs={{4,8},{8,4},{5,9},{9,5},{6,10},{10,6},{7,11},{11,7},{20,24},{24,20... | collective-permute-start | bytes 786440 | tf_op jit(solution)/shard_map/ppermute | solution.py:511
  31.8 2.0 %collective-permute-start.14 = (bf16[512,256]{1,0:T(8,128)(2,1)S(1)}, bf16[512,256]{1,0:T(8,128)(2,1)S(1)}, u32[]{:S(2)}, u32[]{:S(2)}) collective-permute-start(bf16[512,256]{1,0:T(8,128)(2,1)S(1)} %get-tuple-element.36.refs_0_), channel_id=1, source_target_pairs={{4,8},{8,4},{5,9},{9,5},{6,10},{10,6},{7,11},{11,7},{20,24},{24,20... | collective-permute-start | bytes 786440 | tf_op jit(solution)/shard_map/ppermute | solution.py:511
  32.5 12.5 %collective-permute-start.12 = (bf16[512,256]{1,0:T(8,128)(2,1)S(1)}, bf16[512,256]{1,0:T(8,128)(2,1)S(1)}, u32[]{:S(2)}, u32[]{:S(2)}) collective-permute-start(bf16[512,256]{1,0:T(8,128)(2,1)S(1)} %shard_map.55.refs_2_), channel_id=1, source_target_pairs={{8,12},{4,0},{9,13},{5,1},{10,14},{6,2},{11,15},{7,3},{24,28},{20,... | collective-permute-start | bytes 786440 | tf_op jit(solution)/shard_map/ppermute | solution.py:565
  33.8 16.4 %collective-permute-start.15 = (bf16[512,256]{1,0:T(8,128)(2,1)S(1)}, bf16[512,256]{1,0:T(8,128)(2,1)S(1)}, u32[]{:S(2)}, u32[]{:S(2)}) collective-permute-start(bf16[512,256]{1,0:T(8,128)(2,1)S(1)} %shard_map.59.refs_3_), channel_id=1, source_target_pairs={{8,12},{4,0},{9,13},{5,1},{10,14},{6,2},{11,15},{7,3},{24,28},{20,... | collective-permute-start | bytes 786440 | tf_op jit(solution)/shard_map/ppermute | solution.py:565

commit v7 on v6

--- a/solution.py
+++ b/solution.py
@@ -458,7 +458,7 @@
         done_refs = refs[:k]
         state_ref, new_ref, tip_ref = refs[k : k + 3]
         spike_refs = refs[k + 3 : k + 3 + n]
-        out, source, whole, sems = refs[k + 3 + n :]
+        out, whole, sems = refs[k + 3 + n :]
 
         copies = []
         first = 0
@@ -472,19 +472,21 @@
                 copies.append(part)
             first += w
 
+        def update(source):
+            starts = row_starts(height, n, 1)
+            for rows, value in each_product(at_level(spike_refs, level), starts, source[...]):
+                new = state_ref[rows, :] - value
+                whole[0, rows, :] = new[:, :own]
+                whole[1, rows, :] = new[:, own:]
+
         @pl.when(use_new())
         def _():
-            source[...] = new_ref[...]
+            update(new_ref)
 
         @pl.when(jnp.logical_not(use_new()))
         def _():
-            source[...] = tip_ref[...]
-
-        starts = row_starts(height, n, 1)
-        for rows, value in each_product(at_level(spike_refs, level), starts, source[...]):
-            new = state_ref[rows, :] - value
-            whole[0, rows, :] = new[:, :own]
-            whole[1, rows, :] = new[:, own:]
+            update(tip_ref)
+
         copies.append(pltpu.make_async_copy(whole, out.at[:, :, pl.ds(before, own)], sems.at[2 * k]))
         copies[-1].start()
         for copy in copies:
@@ -496,7 +498,6 @@
         in_specs=[VMEM] * (k + 3 + n),
         out_specs=pl.BlockSpec(memory_space=pl.ANY),
         scratch_shapes=[
-            pltpu.VMEM((height, width), jnp.bfloat16),
             pltpu.VMEM((2, height, own), jnp.float32),
             pltpu.SemaphoreType.DMA((2 * k + 1,)),
         ],

time: 51.8 us -> 51.8 us (level)
  no operation moved by 1% of the time
where the time goes in v7:
time: 51.8 us; the launch traced here: 51.5 us
  waiting for transfers between devices  24.5 us (47%)
  starting transfers between devices  16.8 us (32%)
  Pallas kernels  7.62 us (15%)
  local copies, waits for them, and re-layouts  2.28 us (4%)
    ppermute x2, waiting for transfers between devices, per_device(): moved = [lax.ppermute(tips[c], 'slab', route) for c in chunks]  14.6 us
    ppermute x6, starting transfers between devices, swap(): return lax.ppermute(block, 'slab', pairs + [(b, a) for a, b in pairs])  10.1 us
    ppermute x6, waiting for transfers between devices, swap(): return lax.ppermute(block, 'slab', pairs + [(b, a) for a, b in pairs])  8.18 us
    pallas_call x13, Pallas kernels, call(): pl.pallas_call(body, out_shape=outs, in_specs=[VMEM] * len(args), out_spe...  6.23 us
    ppermute x8, starting transfers between devices, ring_gather(): lax.ppermute(block, axis, [((i + step) % count, i) for i in range(count)])  4.14 us
    ppermute x2, starting transfers between devices, per_device(): moved = [lax.ppermute(tips[c], 'slab', route) for c in chunks]  2.58 us
    unnamed x8, local copies, waits for them, and re-layouts  2.28 us
    ppermute x8, waiting for transfers between devices, ring_gather(): lax.ppermute(block, axis, [((i + step) % count, i) for i in range(count)])  1.68 us
  transfers between devices with their start and end apart: 16, of which 6 were waited for; matrix products, arithmetic and copies ran while one was open for 0% of the time, Pallas kernels for 12%

profile of v7, /device:TPU:0, one launch (start us, length us, event | category | flops | bytes accessed | tf_op | source)
XLA Modules:
  0.0 51.5 jit_solution(11957402135130546829)
XLA Ops:
  0.0 0.5 collective-permute-start.3
  0.5 0.5 collective-permute-start.1
  1.0 1.2 %copy-done.2 = bf16[2,1,2,256,512]{4,3,2,1,0:T(8,128)(2,1)S(1)} copy-done((bf16[2,1,2,256,512]{4,3,2,1,0:T(8,128)(2,1)S(1)}, bf16[2,1,2,256,512]{4,3,2,1,0:T(8,128)(2,1)}, u32[]{:S(2)}) %copy-start.2) | copy-done | bytes 1048600
  2.2 1.0 %copy-done.3 = bf16[2,1,256,512]{3,2,1,0:T(8,128)(2,1)S(1)} copy-done((bf16[2,1,256,512]{3,2,1,0:T(8,128)(2,1)S(1)}, bf16[2,1,256,512]{3,2,1,0:T(8,128)(2,1)}, u32[]{:S(2)}) %copy-start.3) | copy-done | bytes 524312
  3.4 0.8 %shard_map.49 = (bf16[2,256,512]{2,1,0:T(8,128)(2,1)S(1)}, bf16[2,256,512]{2,1,0:T(8,128)(2,1)S(1)}) custom-call(bf16[2,2,256,512]{3,2,1,0:T(8,128)(2,1)S(1)} %get-tuple-element.24.refs_0_.refs_7_.refs_3_.refs_4_, bf16[2,2,256,512]{3,2,1,0:T(8,128)(2,1)S(1)} %collective-permute-done.3.refs_1_.refs_8_.refs_4_.refs_5_, ...), custom_call_target="tpu_custom_call" | custom-call | flops 536870912 | bytes 3670016 | tf_op jit(solution)/shard_map/pallas_call | solution.py:62
  4.3 0.5 shard_map.51
  4.7 2.7 %collective-permute-start.5 = (bf16[2,128,512]{2,1,0:T(8,128)(2,1)S(1)}, bf16[2,128,512]{2,1,0:T(8,128)(2,1)S(1)}, u32[]{:S(2)}, u32[]{:S(2)}) collective-permute-start(bf16[2,128,512]{2,1,0:T(8,128)(2,1)S(1)} %shard_map.51), channel_id=1, source_target_pairs={{0,4},{8,12},{4,0},{12,8},{1,5},{9,13},{5,1},{13,9},{2,6},{10,14},... | collective-permute-start | bytes 786440 | tf_op jit(solution)/shard_map/ppermute | solution.py:512
  7.4 0.7 %collective-permute-start.10 = (bf16[2,256,512]{2,1,0:T(8,128)(2,1)S(1)}, bf16[2,256,512]{2,1,0:T(8,128)(2,1)S(1)}, u32[]{:S(2)}, u32[]{:S(2)}) collective-permute-start(bf16[2,256,512]{2,1,0:T(8,128)(2,1)S(1)} %get-tuple-element.32), channel_id=1, source_target_pairs={{4,8},{8,4},{5,9},{9,5},{6,10},{10,6},{7,11},{11,7},{20,24},{24,20... | collective-permute-start | bytes 1572872 | tf_op jit(solution)/shard_map/ppermute | solution.py:512
  8.1 0.4 shard_map.46
  8.6 0.5 shard_map.48.refs_0_
  9.0 4.0 %collective-permute-start.2 = (bf16[512,256]{1,0:T(8,128)(2,1)S(1)}, bf16[512,256]{1,0:T(8,128)(2,1)S(1)}, u32[]{:S(2)}, u32[]{:S(2)}) collective-permute-start(bf16[512,256]{1,0:T(8,128)(2,1)S(1)} %shard_map.48.refs_0_), channel_id=1, source_target_pairs={{0,4},{8,12},{4,0},{12,8},{1,5},{9,13},{5,1},{13,9},{2,6},{10,14},... | collective-permute-start | bytes 786440 | tf_op jit(solution)/shard_map/ppermute | solution.py:512
  13.1 0.4 shard_map.52
  13.5 0.5 shard_map.53.refs_0_
  14.0 0.4 collective-permute-done.5.refs_3_
  14.4 2.5 %collective-permute-start.6 = (bf16[2,128,512]{2,1,0:T(8,128)(2,1)S(1)}, bf16[2,128,512]{2,1,0:T(8,128)(2,1)S(1)}, u32[]{:S(2)}, u32[]{:S(2)}) collective-permute-start(bf16[2,128,512]{2,1,0:T(8,128)(2,1)S(1)} %collective-permute-done.5.refs_3_), channel_id=1, source_target_pairs={{2,0},{0,2},{3,1},{1,3},{6,4},{4,6},{7,5},{5,7},{10,8},{8,10},{11,... | collective-permute-start | bytes 786440 | tf_op jit(solution)/shard_map/ppermute | solution.py:16
  16.9 2.6 %collective-permute-done.2.refs_1_.refs_2_ = bf16[512,256]{1,0:T(8,128)(2,1)S(1)} collective-permute-done((bf16[512,256]{1,0:T(8,128)(2,1)S(1)}, bf16[512,256]{1,0:T(8,128)(2,1)S(1)}, u32[]{:S(2)}, u32[]{:S(2)}) %collective-permute-start.2) | collective-permute-done | bytes 262176 | tf_op jit(solution)/shard_map/ppermute | solution.py:512
  19.5 0.4 shard_map.50.refs_1_
  20.0 1.7 %collective-permute-done.6.refs_4_ = bf16[2,128,512]{2,1,0:T(8,128)(2,1)S(1)} collective-permute-done((bf16[2,128,512]{2,1,0:T(8,128)(2,1)S(1)}, bf16[2,128,512]{2,1,0:T(8,128)(2,1)S(1)}, u32[]{:S(2)}, u32[]{:S(2)}) %collective-permute-start.6) | collective-permute-done | bytes 262176 | tf_op jit(solution)/shard_map/ppermute | solution.py:16
  21.6 0.5 collective-permute-start.8
  22.2 1.4 %collective-permute-start.13 = (bf16[512,256]{1,0:T(8,128)(2,1)S(1)}, bf16[512,256]{1,0:T(8,128)(2,1)S(1)}, u32[]{:S(2)}, u32[]{:S(2)}) collective-permute-start(bf16[512,256]{1,0:T(8,128)(2,1)S(1)} %shard_map.53.refs_0_), channel_id=1, source_target_pairs={{0,4},{8,12},{4,0},{12,8},{1,5},{9,13},{5,1},{13,9},{2,6},{10,14},... | collective-permute-start | bytes 786440 | tf_op jit(solution)/shard_map/ppermute | solution.py:512
  23.6 0.9 %shard_map.54 = (f32[512,256]{1,0:T(8,128)S(1)}, bf16[512,256]{1,0:T(8,128)(2,1)S(1)}) custom-call(f32[512,256]{1,0:T(8,128)S(1)} %get-tuple-element.21.refs_0_, bf16[512,256]{1,0:T(8,128)(2,1)S(1)} %shard_map.50.refs_1_, bf16[512,256]{1,0:T(8,128)(2,1)S(1)} %collective-permute-done.2.refs_1_.refs_2_, ...), custom_call_target="tpu_custom_call" | custom-call | flops 805306368 | bytes 6029312 | tf_op jit(solution)/shard_map/pallas_call | solution.py:62
  24.5 0.7 %collective-permute-start.9 = (bf16[512,256]{1,0:T(8,128)(2,1)S(1)}, bf16[512,256]{1,0:T(8,128)(2,1)S(1)}, u32[]{:S(2)}, u32[]{:S(2)}) collective-permute-start(bf16[512,256]{1,0:T(8,128)(2,1)S(1)} %get-tuple-element.31.refs_0_), channel_id=1, source_target_pairs={{4,8},{8,4},{5,9},{9,5},{6,10},{10,6},{7,11},{11,7},{20,24},{24,20... | collective-permute-start | bytes 786440 | tf_op jit(solution)/shard_map/ppermute | solution.py:512
  25.2 5.2 %collective-permute-done.13.refs_1_.refs_2_ = bf16[512,256]{1,0:T(8,128)(2,1)S(1)} collective-permute-done((bf16[512,256]{1,0:T(8,128)(2,1)S(1)}, bf16[512,256]{1,0:T(8,128)(2,1)S(1)}, u32[]{:S(2)}, u32[]{:S(2)}) %collective-permute-start.13) | collective-permute-done | bytes 262176 | tf_op jit(solution)/shard_map/ppermute | solution.py:512
  30.4 0.4 shard_map.57.refs_1_
  30.8 0.9 %shard_map.58 = (f32[512,256]{1,0:T(8,128)S(1)}, bf16[512,256]{1,0:T(8,128)(2,1)S(1)}) custom-call(f32[512,256]{1,0:T(8,128)S(1)} %get-tuple-element.33.refs_0_, bf16[512,256]{1,0:T(8,128)(2,1)S(1)} %shard_map.57.refs_1_, bf16[512,256]{1,0:T(8,128)(2,1)S(1)} %collective-permute-done.13.refs_1_.refs_2_, ...), custom_call_target="tpu_custom_call" | custom-call | flops 805306368 | bytes 6029312 | tf_op jit(solution)/shard_map/pallas_call | solution.py:62
  31.8 0.7 %collective-permute-start.14 = (bf16[512,256]{1,0:T(8,128)(2,1)S(1)}, bf16[512,256]{1,0:T(8,128)(2,1)S(1)}, u32[]{:S(2)}, u32[]{:S(2)}) collective-permute-start(bf16[512,256]{1,0:T(8,128)(2,1)S(1)} %get-tuple-element.36.refs_0_), channel_id=1, source_target_pairs={{4,8},{8,4},{5,9},{9,5},{6,10},{10,6},{7,11},{11,7},{20,24},{24,20... | collective-permute-start | bytes 786440 | tf_op jit(solution)/shard_map/ppermute | solution.py:512
  32.5 1.3 %collective-permute-start.12 = (bf16[512,256]{1,0:T(8,128)(2,1)S(1)}, bf16[512,256]{1,0:T(8,128)(2,1)S(1)}, u32[]{:S(2)}, u32[]{:S(2)}) collective-permute-start(bf16[512,256]{1,0:T(8,128)(2,1)S(1)} %shard_map.55.refs_2_), channel_id=1, source_target_pairs={{8,12},{4,0},{9,13},{5,1},{10,14},{6,2},{11,15},{7,3},{24,28},{20,... | collective-permute-start | bytes 786440 | tf_op jit(solution)/shard_map/ppermute | solution.py:566
  33.8 1.3 %collective-permute-start.15 = (bf16[512,256]{1,0:T(8,128)(2,1)S(1)}, bf16[512,256]{1,0:T(8,128)(2,1)S(1)}, u32[]{:S(2)}, u32[]{:S(2)}) collective-permute-start(bf16[512,256]{1,0:T(8,128)(2,1)S(1)} %shard_map.59.refs_3_), channel_id=1, source_target_pairs={{8,12},{4,0},{9,13},{5,1},{10,14},{6,2},{11,15},{7,3},{24,28},{20,... | collective-permute-start | bytes 786440 | tf_op jit(solution)/shard_map/ppermute | solution.py:566
  35.1 9.9 %collective-permute-done.12.refs_1_ = bf16[512,256]{1,0:T(8,128)(2,1)S(1)} collective-permute-done((bf16[512,256]{1,0:T(8,128)(2,1)S(1)}, bf16[512,256]{1,0:T(8,128)(2,1)S(1)}, u32[]{:S(2)}, u32[]{:S(2)}) %collective-permute-start.12) | collective-permute-done | bytes 262176 | tf_op jit(solution)/shard_map/ppermute | solution.py:566
  45.0 0.5 shard_map.56.refs_0_
  45.5 4.8 %collective-permute-done.15.refs_2_ = bf16[512,256]{1,0:T(8,128)(2,1)S(1)} collective-permute-done((bf16[512,256]{1,0:T(8,128)(2,1)S(1)}, bf16[512,256]{1,0:T(8,128)(2,1)S(1)}, u32[]{:S(2)}, u32[]{:S(2)}) %collective-permute-start.15) | collective-permute-done | bytes 262176 | tf_op jit(solution)/shard_map/ppermute | solution.py:566
  50.2 1.3 %shard_map.60 = f32[2,512,256]{2,1,0:T(8,128)} custom-call(f32[512,256]{1,0:T(8,128)S(1)} %shard_map.56.refs_0_, f32[512,256]{1,0:T(8,128)S(1)} %get-tuple-element.35.refs_1_, bf16[512,256]{1,0:T(8,128)(2,1)S(1)} %collective-permute-done.15.refs_2_, bf16[512,256]{1,0:T(8,128)(2,1)S(1)} %shard_map.59.refs_3_, ...), custom_call_target="tpu_custom_call" | custom-call | flops 268435456 | bytes 1572864 | tf_op jit(solution)/shard_map/pallas_call | solution.py:495
  (23 shorter events, 0.4 us)
Async XLA Ops:
  0.0 3.4 %collective-permute-start.3 = (bf16[2,2,256,512]{3,2,1,0:T(8,128)(2,1)}, bf16[2,2,256,512]{3,2,1,0:T(8,128)(2,1)S(1)}, u32[]{:S(2)}, u32[]{:S(2)}) collective-permute-start(bf16[2,2,256,512]{3,2,1,0:T(8,128)(2,1)} %bitcast.12), channel_id=1, source_target_pairs={{1,0},{0,1},{3,2},{2,3},{5,4},{4,5},{7,6},{6,7},{9,8},{8,9},{11,10... | collective-permute-start | bytes 3145736 | tf_op jit(solution)/shard_map/ppermute | solution.py:16
  0.5 7.6 %collective-permute-start = (bf16[2,256,512]{2,1,0:T(8,128)(2,1)}, bf16[2,256,512]{2,1,0:T(8,128)(2,1)S(1)}, u32[]{:S(2)}, u32[]{:S(2)}) collective-permute-start(bf16[2,256,512]{2,1,0:T(8,128)(2,1)} %bitcast.7), channel_id=1, source_target_pairs={{1,0},{0,1},{3,2},{2,3},{5,4},{4,5},{7,6},{6,7},{9,8},{8,9},{11,10... | collective-permute-start | bytes 1572872 | tf_op jit(solution)/shard_map/ppermute | solution.py:16
  0.5 8.1 %collective-permute-start.1 = (bf16[2,256,512]{2,1,0:T(8,128)(2,1)}, bf16[2,256,512]{2,1,0:T(8,128)(2,1)S(1)}, u32[]{:S(2)}, u32[]{:S(2)}) collective-permute-start(bf16[2,256,512]{2,1,0:T(8,128)(2,1)} %bitcast.14), channel_id=1, source_target_pairs={{1,0},{0,1},{3,2},{2,3},{5,4},{4,5},{7,6},{6,7},{9,8},{8,9},{11,10... | collective-permute-start | bytes 1572872 | tf_op jit(solution)/shard_map/ppermute | solution.py:16
  1.0 1.2 %copy-start.2 = (bf16[2,1,2,256,512]{4,3,2,1,0:T(8,128)(2,1)S(1)}, bf16[2,1,2,256,512]{4,3,2,1,0:T(8,128)(2,1)}, u32[]{:S(2)}) copy-start(bf16[2,1,2,256,512]{4,3,2,1,0:T(8,128)(2,1)} %param.6) | copy-start | bytes 3145732
  2.2 1.0 %copy-start.3 = (bf16[2,1,256,512]{3,2,1,0:T(8,128)(2,1)S(1)}, bf16[2,1,256,512]{3,2,1,0:T(8,128)(2,1)}, u32[]{:S(2)}) copy-start(bf16[2,1,256,512]{3,2,1,0:T(8,128)(2,1)} %param.7) | copy-start | bytes 1572868
  4.1 4.0 %copy-start = (bf16[2,1,256,512]{3,2,1,0:T(8,128)(2,1)S(1)}, bf16[2,1,256,512]{3,2,1,0:T(8,128)(2,1)}, u32[]{:S(2)}) copy-start(bf16[2,1,256,512]{3,2,1,0:T(8,128)(2,1)} %param.5) | copy-start | bytes 1572868
  4.2 4.0 %copy-start.1 = (bf16[2,1,512,256]{3,2,1,0:T(8,128)(2,1)S(1)}, bf16[2,1,512,256]{3,2,1,0:T(8,128)(2,1)}, u32[]{:S(2)}) copy-start(bf16[2,1,512,256]{3,2,1,0:T(8,128)(2,1)} %param.4) | copy-start | bytes 1572868
  4.2 15.4 %collective-permute-start.4 = (bf16[2,256,512]{2,1,0:T(8,128)(2,1)S(1)}, bf16[2,256,512]{2,1,0:T(8,128)(2,1)S(1)}, u32[]{:S(2)}, u32[]{:S(2)}) collective-permute-start(bf16[2,256,512]{2,1,0:T(8,128)(2,1)S(1)} %get-tuple-element.25.refs_2_.refs_4_), channel_id=1, source_target_pairs={{1,0},{0,1},{3,2},{2,3},{5,4},{4,5},{7,6},{6,7},{9,8},{8,9},{11,10... | collective-permute-start | bytes 1572872 | tf_op jit(solution)/shard_map/ppermute | solution.py:16
  4.7 9.6 %collective-permute-start.5 = (bf16[2,128,512]{2,1,0:T(8,128)(2,1)S(1)}, bf16[2,128,512]{2,1,0:T(8,128)(2,1)S(1)}, u32[]{:S(2)}, u32[]{:S(2)}) collective-permute-start(bf16[2,128,512]{2,1,0:T(8,128)(2,1)S(1)} %shard_map.51), channel_id=1, source_target_pairs={{0,4},{8,12},{4,0},{12,8},{1,5},{9,13},{5,1},{13,9},{2,6},{10,14},... | collective-permute-start | bytes 786440 | tf_op jit(solution)/shard_map/ppermute | solution.py:512
  7.4 16.2 %collective-permute-start.10 = (bf16[2,256,512]{2,1,0:T(8,128)(2,1)S(1)}, bf16[2,256,512]{2,1,0:T(8,128)(2,1)S(1)}, u32[]{:S(2)}, u32[]{:S(2)}) collective-permute-start(bf16[2,256,512]{2,1,0:T(8,128)(2,1)S(1)} %get-tuple-element.32), channel_id=1, source_target_pairs={{4,8},{8,4},{5,9},{9,5},{6,10},{10,6},{7,11},{11,7},{20,24},{24,20... | collective-permute-start | bytes 1572872 | tf_op jit(solution)/shard_map/ppermute | solution.py:512
  9.0 10.5 %collective-permute-start.2 = (bf16[512,256]{1,0:T(8,128)(2,1)S(1)}, bf16[512,256]{1,0:T(8,128)(2,1)S(1)}, u32[]{:S(2)}, u32[]{:S(2)}) collective-permute-start(bf16[512,256]{1,0:T(8,128)(2,1)S(1)} %shard_map.48.refs_0_), channel_id=1, source_target_pairs={{0,4},{8,12},{4,0},{12,8},{1,5},{9,13},{5,1},{13,9},{2,6},{10,14},... | collective-permute-start | bytes 786440 | tf_op jit(solution)/shard_map/ppermute | solution.py:512
  14.4 7.3 %collective-permute-start.6 = (bf16[2,128,512]{2,1,0:T(8,128)(2,1)S(1)}, bf16[2,128,512]{2,1,0:T(8,128)(2,1)S(1)}, u32[]{:S(2)}, u32[]{:S(2)}) collective-permute-start(bf16[2,128,512]{2,1,0:T(8,128)(2,1)S(1)} %collective-permute-done.5.refs_3_), channel_id=1, source_target_pairs={{2,0},{0,2},{3,1},{1,3},{6,4},{4,6},{7,5},{5,7},{10,8},{8,10},{11,... | collective-permute-start | bytes 786440 | tf_op jit(solution)/shard_map/ppermute | solution.py:16
  21.6 1.9 %collective-permute-start.7 = (bf16[2,128,512]{2,1,0:T(8,128)(2,1)S(1)}, bf16[2,128,512]{2,1,0:T(8,128)(2,1)S(1)}, u32[]{:S(2)}, u32[]{:S(2)}) collective-permute-start(bf16[2,128,512]{2,1,0:T(8,128)(2,1)S(1)} %collective-permute-done.5.refs_3_), channel_id=1, source_target_pairs={{1,0},{0,1},{3,2},{2,3},{5,4},{4,5},{7,6},{6,7},{9,8},{8,9},{11,10... | collective-permute-start | bytes 786440 | tf_op jit(solution)/shard_map/ppermute | solution.py:16
  21.6 1.9 %collective-permute-start.8 = (bf16[2,128,512]{2,1,0:T(8,128)(2,1)S(1)}, bf16[2,128,512]{2,1,0:T(8,128)(2,1)S(1)}, u32[]{:S(2)}, u32[]{:S(2)}) collective-permute-start(bf16[2,128,512]{2,1,0:T(8,128)(2,1)S(1)} %collective-permute-done.6.refs_4_), channel_id=1, source_target_pairs={{1,0},{0,1},{3,2},{2,3},{5,4},{4,5},{7,6},{6,7},{9,8},{8,9},{11,10... | collective-permute-start | bytes 786440 | tf_op jit(solution)/shard_map/ppermute | solution.py:16
  22.2 8.2 %collective-permute-start.13 = (bf16[512,256]{1,0:T(8,128)(2,1)S(1)}, bf16[512,256]{1,0:T(8,128)(2,1)S(1)}, u32[]{:S(2)}, u32[]{:S(2)}) collective-permute-start(bf16[512,256]{1,0:T(8,128)(2,1)S(1)} %shard_map.53.refs_0_), channel_id=1, source_target_pairs={{0,4},{8,12},{4,0},{12,8},{1,5},{9,13},{5,1},{13,9},{2,6},{10,14},... | collective-permute-start | bytes 786440 | tf_op jit(solution)/shard_map/ppermute | solution.py:512
  23.6 8.9 %collective-permute-start.11 = (bf16[2,256,512]{2,1,0:T(8,128)(2,1)S(1)}, bf16[2,256,512]{2,1,0:T(8,128)(2,1)S(1)}, u32[]{:S(2)}, u32[]{:S(2)}) collective-permute-start(bf16[2,256,512]{2,1,0:T(8,128)(2,1)S(1)} %collective-permute-done.10.refs_2_), channel_id=1, source_target_pairs={{1,0},{0,1},{3,2},{2,3},{5,4},{4,5},{7,6},{6,7},{9,8},{8,9},{11,10... | collective-permute-start | bytes 1572872 | tf_op jit(solution)/shard_map/ppermute | solution.py:16
  24.5 7.9 %collective-permute-start.9 = (bf16[512,256]{1,0:T(8,128)(2,1)S(1)}, bf16[512,256]{1,0:T(8,128)(2,1)S(1)}, u32[]{:S(2)}, u32[]{:S(2)}) collective-permute-start(bf16[512,256]{1,0:T(8,128)(2,1)S(1)} %get-tuple-element.31.refs_0_), channel_id=1, source_target_pairs={{4,8},{8,4},{5,9},{9,5},{6,10},{10,6},{7,11},{11,7},{20,24},{24,20... | collective-permute-start | bytes 786440 | tf_op jit(solution)/shard_map/ppermute | solution.py:512
  31.8 2.0 %collective-permute-start.14 = (bf16[512,256]{1,0:T(8,128)(2,1)S(1)}, bf16[512,256]{1,0:T(8,128)(2,1)S(1)}, u32[]{:S(2)}, u32[]{:S(2)}) collective-permute-start(bf16[512,256]{1,0:T(8,128)(2,1)S(1)} %get-tuple-element.36.refs_0_), channel_id=1, source_target_pairs={{4,8},{8,4},{5,9},{9,5},{6,10},{10,6},{7,11},{11,7},{20,24},{24,20... | collective-permute-start | bytes 786440 | tf_op jit(solution)/shard_map/ppermute | solution.py:512
  32.5 12.5 %collective-permute-start.12 = (bf16[512,256]{1,0:T(8,128)(2,1)S(1)}, bf16[512,256]{1,0:T(8,128)(2,1)S(1)}, u32[]{:S(2)}, u32[]{:S(2)}) collective-permute-start(bf16[512,256]{1,0:T(8,128)(2,1)S(1)} %shard_map.55.refs_2_), channel_id=1, source_target_pairs={{8,12},{4,0},{9,13},{5,1},{10,14},{6,2},{11,15},{7,3},{24,28},{20,... | collective-permute-start | bytes 786440 | tf_op jit(solution)/shard_map/ppermute | solution.py:566
  33.8 16.4 %collective-permute-start.15 = (bf16[512,256]{1,0:T(8,128)(2,1)S(1)}, bf16[512,256]{1,0:T(8,128)(2,1)S(1)}, u32[]{:S(2)}, u32[]{:S(2)}) collective-permute-start(bf16[512,256]{1,0:T(8,128)(2,1)S(1)} %shard_map.59.refs_3_), channel_id=1, source_target_pairs={{8,12},{4,0},{9,13},{5,1},{10,14},{6,2},{11,15},{7,3},{24,28},{20,... | collective-permute-start | bytes 786440 | tf_op jit(solution)/shard_map/ppermute | solution.py:566
